TPU v7x, 128 devices: a whole 4x4x4 slice. The times are simulated.
128 devices in a mesh: head: 4 (over x), wide: 32 (over y, z, core).
Axes of the slice: x: 4, y: 4, z: 4, core: 2. Of those that a mesh axis runs over, the one named last changes fastest.
Arguments:
- kv_cache: bfloat16 [64, 8192, 1024], P(None, 'wide', 'head'), may hold values from -8 to 8, as said below
- lin_states: float32 [64, 32, 128, 128], P(None, 'head', 'wide'), may hold values from -6 to 6
- row_order: int32 [64], replicated, may hold values from 0 to 63, each once
- prompt_lengths: int32 [64], replicated, may hold values from 512 to 8192, as said below
- att_query: bfloat16 [64, 3, 16, 256], P('wide'), may hold values from -8 to 8
- new_kv: bfloat16 [64, 3, 1024], P('wide'), may hold values from -6 to 6
- att_gate: bfloat16 [64, 3, 4096], P('wide', None, 'head'), may hold values from -6 to 6
- lin_query: bfloat16 [64, 3, 16, 128], P('wide', None, 'head'), may hold values from -6 to 6
- lin_key: bfloat16 [64, 3, 16, 128], P('wide', None, 'head'), may hold values from -6 to 6
- lin_value: bfloat16 [64, 3, 32, 128], P('wide', None, 'head'), may hold values from -6 to 6
- lin_decay: float32 [64, 3, 32], P('wide', None, 'head'), may hold values from 0.3 to 1
- lin_beta: float32 [64, 3, 32], P('wide', None, 'head'), may hold values from 0.2 to 1
- lin_gate: bfloat16 [64, 3, 32, 128], P('wide', None, 'head'), may hold values from -6 to 6
Outputs:
- att_out: bfloat16 [64, 3, 4096], P('wide', None, 'head')
- lin_out: bfloat16 [64, 3, 32, 128], P('wide', None, 'head')
- final_states: float32 [64, 32, 128, 128], P('wide', 'head')
Inputs may be any that keep to these rules, and one draw needn't show every extreme that they name: `kv_cache`: keys and values of every prompt position, also beyond a row's length. `row_order`: each prefill row appears once. `prompt_lengths`: some row has length 8192.
All inputs are finite; a program needn't handle non-finite values.
Results may differ from a plain program's by a relative error of at most 0.015.
Values may be sent and summed in bfloat16 or wider, within the bound.
No kernel may reach another device: no remote copies, remote signals or barrier semaphores. Data moves between devices by JAX's collectives and lax.ppermute only.
A program may use at most 128 MiB of HBM per device.

v0:
```python
import jax
import jax.numpy as jnp
from jax import lax
from jax.sharding import PartitionSpec as P

HQ = 16
KVH = 2
HD = 256
STEPS = 3
KB = 512


NEGATIVE = -1e30


def combined_all(shard, axis, combine):
    everything = jax.tree.map(
        lambda part, kind: lax.all_gather(part.astype(kind), axis),
        shard,
        (jnp.bfloat16, jnp.bfloat16, jnp.bfloat16),
    )

    def take(k):
        return jax.tree.map(lambda part, own: part[k].astype(own.dtype), everything, shard)

    return lax.fori_loop(
        1, lax.axis_size(axis), lambda k, so_far: combine(so_far, take(k)), take(0)
    )


def delta_rule(states, query, key, value, decay, beta, gate):
    ratio = value.shape[2] // query.shape[2]
    queries = jnp.repeat(query.astype(jnp.float32), ratio, axis=2)
    keyed = jnp.repeat(key.astype(jnp.float32), ratio, axis=2)
    queries = (
        queries
        * lax.rsqrt(jnp.sum(queries * queries, -1, keepdims=True) + 1e-06)
        * queries.shape[-1] ** (-0.5)
    )
    keyed = keyed * lax.rsqrt(jnp.sum(keyed * keyed, -1, keepdims=True) + 1e-06)
    outputs = []
    for step in range(value.shape[1]):
        key_now = keyed[:, step]
        rates = decay[:, step][..., None]
        strength = beta[:, step][..., None]
        recalled = jnp.einsum("rhk,rhkv->rhv", key_now, states, precision=lax.Precision.HIGHEST)
        change = strength * (value[:, step].astype(jnp.float32) - rates * recalled)
        states = rates[..., None] * states + key_now[..., None] * change[..., None, :]
        reading = jnp.einsum(
            "rhk,rhkv->rhv", queries[:, step], states, precision=lax.Precision.HIGHEST
        )
        normed = reading * lax.rsqrt(jnp.mean(reading * reading, -1, keepdims=True) + 1e-06)
        outputs.append(
            (normed * jax.nn.silu(gate[:, step].astype(jnp.float32))).astype(jnp.bfloat16)
        )
    return (jnp.stack(outputs, axis=1), states)


def fold_pair(first, second):
    top_first, total_first, mixed_first = first
    top_second, total_second, mixed_second = second
    top = jnp.maximum(top_first, top_second)
    scale_first = jnp.exp(top_first - top)
    scale_second = jnp.exp(top_second - top)
    total = total_first * scale_first + total_second * scale_second
    mixed = mixed_first * scale_first[..., None] + mixed_second * scale_second[..., None]
    return (top, total, mixed)


def on_device(
    kv_cache,
    lin_states,
    row_order,
    prompt_lengths,
    att_query,
    new_kv,
    att_gate,
    lin_query,
    lin_key,
    lin_value,
    lin_decay,
    lin_beta,
    lin_gate,
):
    head_count = lax.axis_size("head")
    wide_count = lax.axis_size("wide")
    head_index = lax.axis_index("head")
    wide_index = lax.axis_index("wide")
    row_dev = att_query.shape[0]
    rows_all = row_order.shape[0]
    mine = lax.dynamic_slice_in_dim(row_order, wide_index * row_dev, row_dev)
    matches = mine[:, None] == jnp.arange(rows_all, dtype=jnp.int32)[None, :]
    lengths = jnp.sum(jnp.where(matches, prompt_lengths[None, :], 0), axis=1)
    reordered = jnp.take(kv_cache, row_order, axis=0)
    seq_len = reordered.shape[1] * wide_count
    feat_part = reordered.shape[2]
    blocks = seq_len // (head_count * KB)
    gathered = lax.all_to_all(reordered, "wide", split_axis=0, concat_axis=1, tiled=True)
    pieces = gathered.reshape(row_dev, head_count, blocks, KB, feat_part)
    moved = lax.all_to_all(pieces, "head", split_axis=1, concat_axis=4, tiled=True)
    starts = head_index * (blocks * KB) + jnp.arange(blocks, dtype=jnp.int32) * KB
    cache = moved.reshape(row_dev, blocks, KB, feat_part * head_count)
    half = cache.shape[-1] // 2
    group = HQ // KVH
    scale = HD ** (-0.5)
    queries = att_query.reshape(row_dev, STEPS, KVH, group, HD)
    fresh_keys = new_kv[..., :half].reshape(row_dev, STEPS, KVH, HD)
    fresh_values = new_kv[..., half:].reshape(row_dev, STEPS, KVH, HD)
    fresh_scores = (
        jnp.einsum("rsgjd,rtgd->rsgjt", queries, fresh_keys, preferred_element_type=jnp.float32)
        * scale
    )
    causal = jnp.arange(STEPS)[None, :] <= jnp.arange(STEPS)[:, None]
    keep = causal[None, :, None, None, :] & (head_index == 0)
    fresh_scores = jnp.where(keep, fresh_scores, NEGATIVE)
    top = jnp.max(fresh_scores, -1)
    probs = jnp.where(keep, jnp.exp(fresh_scores - top[..., None]), 0.0)
    total = jnp.sum(probs, -1)
    mixed = jnp.einsum(
        "rsgjt,rtgd->rsgjd",
        probs.astype(jnp.bfloat16),
        fresh_values,
        preferred_element_type=jnp.float32,
    )
    limit = jnp.max(lengths)
    active = jnp.sum((starts < limit).astype(jnp.int32))

    def visit(block_index, carry):
        top_now, total_now, mixed_now = carry
        block = lax.dynamic_index_in_dim(cache, block_index, 1, keepdims=False)
        keys = block[..., :half].reshape(row_dev, KB, KVH, HD)
        values = block[..., half:].reshape(row_dev, KB, KVH, HD)
        scores = (
            jnp.einsum("rsgjd,rkgd->rsgjk", queries, keys, preferred_element_type=jnp.float32)
            * scale
        )
        position = starts[block_index] + jnp.arange(KB, dtype=jnp.int32)
        valid = (position[None, :] < lengths[:, None])[:, None, None, None, :]
        scores = jnp.where(valid, scores, NEGATIVE)
        new_top = jnp.maximum(top_now, jnp.max(scores, -1))
        factor = jnp.exp(top_now - new_top)
        weights = jnp.where(valid, jnp.exp(scores - new_top[..., None]), 0.0)
        total_next = total_now * factor + jnp.sum(weights, -1)
        mixed_next = mixed_now * factor[..., None] + jnp.einsum(
            "rsgjk,rkgd->rsgjd",
            weights.astype(jnp.bfloat16),
            values,
            preferred_element_type=jnp.float32,
        )
        return (new_top, total_next, mixed_next)

    top, total, mixed = lax.fori_loop(0, active, visit, (top, total, mixed))
    heads_mine = HQ // head_count
    top, total, mixed = combined_all((top, total, mixed), "head", fold_pair)
    result = (mixed / total[..., None]).reshape(row_dev, STEPS, HQ, HD)
    result = lax.dynamic_slice_in_dim(result, head_index * heads_mine, heads_mine, 2)
    att_out = (
        result.reshape(row_dev, STEPS, heads_mine * HD)
        * jax.nn.sigmoid(att_gate.astype(jnp.float32))
    ).astype(jnp.bfloat16)
    reordered_states = jnp.take(lin_states, row_order, axis=0)
    states = lax.all_to_all(
        reordered_states.astype(jnp.bfloat16), "wide", split_axis=0, concat_axis=2, tiled=True
    ).astype(reordered_states.dtype)
    lin_out, final_states = delta_rule(
        states, lin_query, lin_key, lin_value, lin_decay, lin_beta, lin_gate
    )
    return (att_out, lin_out, final_states)


def solution(mesh):
    placed = (
        P(None, "wide", "head"),
        P(None, "head", "wide", None),
        P(),
        P(),
        P("wide", None, None, None),
        P("wide", None, None),
        P("wide", None, "head"),
        P("wide", None, "head", None),
        P("wide", None, "head", None),
        P("wide", None, "head", None),
        P("wide", None, "head"),
        P("wide", None, "head"),
        P("wide", None, "head", None),
    )
    return jax.shard_map(
        on_device,
        mesh=mesh,
        in_specs=placed,
        out_specs=(
            P("wide", None, "head"),
            P("wide", None, "head", None),
            P("wide", "head", None, None),
        ),
        check_vma=False,
    )
```

profile of v0, /device:TPU:0, one launch (start us, length us, event | category | flops | bytes accessed | tf_op | source)
XLA Modules:
  0.0 342.8 jit_solution(17226482888763375027)
XLA Ops:
  0.6 0.7 compare_select_fusion
  1.4 0.7 compare_and_fusion
  2.1 8.9 %gather_fusion = bf16[64,256,256]{2,1,0:T(8,128)(2,1)} fusion(bf16[64,256,256]{2,1,0:T(8,128)(2,1)} %param.17, s32[1024]{0:T(1024)S(1)} %pad_clamp_fusion), kind=kCustom, calls=%fused_computation | custom fusion | bytes 16777472 | tf_op jit(solution)/shard_map/jit(_take)/gather | solution.py:94
  11.0 7.5 %broadcast_select_fusion = bf16[64,256,256]{2,1,0:T(8,128)(2,1)} fusion(bf16[64,256,256]{2,1,0:T(8,128)(2,1)} %gather_fusion, pred[64]{0:T(512)(128)(4,1)S(1)} %compare_and_fusion), kind=kLoop, calls=%fused_computation.27 | loop fusion | flops 4194304 | bytes 16777280 | tf_op jit(solution)/shard_map/jit(_take)/select_n | solution.py:94
  18.4 8.7 %all-to-all-start = ((bf16[64,256,256]{2,1,0:T(8,128)(2,1)}), bf16[64,256,256]{2,1,0:T(8,128)(2,1)}, u32[]{:S(2)}, u32[]{:S(2)}) async-start(bf16[64,256,256]{2,1,0:T(8,128)(2,1)} %broadcast_select_fusion), calls=%async_computation | async-start | bytes 16777216 | tf_op jit(solution)/shard_map/all_to_all | solution.py:98
  27.1 1.1 gather_fusion.1
  28.3 1.1 select_convert_fusion
  29.4 111.4 %all-to-all-done = bf16[64,256,256]{2,1,0:T(8,128)(2,1)} async-done(((bf16[64,256,256]{2,1,0:T(8,128)(2,1)}), bf16[64,256,256]{2,1,0:T(8,128)(2,1)}, u32[]{:S(2)}, u32[]{:S(2)}) %all-to-all-start) | async-done | bytes 8388640 | tf_op jit(solution)/shard_map/all_to_all | solution.py:98
  140.8 16.2 %all-to-all-start.2 = ((bf16[64,8,4,128]{3,2,1,0:T(4,128)(2,1)}), bf16[64,8,4,128]{3,2,1,0:T(4,128)(2,1)S(1)}, u32[]{:S(2)}, u32[]{:S(2)}) async-start(bf16[64,8,4,128]{3,2,1,0:T(4,128)(2,1)} %select_convert_fusion), calls=%async_computation.2 | async-start | bytes 1048576 | tf_op jit(solution)/shard_map/all_to_all | solution.py:162
  157.3 7.6 %copy.96 = bf16[2,32,256,256]{3,2,1,0:T(8,128)(2,1)} copy(bf16[2,32,256,256]{3,2,0,1:T(8,128)(2,1)} %bitcast.18) | data formatting | bytes 16777216 | tf_op jit(solution)/shard_map/all_to_all | solution.py:98
  164.9 7.5 %copy.97 = bf16[2,4,4,512,256]{4,3,2,0,1:T(8,128)(2,1)} copy(bf16[2,4,4,512,256]{4,3,2,1,0:T(8,128)(2,1)} %bitcast.196) | data formatting | bytes 16777216 | tf_op jit(solution)/shard_map/reshape | solution.py:99
  172.4 6.0 %all-to-all-start.1 = ((bf16[2,4,4,512,256]{4,3,2,0,1:T(8,128)(2,1)}), bf16[2,4,4,512,256]{4,3,2,0,1:T(8,128)(2,1)}, u32[]{:S(2)}, u32[]{:S(2)}) async-start(bf16[2,4,4,512,256]{4,3,2,0,1:T(8,128)(2,1)} %copy.97), calls=%async_computation.1 | async-start | bytes 16777216 | tf_op jit(solution)/shard_map/all_to_all | solution.py:100
  179.1 0.6 reduce_max.28
  179.8 1.3 fusion.69
  182.1 0.5 fusion.78
  182.7 1.1 fusion.16
  183.9 1.2 fusion.15
  185.2 1.4 fusion.17
  186.7 1.1 multiply_add_fusion.1
  187.7 1.0 fusion.79
  188.8 1.4 fusion.18
  190.4 0.6 pad_maximum_fusion
  191.1 81.7 %all-to-all-done.1 = bf16[2,4,4,512,256]{4,3,2,0,1:T(8,128)(2,1)} async-done(((bf16[2,4,4,512,256]{4,3,2,0,1:T(8,128)(2,1)}), bf16[2,4,4,512,256]{4,3,2,0,1:T(8,128)(2,1)}, u32[]{:S(2)}, u32[]{:S(2)}) %all-to-all-start.1) | async-done | bytes 8388640 | tf_op jit(solution)/shard_map/all_to_all | solution.py:100
  272.8 13.3 %copy.139 = bf16[2,4,4,512,256]{3,4,1,0,2:T(8,128)(2,1)} copy(bf16[2,4,4,512,256]{4,3,2,0,1:T(8,128)(2,1)} %all-to-all-done.1) | data formatting | bytes 16777216 | tf_op jit(solution)/shard_map/reshape | solution.py:102
  286.1 19.4 %while.33 = (s32[]{:T(128)}, f32[2,3,2,8]{3,1,2,0:T(4,128)S(1)}, f32[2,3,2,8]{3,1,2,0:T(4,128)S(1)}, f32[2,3,2,8,256]{4,3,1,2,0:T(8,128)S(1)}, s32[]{:T(128)}, /...) while((s32[]{:T(128)}, f32[2,3,2,8]{3,1,2,0:T(4,128)S(1)}, ...), condition=%wide.region_8.9_spmd, body=%wide.region_5.8_spmd.sunk | while | flops 50824900 | bytes 11335867 | solution.py:152
  286.7 1.7 dynamic-slice_bitcast_fusion.2
  288.6 0.6 dynamic_slice.58
  289.2 0.6 iota_add_fusion.2
  289.8 0.3 fusion.107
  290.4 0.4 fusion.109
  291.4 1.7 dynamic-slice_bitcast_fusion.2
  293.3 0.6 dynamic_slice.58
  293.9 0.6 iota_add_fusion.2
  295.1 0.4 fusion.109
  296.1 1.7 dynamic-slice_bitcast_fusion.2
  298.0 0.6 dynamic_slice.58
  298.6 0.6 iota_add_fusion.2
  299.2 0.3 fusion.107
  299.8 0.4 fusion.109
  300.8 1.7 dynamic-slice_bitcast_fusion.2
  302.7 0.6 dynamic_slice.58
  303.3 0.6 iota_add_fusion.2
  304.5 0.4 fusion.109
  305.5 12.0 %all-gather = bf16[8,3,2,8]{3,2,1,0:T(2,128)(2,1)S(1)} all-gather(bf16[2,3,2,8]{3,2,1,0:T(2,128)(2,1)S(1)} %copy.155), channel_id=2, replica_groups=mesh['head'=4,'wide'=32] {'head'}, dimensions={0}, use_global_device_ids=true | all-gather | bytes 960 | tf_op jit(solution)/shard_map/all_gather | solution.py:18
  317.5 11.9 %all-gather.1 = bf16[8,3,2,8]{3,2,1,0:T(2,128)(2,1)S(1)} all-gather(bf16[2,3,2,8]{3,2,1,0:T(2,128)(2,1)S(1)} %copy.154), channel_id=3, replica_groups=mesh['head'=4,'wide'=32] {'head'}, dimensions={0}, use_global_device_ids=true | all-gather | bytes 960 | tf_op jit(solution)/shard_map/all_gather | solution.py:18
  329.4 12.1 %all-gather.2 = bf16[8,3,2,8,256]{4,3,2,1,0:T(8,128)(2,1)S(1)} all-gather(bf16[2,3,2,8,256]{4,3,2,1,0:T(8,128)(2,1)S(1)} %copy.153), channel_id=4, replica_groups=mesh['head'=4,'wide'=32] {'head'}, dimensions={0}, use_global_device_ids=true | all-gather | bytes 245760 | tf_op jit(solution)/shard_map/all_gather | solution.py:18
  341.5 0.5 while.34
  342.2 0.6 fusion.37
  (112 shorter events, 5.7 us)
Async XLA Ops:
  0.6 26.5 %copy-start = (f32[64,8,4,128]{3,2,1,0:T(4,128)S(1)}, f32[64,8,4,128]{3,2,1,0:T(4,128)}, u32[]{:S(2)}) copy-start(f32[64,8,4,128]{3,2,1,0:T(4,128)} %param.18) | copy-start | bytes 3145732
  18.4 138.6 %copy-start.6 = (bf16[2,3,1024]{2,0,1:T(2,128)(2,1)S(1)}, bf16[2,3,1024]{2,0,1:T(2,128)(2,1)}, u32[]{:S(2)}) copy-start(bf16[2,3,1024]{2,0,1:T(2,128)(2,1)} %param.22) | copy-start | bytes 36868
  18.4 138.7 %copy-start.12 = (s32[64]{0:T(128)S(1)}, s32[64]{0:T(128)}, u32[]{:S(2)}) copy-start(s32[64]{0:T(128)} %param.19) | copy-start | bytes 772
  18.4 138.8 %copy-start.3 = (bf16[2,3,16,256]{3,2,1,0:T(8,128)(2,1)S(1)}, bf16[2,3,16,256]{3,2,1,0:T(8,128)(2,1)}, u32[]{:S(2)}) copy-start(bf16[2,3,16,256]{3,2,1,0:T(8,128)(2,1)} %param.21) | copy-start | bytes 147460
  18.4 138.8 %copy-start.5 = (bf16[2,3,4,128]{3,2,1,0:T(4,128)(2,1)S(1)}, bf16[2,3,4,128]{3,2,1,0:T(4,128)(2,1)}, u32[]{:S(2)}) copy-start(bf16[2,3,4,128]{3,2,1,0:T(4,128)(2,1)} %param.24) | copy-start | bytes 18436
  18.4 122.4 %all-to-all-start = ((bf16[64,256,256]{2,1,0:T(8,128)(2,1)}), bf16[64,256,256]{2,1,0:T(8,128)(2,1)}, u32[]{:S(2)}, u32[]{:S(2)}) async-start(bf16[64,256,256]{2,1,0:T(8,128)(2,1)} %broadcast_select_fusion), calls=%async_computation | async-start | bytes 16777216 | tf_op jit(solution)/shard_map/all_to_all | solution.py:98
  140.8 31.6 %all-to-all-start.2 = ((bf16[64,8,4,128]{3,2,1,0:T(4,128)(2,1)}), bf16[64,8,4,128]{3,2,1,0:T(4,128)(2,1)S(1)}, u32[]{:S(2)}, u32[]{:S(2)}) async-start(bf16[64,8,4,128]{3,2,1,0:T(4,128)(2,1)} %select_convert_fusion), calls=%async_computation.2 | async-start | bytes 1048576 | tf_op jit(solution)/shard_map/all_to_all | solution.py:162
  172.4 6.3 %copy-start.4 = (bf16[2,3,4,128]{3,2,1,0:T(4,128)(2,1)S(1)}, bf16[2,3,4,128]{3,2,1,0:T(4,128)(2,1)}, u32[]{:S(2)}) copy-start(bf16[2,3,4,128]{3,2,1,0:T(4,128)(2,1)} %param.25) | copy-start | bytes 18436
  172.4 6.5 %copy-start.13 = (s32[64]{0:T(128)S(1)}, s32[64]{0:T(128)}, u32[]{:S(2)}) copy-start(s32[64]{0:T(128)} %param.20) | copy-start | bytes 772
  172.4 9.0 %copy-start.10 = (f32[2,3,8]{2,0,1:T(2,128)S(1)}, f32[2,3,8]{2,0,1:T(2,128)}, u32[]{:S(2)}) copy-start(f32[2,3,8]{2,0,1:T(2,128)} %param.27) | copy-start | bytes 580
  172.4 9.0 %copy-start.11 = (f32[2,3,8]{2,0,1:T(2,128)S(1)}, f32[2,3,8]{2,0,1:T(2,128)}, u32[]{:S(2)}) copy-start(f32[2,3,8]{2,0,1:T(2,128)} %param.28) | copy-start | bytes 580
  172.4 10.2 %copy-start.9 = (bf16[2,3,8,128]{3,2,1,0:T(8,128)(2,1)S(1)}, bf16[2,3,8,128]{3,2,1,0:T(8,128)(2,1)}, u32[]{:S(2)}) copy-start(bf16[2,3,8,128]{3,2,1,0:T(8,128)(2,1)} %param.26) | copy-start | bytes 36868
  172.4 100.4 %all-to-all-start.1 = ((bf16[2,4,4,512,256]{4,3,2,0,1:T(8,128)(2,1)}), bf16[2,4,4,512,256]{4,3,2,0,1:T(8,128)(2,1)}, u32[]{:S(2)}, u32[]{:S(2)}) async-start(bf16[2,4,4,512,256]{4,3,2,0,1:T(8,128)(2,1)} %copy.97), calls=%async_computation.1 | async-start | bytes 16777216 | tf_op jit(solution)/shard_map/all_to_all | solution.py:100
  178.4 11.9 %copy-start.7 = (bf16[2,3,8,128]{3,2,1,0:T(8,128)(2,1)S(1)}, bf16[2,3,8,128]{3,2,1,0:T(8,128)(2,1)}, u32[]{:S(2)}) copy-start(bf16[2,3,8,128]{3,2,1,0:T(8,128)(2,1)} %param.29) | copy-start | bytes 36868
  187.7 98.3 %copy-start.2 = (f32[2,8,128,128]{3,2,1,0:T(8,128)}, f32[2,8,128,128]{3,2,1,0:T(8,128)S(1)}, u32[]{:S(2)}) copy-start(f32[2,8,128,128]{3,2,1,0:T(8,128)S(1)} %multiply_add_fusion.1) | copy-start | bytes 3145732
  286.1 56.1 %copy-start.8 = (bf16[2,3,1024]{2,0,1:T(2,128)(2,1)S(1)}, bf16[2,3,1024]{2,0,1:T(2,128)(2,1)}, u32[]{:S(2)}) copy-start(bf16[2,3,1024]{2,0,1:T(2,128)(2,1)} %param.23) | copy-start | bytes 36868
  305.5 37.3 %copy-start.1 = (f32[64,8,4,128]{3,2,1,0:T(4,128)S(1)}, f32[64,8,4,128]{3,2,1,0:T(4,128)}, u32[]{:S(2)}) copy-start(f32[64,8,4,128]{3,2,1,0:T(4,128)} %param.18) | copy-start | bytes 3145732
where the time goes:
time: 344 us; the launch traced here: 343 us
  waiting for transfers between devices  193 us (56%)
  local copies, waits for them, and re-layouts  49.2 us (14%)
  blocking collectives  36 us (10%)
  starting transfers between devices  30.9 us (9%)
  other arithmetic  19.4 us (6%)
  matrix products  10.1 us (3%)
    all_to_all x1, waiting for transfers between devices, on_device(): lax.all_to_all(reordered, 'wide', split_axis=0, concat_axis=1, tiled=True)  111 us
    all_to_all x1, waiting for transfers between devices, on_device(): lax.all_to_all(pieces, 'head', split_axis=1, concat_axis=4, tiled=True)  81.7 us
    all_gather x3, blocking collectives, combined_all(): lax.all_gather(part.astype(kind), axis)  36 us
    all_to_all x1, starting transfers between devices, on_device(): lax.all_to_all(reordered_states.astype(jnp.bfloat16), 'wide', split_axis=...  16.2 us
    reshape x1, local copies, waits for them, and re-layouts, on_device(): cache = moved.reshape(row_dev, blocks, KB, feat_part * head_count)  13.3 us
    gather x1, local copies, waits for them, and re-layouts, on_device(): reordered = jnp.take(kv_cache, row_order, axis=0)  8.91 us
    all_to_all x1, starting transfers between devices, on_device(): lax.all_to_all(reordered, 'wide', split_axis=0, concat_axis=1, tiled=True)  8.69 us
    select_n x2, other arithmetic, on_device(): reordered = jnp.take(kv_cache, row_order, axis=0)  8.21 us
  transfers between devices with their start and end apart: 3, of which 2 were waited for; matrix products, arithmetic and copies ran while one was open for 9% of the time, Pallas kernels for 0%

commit v1 on v0

v1 whole, which is shorter than its diff:
```python
import functools

import jax
import jax.numpy as jnp
from jax import lax
from jax.experimental import pallas as pl
from jax.experimental.pallas import tpu as pltpu
from jax.sharding import PartitionSpec as P

HQ = 16
KVH = 2
HD = 256
STEPS = 3
GROUP = HQ // KVH
QROWS = STEPS * GROUP
LANES = 128
NEGATIVE = -1e30

CHUNK = 8
CHUNKS = 4
PER_STEP = 4
NT = (((1,), (1,)), ((), ()))


def row_at(place, slot, other):
    core = (place[1] & 1) ^ other
    return 4 * ((place[1] >> 1) ^ (slot >> 1)) + 2 * core + (slot & 1)


def cache_spec(chunk, n, other, span):
    def at(step, order, lengths, place):
        return (order[row_at(place, chunk * CHUNK + step * PER_STEP + n, other)], 0, 0)

    return pl.BlockSpec((1, span, HD), at)


def gather_kernel(order, lengths, place, *refs):
    out = refs[-1]
    for n in range(PER_STEP):
        out[n] = refs[n][0]


def gather_rows(order, lengths, place, cache, first, count):
    span = cache.shape[1]
    return pl.pallas_call(
        gather_kernel,
        name="gather_rows",
        out_shape=jax.ShapeDtypeStruct((count * CHUNK, span, HD), cache.dtype),
        grid_spec=pltpu.PrefetchScalarGridSpec(
            num_scalar_prefetch=3,
            grid=(count * CHUNK // PER_STEP,),
            in_specs=[cache_spec(first, n, 1, span) for n in range(PER_STEP)],
            out_specs=pl.BlockSpec((PER_STEP, span, HD), lambda s, *_: (s, 0, 0)),
        ),
        cost_estimate=pl.CostEstimate(
            flops=0, bytes_accessed=2 * count * CHUNK * span * HD * 2, transcendentals=0
        ),
    )(order, lengths, place, *([cache] * PER_STEP))


def score_kernel(order, lengths, place, query, *refs, chunk):
    own, swapped, out = refs[:PER_STEP], refs[PER_STEP], refs[PER_STEP + 1]
    span = swapped.shape[1]
    step = pl.program_id(0)
    width = 2 * span
    tail = CHUNK * width

    @pl.when(step == 0)
    def _():
        out[:, tail:] = jnp.zeros((QROWS, LANES), out.dtype)

    @pl.when(place[0] < 2)
    def _():
        lane = lax.broadcasted_iota(jnp.int32, (QROWS, LANES), 1)
        column = lax.broadcasted_iota(jnp.int32, (QROWS, span), 1)
        position = jnp.concatenate(
            [column + place[1] * span, column + (place[1] ^ 1) * span], axis=1
        )
        extra = out[:, tail:].astype(jnp.float32)
        for n in range(PER_STEP):
            slot = step * PER_STEP + n
            length = lengths[order[row_at(place, chunk * CHUNK + slot, 0)]]
            q = query[n]
            scores = jnp.concatenate(
                [
                    lax.dot_general(q, own[n][0], NT, preferred_element_type=jnp.float32),
                    lax.dot_general(q, swapped[n], NT, preferred_element_type=jnp.float32),
                ],
                axis=1,
            ) * (HD ** (-0.5))
            valid = position < length
            scores = jnp.where(valid, scores, NEGATIVE)
            top = jnp.max(scores, axis=1, keepdims=True)
            top = top.astype(jnp.bfloat16).astype(jnp.float32)
            weights = jnp.where(valid, jnp.exp(scores - top), 0.0)
            total = jnp.sum(weights, axis=1, keepdims=True)
            coarse = total.astype(jnp.bfloat16).astype(jnp.float32)
            start = pl.multiple_of(slot * width, width)
            out[:, pl.ds(start, width)] = weights.astype(out.dtype)
            extra = jnp.where(lane == slot, top, extra)
            extra = jnp.where(lane == slot + CHUNK, coarse, extra)
            extra = jnp.where(lane == slot + 2 * CHUNK, total - coarse, extra)
        out[:, tail:] = extra.astype(out.dtype)


def score_rows(order, lengths, place, query, cache, swapped, chunk, swapped_at):
    span = cache.shape[1]
    steps = CHUNK // PER_STEP
    width = CHUNK * 2 * span + LANES
    return pl.pallas_call(
        functools.partial(score_kernel, chunk=chunk),
        name="score_rows",
        out_shape=jax.ShapeDtypeStruct((QROWS, width), jnp.bfloat16),
        grid_spec=pltpu.PrefetchScalarGridSpec(
            num_scalar_prefetch=3,
            grid=(steps,),
            in_specs=[pl.BlockSpec((PER_STEP, QROWS, HD), lambda s, *_: (s, 0, 0))]
            + [cache_spec(chunk, n, 0, span) for n in range(PER_STEP)]
            + [pl.BlockSpec((PER_STEP, span, HD), lambda s, *_: (swapped_at * steps + s, 0, 0))],
            out_specs=pl.BlockSpec((QROWS, width), lambda s, *_: (0, 0)),
        ),
        cost_estimate=pl.CostEstimate(
            flops=CHUNK * 4 * QROWS * span * HD,
            bytes_accessed=2 * CHUNK * span * HD * 2,
            transcendentals=CHUNK * QROWS * 2 * span,
        ),
    )(order, lengths, place, query, *([cache] * PER_STEP), swapped)


def mix_kernel(order, lengths, place, weights, *refs):
    own, swapped, out = refs[:PER_STEP], refs[PER_STEP], refs[-1]
    span = swapped.shape[1]
    step = pl.program_id(0)
    width = 2 * span
    tail = CHUNK * width

    @pl.when(place[0] >= 2)
    def _():
        extra = weights[:, tail:].astype(jnp.float32)
        for pair in range(PER_STEP // 2):
            rows = []
            for n in (2 * pair, 2 * pair + 1):
                slot = step * PER_STEP + n
                start = pl.multiple_of(slot * width, width)
                part = weights[:, pl.ds(start, width)]
                mixed = jnp.dot(
                    part[:, :span], own[n][0], preferred_element_type=jnp.float32
                ) + jnp.dot(part[:, span:], swapped[n], preferred_element_type=jnp.float32)
                mine = pltpu.roll(extra, (LANES - slot) % LANES, 1)
                rows.append(jnp.concatenate([mixed, mine], axis=1))
            chip = ((place[1] >> 1) & 1) ^ pair
            out[chip] = jnp.concatenate(rows, axis=0).astype(out.dtype)


def mix_rows(order, lengths, place, weights, cache, swapped, chunk, swapped_at, before):
    span = cache.shape[1]
    steps = CHUNK // PER_STEP
    chips = CHUNK * CHUNKS // 2
    width = HD + LANES

    def target(step, order, lengths, place):
        return ((place[1] >> 2) ^ (chunk * steps + step), 0, 0)

    in_specs = (
        [pl.BlockSpec(weights.shape, lambda s, *_: (0, 0))]
        + [cache_spec(chunk, n, 0, span) for n in range(PER_STEP)]
        + [pl.BlockSpec((PER_STEP, span, HD), lambda s, *_: (swapped_at * steps + s, 0, 0))]
    )
    operands = [order, lengths, place, weights, *([cache] * PER_STEP), swapped]
    aliases = {}
    if before is not None:
        in_specs.append(pl.BlockSpec(memory_space=pl.ANY))
        aliases = {len(operands): 0}
        operands.append(before)
    return pl.pallas_call(
        mix_kernel,
        name="mix_rows",
        out_shape=jax.ShapeDtypeStruct((chips, 2 * QROWS, width), jnp.bfloat16),
        grid_spec=pltpu.PrefetchScalarGridSpec(
            num_scalar_prefetch=3,
            grid=(steps,),
            in_specs=in_specs,
            out_specs=pl.BlockSpec((PER_STEP // 2, 2 * QROWS, width), target),
        ),
        input_output_aliases=aliases,
        cost_estimate=pl.CostEstimate(
            flops=CHUNK * 4 * QROWS * span * HD,
            bytes_accessed=2 * CHUNK * span * HD * 2,
            transcendentals=0,
        ),
    )(*operands)


def combine_kernel(place, parts, query, fresh, low, high):
    @pl.when(place[0] >= 2)
    def _():
        chips = parts.shape[0]
        second = place[0] & 1
        step = lax.broadcasted_iota(jnp.int32, (QROWS, STEPS), 0) // GROUP
        time = lax.broadcasted_iota(jnp.int32, (QROWS, STEPS), 1)
        keep = time <= step
        half = KVH * HD
        tops, totals = [], []
        for chip in range(chips):
            extra = parts[chip, :, HD:].astype(jnp.float32)
            tops.append(extra[:, 0:1])
            totals.append(extra[:, CHUNK : CHUNK + 1] + extra[:, 2 * CHUNK : 2 * CHUNK + 1])
        scores, values = [], []
        for row in range(2):
            news = fresh[row].astype(jnp.float32)
            keys = jnp.where(second == 1, news[:, HD:half], news[:, :HD])
            values.append(jnp.where(second == 1, news[:, half + HD :], news[:, half : half + HD]))
            q = query[row].astype(jnp.float32)
            columns = [
                jnp.sum(q * keys[t : t + 1], axis=1, keepdims=True) for t in range(STEPS)
            ]
            score = jnp.concatenate(columns, axis=1) * (HD ** (-0.5))
            scores.append(jnp.where(keep, score, NEGATIVE))
        score = jnp.concatenate(scores, axis=0)
        keep = jnp.concatenate([keep, keep], axis=0)
        top = jnp.max(score, axis=1, keepdims=True)
        for chip in range(chips):
            top = jnp.maximum(top, tops[chip])
        probs = jnp.where(keep, jnp.exp(score - top), 0.0)
        total = jnp.sum(probs, axis=1, keepdims=True)
        probs = probs.astype(jnp.bfloat16).astype(jnp.float32)
        mixed = []
        for row in range(2):
            mine = probs[row * QROWS : (row + 1) * QROWS]
            mixed.append(sum(mine[:, t : t + 1] * values[row][t : t + 1] for t in range(STEPS)))
        mixed = jnp.concatenate(mixed, axis=0)
        for chip in range(chips):
            factor = jnp.exp(tops[chip] - top)
            total = total + factor * totals[chip]
            mixed = mixed + factor * parts[chip, :, :HD].astype(jnp.float32)
        result = mixed / total
        heads = GROUP // 2
        for row in range(2):
            for s in range(STEPS):
                for a in range(heads):
                    at = row * QROWS + s * GROUP + a
                    low[row, s : s + 1, a * HD : (a + 1) * HD] = result[at : at + 1]
                    at = at + heads
                    high[row, s : s + 1, a * HD : (a + 1) * HD] = result[at : at + 1]


def combine(place, parts, query, fresh):
    heads = GROUP // 2
    shape = jax.ShapeDtypeStruct((2, STEPS, heads * HD), jnp.float32)
    whole = pl.BlockSpec(memory_space=pltpu.VMEM)
    return pl.pallas_call(
        combine_kernel,
        name="combine_parts",
        out_shape=(shape, shape),
        in_specs=[pl.BlockSpec(memory_space=pltpu.SMEM), whole, whole, whole],
        out_specs=(whole, whole),
        cost_estimate=pl.CostEstimate(
            flops=4 * parts.size, bytes_accessed=2 * parts.size, transcendentals=2000
        ),
    )(place, parts, query, fresh)


def delta_rule(states, query, key, value, decay, beta, gate):
    ratio = value.shape[2] // query.shape[2]
    queries = jnp.repeat(query.astype(jnp.float32), ratio, axis=2)
    keyed = jnp.repeat(key.astype(jnp.float32), ratio, axis=2)
    queries = (
        queries
        * lax.rsqrt(jnp.sum(queries * queries, -1, keepdims=True) + 1e-06)
        * queries.shape[-1] ** (-0.5)
    )
    keyed = keyed * lax.rsqrt(jnp.sum(keyed * keyed, -1, keepdims=True) + 1e-06)
    outputs = []
    for step in range(value.shape[1]):
        key_now = keyed[:, step]
        rates = decay[:, step][..., None]
        strength = beta[:, step][..., None]
        recalled = jnp.einsum("rhk,rhkv->rhv", key_now, states, precision=lax.Precision.HIGHEST)
        change = strength * (value[:, step].astype(jnp.float32) - rates * recalled)
        states = rates[..., None] * states + key_now[..., None] * change[..., None, :]
        reading = jnp.einsum(
            "rhk,rhkv->rhv", queries[:, step], states, precision=lax.Precision.HIGHEST
        )
        normed = reading * lax.rsqrt(jnp.mean(reading * reading, -1, keepdims=True) + 1e-06)
        outputs.append(
            (normed * jax.nn.silu(gate[:, step].astype(jnp.float32))).astype(jnp.bfloat16)
        )
    return (jnp.stack(outputs, axis=1), states)


def on_device(
    kv_cache,
    lin_states,
    row_order,
    prompt_lengths,
    att_query,
    new_kv,
    att_gate,
    lin_query,
    lin_key,
    lin_value,
    lin_decay,
    lin_beta,
    lin_gate,
):
    wide_count = lax.axis_size("wide")
    chips = wide_count // 2
    head_index = lax.axis_index("head")
    place = jnp.stack([head_index, lax.axis_index("wide")]).astype(jnp.int32)

    def across(array, distance):
        pairs = [(i, i ^ distance) for i in range(wide_count)]
        return lax.ppermute(array, "wide", pairs)

    query = lax.dynamic_slice_in_dim(att_query, (head_index % KVH) * GROUP, GROUP, 2)
    query = query.reshape(2, QROWS, HD)
    near = jnp.concatenate([query] + [across(query, 2 * t) for t in range(1, 4)], axis=0)

    first = across(gather_rows(row_order, prompt_lengths, place, kv_cache, 0, 1), 1)
    later = across(gather_rows(row_order, prompt_lengths, place, kv_cache, 1, 3), 1)
    swapped = [(first, 0), (later, 0), (later, 1), (later, 2)]

    asked = [near] + [across(near, 8 * u) for u in range(1, 4)]
    weights = []
    for chunk in range(CHUNKS):
        made = score_rows(
            row_order, prompt_lengths, place, asked[chunk], kv_cache,
            swapped[chunk][0], chunk, swapped[chunk][1],
        )
        weights.append(made)
    moved = [lax.ppermute(made, "head", [(0, 2), (1, 3)]) for made in weights]

    taken = lin_states.at[row_order].get(mode="promise_in_bounds", unique_indices=True)
    sent, _ = lax.optimization_barrier((taken.astype(jnp.bfloat16), weights[-1]))
    states = lax.all_to_all(sent, "wide", split_axis=0, concat_axis=2, tiled=True)

    payload = None
    for chunk in range(CHUNKS):
        payload = mix_rows(
            row_order, prompt_lengths, place, moved[chunk], kv_cache,
            swapped[chunk][0], chunk, swapped[chunk][1], payload,
        )
    same_core = [[2 * k + c for k in range(chips)] for c in range(2)]
    parts = lax.all_to_all(payload, "wide", 0, 0, tiled=True, axis_index_groups=same_core)
    low, high = combine(place, parts, query, new_kv)
    low_here = lax.ppermute(low, "head", [(2, 0), (3, 2)])
    high_here = lax.ppermute(high, "head", [(2, 1)])
    result = jnp.where(
        head_index == 3, high, jnp.where(head_index == 1, high_here, low_here)
    )
    att_out = (result * jax.nn.sigmoid(att_gate.astype(jnp.float32))).astype(jnp.bfloat16)

    lin_out, final_states = delta_rule(
        states.astype(jnp.float32), lin_query, lin_key, lin_value, lin_decay, lin_beta, lin_gate
    )
    return (att_out, lin_out, final_states)


def solution(mesh):
    placed = (
        P(None, "wide", "head"),
        P(None, "head", "wide", None),
        P(),
        P(),
        P("wide", None, None, None),
        P("wide", None, None),
        P("wide", None, "head"),
        P("wide", None, "head", None),
        P("wide", None, "head", None),
        P("wide", None, "head", None),
        P("wide", None, "head"),
        P("wide", None, "head"),
        P("wide", None, "head", None),
    )
    return jax.shard_map(
        on_device,
        mesh=mesh,
        in_specs=placed,
        out_specs=(
            P("wide", None, "head"),
            P("wide", None, "head", None),
            P("wide", "head", None, None),
        ),
        check_vma=False,
    )
```

time: 344 us -> 108 us (0.31)
  waiting for transfers between devices: 193 us -> 12.5 us
  local copies, waits for them, and re-layouts: 49.2 us -> 10.2 us
  Pallas kernels: 0 us -> 38.7 us
  blocking collectives: 36 us -> 0 us
  other arithmetic: 19.4 us -> 3.29 us
  starting transfers between devices: 30.9 us -> 34.7 us
    all_to_all x3 -> x2, waiting for transfers between devices: 193 us -> 2.51 us  [the longest x1 2.51 us: on_device(): lax.all_to_all(payload, 'wide', 0, 0, tiled=True, axis_index_groups=same_...]
    pallas_call x0 -> x11, Pallas kernels: none -> 38.7 us  [the longest x4 15.8 us: score_rows(): pl.pallas_call(functools.partial(score_kernel, chunk=chunk), name='score_...]
    all_gather x3 -> x0, blocking collectives: 36 us -> none  [combined_all(): lax.all_gather(part.astype(kind), axis)]
    ppermute x0 -> x14, starting transfers between devices: none -> 21.8 us  [the longest x8 12.2 us: across(): return lax.ppermute(array, 'wide', pairs)]
    reshape x6 -> x1, local copies, waits for them, and re-layouts: 20.8 us -> 0.01 us  [on_device(): query = query.reshape(2, QROWS, HD)]
    all_to_all x3 -> x2, starting transfers between devices: 30.9 us -> 12.9 us  [the longest x1 7.13 us: on_device(): lax.all_to_all(sent, 'wide', split_axis=0, concat_axis=2, tiled=True)]
    ppermute x0 -> x14, waiting for transfers between devices: none -> 10 us  [the longest x1 8.25 us: on_device(): low_here = lax.ppermute(low, 'head', [(2, 0), (3, 2)])]
    select_n x2 -> x1, other arithmetic: 8.21 us -> 0.01 us  [on_device(): lin_states.at[row_order].get(mode='promise_in_bounds', unique_indices=True)]
  transfers between devices with their start and end apart: 3 -> 16, of which waited for: 2 -> 5; matrix products, arithmetic and copies ran while one was open for 9% -> 12% of each run, Pallas kernels for 0% -> 29%
where the time goes in v1:
time: 108 us; the launch traced here: 107 us
  Pallas kernels  38.7 us (36%)
  starting transfers between devices  34.7 us (32%)
  waiting for transfers between devices  12.5 us (12%)
  local copies, waits for them, and re-layouts  10.2 us (9%)
  matrix products  6.67 us (6%)
  other arithmetic  3.29 us (3%)
    pallas_call x4, Pallas kernels, score_rows(): pl.pallas_call(functools.partial(score_kernel, chunk=chunk), name='score_...  15.8 us
    ppermute x8, starting transfers between devices, across(): return lax.ppermute(array, 'wide', pairs)  12.2 us
    pallas_call x4, Pallas kernels, mix_rows(): pl.pallas_call(mix_kernel, name='mix_rows', out_shape=jax.ShapeDtypeStruc...  12.2 us
    pallas_call x2, Pallas kernels, gather_rows(): pl.pallas_call(gather_kernel, name='gather_rows', out_shape=jax.ShapeDtyp...  9.02 us
    ppermute x1, waiting for transfers between devices, on_device(): low_here = lax.ppermute(low, 'head', [(2, 0), (3, 2)])  8.25 us
    unnamed x50, local copies, waits for them, and re-layouts  7.66 us
    ppermute x4, starting transfers between devices, on_device(): moved = [lax.ppermute(made, 'head', [(0, 2), (1, 3)]) for made in weights]  7.61 us
    all_to_all x1, starting transfers between devices, on_device(): lax.all_to_all(sent, 'wide', split_axis=0, concat_axis=2, tiled=True)  7.13 us
  transfers between devices with their start and end apart: 16, of which 5 were waited for; matrix products, arithmetic and copies ran while one was open for 12% of the time, Pallas kernels for 29%

profile of v1, /device:TPU:0, one launch (start us, length us, event | category | flops | bytes accessed | tf_op | source)
XLA Modules:
  0.0 107.1 jit_solution(4358730460604405048)
XLA Ops:
  0.7 0.6 pad_add_fusion.place
  1.3 6.2 %gather_rows.2 = bf16[24,256,256]{2,1,0:T(8,128)(2,1)} custom-call(s32[64]{0:T(128)} %order.19, s32[64]{0:T(128)} %lengths.19, s32[2]{0:T(128)} %pad_add_fusion.place, bf16[64,256,256]{2,1,0:T(8,128)(2,1)} %refs_3_.19, bf16[64,256,256]{2,1,0:T(8,128)(2,1)} %refs_3_.19, bf16[64,256,256]{2,1,0:T(8,128)(2,1)} %refs_3_.19, bf16[64,256,256]{2,1,0:T(8,128)(2,1)} %refs_3_.19), custom_call_target="tpu_custom_call" | custom-call | bytes 6291456 | tf_op jit(solution)/shard_map/gather_rows/pallas_call | solution.py:45
  7.5 4.2 %collective-permute-start.2 = (bf16[2,24,256]{2,1,0:T(8,128)(2,1)S(1)}, bf16[2,24,256]{2,1,0:T(8,128)(2,1)S(1)}, u32[]{:S(2)}, u32[]{:S(2)}) collective-permute-start(bf16[2,24,256]{2,1,0:T(8,128)(2,1)S(1)} %dynamic-slice_bitcast_fusion.query), channel_id=1, source_target_pairs={{0,6},{1,7},{2,4},{3,5},{4,2},{5,3},{6,0},{7,1},{8,14},{9,15},{10,... | collective-permute-start | bytes 73736 | tf_op jit(solution)/shard_map/ppermute | solution.py:313
  11.7 0.9 collective-permute-start
  12.7 2.8 %gather_rows.3 = bf16[8,256,256]{2,1,0:T(8,128)(2,1)} custom-call(s32[64]{0:T(128)} %order.19, s32[64]{0:T(128)} %lengths.19, s32[2]{0:T(128)} %pad_add_fusion.place, bf16[64,256,256]{2,1,0:T(8,128)(2,1)} %refs_3_.19, bf16[64,256,256]{2,1,0:T(8,128)(2,1)} %refs_3_.19, bf16[64,256,256]{2,1,0:T(8,128)(2,1)} %refs_3_.19, bf16[64,256,256]{2,1,0:T(8,128)(2,1)} %refs_3_.19), custom_call_target="tpu_custom_call" | custom-call | bytes 2097152 | tf_op jit(solution)/shard_map/gather_rows/pallas_call | solution.py:45
  16.3 0.7 collective-permute-done.1
  17.1 3.1 %collective-permute-start.3 = (bf16[8,24,256]{2,1,0:T(8,128)(2,1)S(1)}, bf16[8,24,256]{2,1,0:T(8,128)(2,1)S(1)}, u32[]{:S(2)}, u32[]{:S(2)}) collective-permute-start(bf16[8,24,256]{2,1,0:T(8,128)(2,1)S(1)} %pad_maximum_fusion.query), channel_id=1, source_target_pairs={{0,24},{1,25},{2,26},{3,27},{4,28},{5,29},{6,30},{7,31},{8,16},{9,... | collective-permute-start | bytes 294920 | tf_op jit(solution)/shard_map/ppermute | solution.py:313
  20.2 1.9 %gather_fusion = bf16[64,8,4,128]{3,2,1,0:T(4,128)(2,1)} fusion(f32[64,8,4,128]{3,2,1,0:T(4,128)S(1)} %copy-done, s32[1024]{0:T(1024)S(1)} %pad_clamp_fusion), kind=kCustom, calls=%fused_computation | custom fusion | bytes 1048832 | tf_op jit(solution)/shard_map/gather | solution.py:333
  22.1 0.9 collective-permute-done.3.query
  23.0 0.6 copy-done.13
  23.7 4.0 %score_rows.4 = bf16[24,4224]{1,0:T(8,128)(2,1)} custom-call(s32[64]{0:T(128)} %order.19, s32[64]{0:T(128)} %lengths.19, s32[2]{0:T(128)} %pad_add_fusion.place, bf16[8,24,256]{2,1,0:T(8,128)(2,1)} %copy-done.13, bf16[64,256,256]{2,1,0:T(8,128)(2,1)} %refs_3_.19, bf16[64,256,256]{2,1,0:T(8,128)(2,1)} %refs_3_.19, bf16[64,256,256]{2,1,0:T(8,128)(2,1)} %refs_3_.19, ...), custom_call_target="tpu_custom_call" | custom-call | flops 50331648 | bytes 2097152 | tf_op jit(solution)/shard_map/score_rows/pallas_call | solution.py:110
  27.6 7.1 %all-to-all-start.1 = ((bf16[64,8,4,128]{3,2,1,0:T(4,128)(2,1)}), bf16[64,8,4,128]{3,2,1,0:T(4,128)(2,1)S(1)}, u32[]{:S(2)}, u32[]{:S(2)}) async-start(bf16[64,8,4,128]{3,2,1,0:T(4,128)(2,1)} %gather_fusion), calls=%async_computation.1 | async-start | bytes 1048576 | tf_op jit(solution)/shard_map/all_to_all | solution.py:335
  34.8 3.4 %collective-permute-start.6 = (bf16[8,24,256]{2,1,0:T(8,128)(2,1)S(1)}, bf16[8,24,256]{2,1,0:T(8,128)(2,1)S(1)}, u32[]{:S(2)}, u32[]{:S(2)}) collective-permute-start(bf16[8,24,256]{2,1,0:T(8,128)(2,1)S(1)} %pad_maximum_fusion.query), channel_id=1, source_target_pairs={{0,16},{1,17},{2,18},{3,19},{4,20},{5,21},{6,22},{7,23},{8,24},{9,... | collective-permute-start | bytes 294920 | tf_op jit(solution)/shard_map/ppermute | solution.py:313
  38.2 0.6 collective-permute-start.8
  38.8 0.6 copy.41.fresh
  39.4 1.0 copy-done.1
  40.4 3.9 %score_rows.7 = bf16[24,4224]{1,0:T(8,128)(2,1)} custom-call(s32[64]{0:T(128)} %order.19, s32[64]{0:T(128)} %lengths.19, s32[2]{0:T(128)} %pad_add_fusion.place, bf16[8,24,256]{2,1,0:T(8,128)(2,1)} %copy-done.4, bf16[64,256,256]{2,1,0:T(8,128)(2,1)} %refs_3_.19, bf16[64,256,256]{2,1,0:T(8,128)(2,1)} %refs_3_.19, bf16[64,256,256]{2,1,0:T(8,128)(2,1)} %refs_3_.19, ...), custom_call_target="tpu_custom_call" | custom-call | flops 50331648 | bytes 2097152 | tf_op jit(solution)/shard_map/score_rows/pallas_call | solution.py:110
  44.3 3.2 %collective-permute-start.11 = (bf16[24,4224]{1,0:T(8,128)(2,1)}, bf16[24,4224]{1,0:T(8,128)(2,1)S(1)}, u32[]{:S(2)}, u32[]{:S(2)}) collective-permute-start(bf16[24,4224]{1,0:T(8,128)(2,1)} %score_rows.7), channel_id=1, source_target_pairs={{0,64},{32,96},{1,65},{33,97},{2,66},{34,98},{3,67},{35,99},{4,68}... | collective-permute-start | bytes 608264 | tf_op jit(solution)/shard_map/ppermute | solution.py:331
  47.4 1.3 %collective-permute-start.5 = (bf16[24,4224]{1,0:T(8,128)(2,1)S(1)}, bf16[24,4224]{1,0:T(8,128)(2,1)S(1)}, u32[]{:S(2)}, u32[]{:S(2)}) collective-permute-start(bf16[24,4224]{1,0:T(8,128)(2,1)S(1)} %copy-done.10), channel_id=1, source_target_pairs={{0,64},{32,96},{1,65},{33,97},{2,66},{34,98},{3,67},{35,99},{4,68}... | collective-permute-start | bytes 608264 | tf_op jit(solution)/shard_map/ppermute | solution.py:331
  48.8 0.6 copy-done.12
  49.4 4.0 %score_rows.5 = bf16[24,4224]{1,0:T(8,128)(2,1)} custom-call(s32[64]{0:T(128)} %order.19, s32[64]{0:T(128)} %lengths.19, s32[2]{0:T(128)} %pad_add_fusion.place, bf16[8,24,256]{2,1,0:T(8,128)(2,1)} %copy-done.12, bf16[64,256,256]{2,1,0:T(8,128)(2,1)} %refs_3_.19, bf16[64,256,256]{2,1,0:T(8,128)(2,1)} %refs_3_.19, bf16[64,256,256]{2,1,0:T(8,128)(2,1)} %refs_3_.19, ...), custom_call_target="tpu_custom_call" | custom-call | flops 50331648 | bytes 2097152 | tf_op jit(solution)/shard_map/score_rows/pallas_call | solution.py:110
  53.4 1.9 %collective-permute-start.7 = (bf16[24,4224]{1,0:T(8,128)(2,1)}, bf16[24,4224]{1,0:T(8,128)(2,1)S(1)}, u32[]{:S(2)}, u32[]{:S(2)}) collective-permute-start(bf16[24,4224]{1,0:T(8,128)(2,1)} %score_rows.5), channel_id=1, source_target_pairs={{0,64},{32,96},{1,65},{33,97},{2,66},{34,98},{3,67},{35,99},{4,68}... | collective-permute-start | bytes 608264 | tf_op jit(solution)/shard_map/ppermute | solution.py:331
  55.3 0.6 copy-done.11
  55.9 3.9 %score_rows.6 = bf16[24,4224]{1,0:T(8,128)(2,1)} custom-call(s32[64]{0:T(128)} %order.19, s32[64]{0:T(128)} %lengths.19, s32[2]{0:T(128)} %pad_add_fusion.place, bf16[8,24,256]{2,1,0:T(8,128)(2,1)} %copy-done.11, bf16[64,256,256]{2,1,0:T(8,128)(2,1)} %refs_3_.19, bf16[64,256,256]{2,1,0:T(8,128)(2,1)} %refs_3_.19, bf16[64,256,256]{2,1,0:T(8,128)(2,1)} %refs_3_.19, ...), custom_call_target="tpu_custom_call" | custom-call | flops 50331648 | bytes 2097152 | tf_op jit(solution)/shard_map/score_rows/pallas_call | solution.py:110
  59.8 1.3 %collective-permute-start.9 = (bf16[24,4224]{1,0:T(8,128)(2,1)}, bf16[24,4224]{1,0:T(8,128)(2,1)S(1)}, u32[]{:S(2)}, u32[]{:S(2)}) collective-permute-start(bf16[24,4224]{1,0:T(8,128)(2,1)} %score_rows.6), channel_id=1, source_target_pairs={{0,64},{32,96},{1,65},{33,97},{2,66},{34,98},{3,67},{35,99},{4,68}... | collective-permute-start | bytes 608264 | tf_op jit(solution)/shard_map/ppermute | solution.py:331
  61.1 0.7 copy-done.7
  61.8 3.1 %mix_rows.4.refs_5_ = bf16[16,48,384]{2,1,0:T(8,128)(2,1)} custom-call(s32[64]{0:T(128)} %order.19, s32[64]{0:T(128)} %lengths.19, s32[2]{0:T(128)} %pad_add_fusion.place, bf16[24,4224]{1,0:T(8,128)(2,1)} %copy-done.7, bf16[64,256,256]{2,1,0:T(8,128)(2,1)} %refs_3_.19, bf16[64,256,256]{2,1,0:T(8,128)(2,1)} %refs_3_.19, bf16[64,256,256]{2,1,0:T(8,128)(2,1)} %refs_3_.19, ...), custom_call_target="tpu_custom_call" | custom-call | flops 50331648 | bytes 2097152 | tf_op jit(solution)/shard_map/mix_rows/pallas_call | solution.py:175
  65.0 0.7 copy-done.9
  65.7 3.0 %mix_rows.5.refs_5_ = bf16[16,48,384]{2,1,0:T(8,128)(2,1)} custom-call(s32[64]{0:T(128)} %order.19, s32[64]{0:T(128)} %lengths.19, s32[2]{0:T(128)} %pad_add_fusion.place, bf16[24,4224]{1,0:T(8,128)(2,1)} %copy-done.9, bf16[64,256,256]{2,1,0:T(8,128)(2,1)} %refs_3_.19, bf16[64,256,256]{2,1,0:T(8,128)(2,1)} %refs_3_.19, ...), custom_call_target="tpu_custom_call", output_to_operand_aliasing={{}: (9, {})} | custom-call | flops 50331648 | bytes 2097152 | tf_op jit(solution)/shard_map/mix_rows/pallas_call | solution.py:175
  68.7 0.7 copy-done.8
  69.4 3.1 %mix_rows.6.refs_5_ = bf16[16,48,384]{2,1,0:T(8,128)(2,1)} custom-call(s32[64]{0:T(128)} %order.19, s32[64]{0:T(128)} %lengths.19, s32[2]{0:T(128)} %pad_add_fusion.place, bf16[24,4224]{1,0:T(8,128)(2,1)} %copy-done.8, bf16[64,256,256]{2,1,0:T(8,128)(2,1)} %refs_3_.19, bf16[64,256,256]{2,1,0:T(8,128)(2,1)} %refs_3_.19, ...), custom_call_target="tpu_custom_call", output_to_operand_aliasing={{}: (9, {})} | custom-call | flops 50331648 | bytes 2097152 | tf_op jit(solution)/shard_map/mix_rows/pallas_call | solution.py:175
  72.5 0.7 copy-done.6
  73.2 3.0 %mix_rows.7 = bf16[16,48,384]{2,1,0:T(8,128)(2,1)} custom-call(s32[64]{0:T(128)} %order.19, s32[64]{0:T(128)} %lengths.19, s32[2]{0:T(128)} %pad_add_fusion.place, bf16[24,4224]{1,0:T(8,128)(2,1)} %copy-done.6, bf16[64,256,256]{2,1,0:T(8,128)(2,1)} %refs_3_.19, bf16[64,256,256]{2,1,0:T(8,128)(2,1)} %refs_3_.19, ...), custom_call_target="tpu_custom_call", output_to_operand_aliasing={{}: (9, {})} | custom-call | flops 50331648 | bytes 2097152 | tf_op jit(solution)/shard_map/mix_rows/pallas_call | solution.py:175
  76.2 5.8 %all-to-all-start = ((bf16[16,48,384]{2,1,0:T(8,128)(2,1)}), bf16[16,48,384]{2,1,0:T(8,128)(2,1)S(1)}, u32[]{:S(2)}, u32[]{:S(2)}) async-start(bf16[16,48,384]{2,1,0:T(8,128)(2,1)} %mix_rows.7), calls=%async_computation | async-start | bytes 1179648 | tf_op jit(solution)/shard_map/all_to_all | solution.py:344
  82.8 1.1 %fusion.1 = f32[2,8,1,128]{3,2,1,0:T(1,128)S(1)} fusion(f32[2,8,128,1]{2,3,1,0:T(1,128)S(1)} %bitcast.134, bf16[2,8,128,128]{3,2,1,0:T(8,128)(2,1)S(1)} %bitcast.114, f32[2,8,128]{2,1,0:T(8,128)S(1)} %fusion.37, f32[2,8,128]{2,1,0:T(8,128)S(1)} %get-tuple-element.22, f32[2,8]{1,0:T(2,128)S(1)} %get-tuple-element.34), kind=kOutput, calls=%fused_computation.5 | convolution fusion | flops 4194304 | bytes 557120 | tf_op jit(solution)/shard_map/rhk,rhkv->rhv/dot_general | solution.py:281
  84.1 1.2 %fusion = f32[2,8,1,128]{3,2,1,0:T(1,128)S(1)} fusion(f32[2,8,128,1]{2,3,1,0:T(1,128)S(1)} %bitcast.132, bf16[2,8,128,128]{3,2,1,0:T(8,128)(2,1)S(1)} %bitcast.115, f32[2,8,128]{2,1,0:T(8,128)S(1)} %fusion.37, f32[2,8,128]{2,1,0:T(8,128)S(1)} %get-tuple-element.22, f32[2,8]{1,0:T(2,128)S(1)} %get-tuple-element.34), kind=kOutput, calls=%fused_computation.4 | convolution fusion | flops 4194304 | bytes 557120 | tf_op jit(solution)/shard_map/rhk,rhkv->rhv/dot_general | solution.py:278
  85.3 1.4 %fusion.3 = f32[2,8,1,128]{3,2,1,0:T(1,128)S(1)} fusion(f32[2,8,128,1]{2,3,1,0:T(1,128)S(1)} %bitcast.133, bf16[2,8,128,128]{3,2,1,0:T(8,128)(2,1)S(1)} %bitcast.116, f32[2,8,128]{2,1,0:T(8,128)S(1)} %fusion.36, f32[2,8,128]{2,1,0:T(8,128)S(1)} %get-tuple-element.23, f32[2,8]{1,0:T(2,128)S(1)} %get-tuple-element.35, f32[2,8,128]{2,1,0:T(8,128)S(1)} %fusion.37, ...), kind=kOutput, calls=%fused_computation.7 | convolution fusion | flops 4980736 | bytes 573568 | tf_op jit(solution)/shard_map/rhk,rhkv->rhv/dot_general | solution.py:281
  86.7 1.4 %fusion.2 = f32[2,8,1,128]{3,2,1,0:T(1,128)S(1)} fusion(f32[2,8,128,1]{2,3,1,0:T(1,128)S(1)} %bitcast.131, bf16[2,8,128,128]{3,2,1,0:T(8,128)(2,1)S(1)} %bitcast.117, f32[2,8,128]{2,1,0:T(8,128)S(1)} %fusion.36, f32[2,8,128]{2,1,0:T(8,128)S(1)} %get-tuple-element.23, f32[2,8]{1,0:T(2,128)S(1)} %get-tuple-element.35, f32[2,8,128]{2,1,0:T(8,128)S(1)} %fusion.37, ...), kind=kOutput, calls=%fused_computation.6 | convolution fusion | flops 4980736 | bytes 573568 | tf_op jit(solution)/shard_map/rhk,rhkv->rhv/dot_general | solution.py:278
  88.3 1.0 multiply_add_fusion
  89.3 1.0 fusion.46
  90.6 2.5 %all-to-all-done.parts = bf16[16,48,384]{2,1,0:T(8,128)(2,1)S(1)} async-done(((bf16[16,48,384]{2,1,0:T(8,128)(2,1)}), bf16[16,48,384]{2,1,0:T(8,128)(2,1)S(1)}, u32[]{:S(2)}, u32[]{:S(2)}) %all-to-all-start) | async-done | bytes 589856 | tf_op jit(solution)/shard_map/all_to_all | solution.py:344
  93.1 0.8 copy-done.3
  93.9 1.7 %combine_parts.1 = (f32[2,3,1024]{2,1,0:T(4,128)}, f32[2,3,1024]{2,1,0:T(4,128)}) custom-call(s32[2]{0:T(128)} %pad_add_fusion.place, bf16[16,48,384]{2,1,0:T(8,128)(2,1)} %copy-done.3, bf16[2,24,256]{2,1,0:T(8,128)(2,1)} %copy-done.5, bf16[2,3,1024]{2,1,0:T(4,128)(2,1)} %copy.41.fresh), custom_call_target="tpu_custom_call" | custom-call | flops 1179648 | bytes 589824 | tf_op jit(solution)/shard_map/combine_parts/pallas_call | solution.py:251
  95.6 0.7 collective-permute-start.12
  96.3 1.3 %collective-permute-start.13 = (f32[2,3,1024]{2,1,0:T(4,128)}, f32[2,3,1024]{2,1,0:T(4,128)S(1)}, u32[]{:S(2)}, u32[]{:S(2)}) collective-permute-start(f32[2,3,1024]{2,1,0:T(4,128)} %get-tuple-element.7), channel_id=1, source_target_pairs={{64,0},{96,64},{65,1},{97,65},{66,2},{98,66},{67,3},{99,67},{68,4}... | collective-permute-start | bytes 73736 | tf_op jit(solution)/shard_map/ppermute | solution.py:346
  97.6 0.6 pad_maximum_fusion.1
  98.2 8.3 %collective-permute-done.13 = f32[2,3,1024]{2,1,0:T(4,128)S(1)} collective-permute-done((f32[2,3,1024]{2,1,0:T(4,128)}, f32[2,3,1024]{2,1,0:T(4,128)S(1)}, u32[]{:S(2)}, u32[]{:S(2)}) %collective-permute-start.13) | collective-permute-done | bytes 24608 | tf_op jit(solution)/shard_map/ppermute | solution.py:346
  106.5 0.6 copy.53
  (90 shorter events, 2.4 us)
Async XLA Ops:
  0.6 19.6 %copy-start = (f32[64,8,4,128]{3,2,1,0:T(4,128)S(1)}, f32[64,8,4,128]{3,2,1,0:T(4,128)}, u32[]{:S(2)}) copy-start(f32[64,8,4,128]{3,2,1,0:T(4,128)} %param.14) | copy-start | bytes 3145732
  1.3 6.2 %copy-start.18 = (bf16[2,3,16,256]{3,2,1,0:T(8,128)(2,1)S(1)}, bf16[2,3,16,256]{3,2,1,0:T(8,128)(2,1)}, u32[]{:S(2)}) copy-start(bf16[2,3,16,256]{3,2,1,0:T(8,128)(2,1)} %param.17) | copy-start | bytes 147460
  7.5 15.6 %collective-permute-start.4 = (bf16[24,256,256]{2,1,0:T(8,128)(2,1)}, bf16[24,256,256]{2,1,0:T(8,128)(2,1)}, u32[]{:S(2)}, u32[]{:S(2)}) collective-permute-start(bf16[24,256,256]{2,1,0:T(8,128)(2,1)} %gather_rows.2), channel_id=1, source_target_pairs={{0,1},{1,0},{2,3},{3,2},{4,5},{5,4},{6,7},{7,6},{8,9},{9,8},{10,11... | collective-permute-start | bytes 9437192 | tf_op jit(solution)/shard_map/ppermute | solution.py:313
  7.5 9.6 %copy-start.5 = (bf16[2,24,256]{2,1,0:T(8,128)(2,1)}, bf16[2,24,256]{2,1,0:T(8,128)(2,1)S(1)}, u32[]{:S(2)}) copy-start(bf16[2,24,256]{2,1,0:T(8,128)(2,1)S(1)} %dynamic-slice_bitcast_fusion.query) | copy-start | bytes 73732
  7.5 8.0 %copy-start.16 = (bf16[2,3,4,128]{3,2,1,0:T(4,128)(2,1)S(1)}, bf16[2,3,4,128]{3,2,1,0:T(4,128)(2,1)}, u32[]{:S(2)}) copy-start(bf16[2,3,4,128]{3,2,1,0:T(4,128)(2,1)} %param.20) | copy-start | bytes 18436
  7.5 8.3 %copy-start.15 = (bf16[2,3,4,128]{3,2,1,0:T(4,128)(2,1)S(1)}, bf16[2,3,4,128]{3,2,1,0:T(4,128)(2,1)}, u32[]{:S(2)}) copy-start(bf16[2,3,4,128]{3,2,1,0:T(4,128)(2,1)} %param.21) | copy-start | bytes 18436
  7.5 8.8 %copy-start.14 = (s32[64]{0:T(128)S(1)}, s32[64]{0:T(128)}, u32[]{:S(2)}) copy-start(s32[64]{0:T(128)} %order.19) | copy-start | bytes 772
  7.5 8.8 %collective-permute-start.2 = (bf16[2,24,256]{2,1,0:T(8,128)(2,1)S(1)}, bf16[2,24,256]{2,1,0:T(8,128)(2,1)S(1)}, u32[]{:S(2)}, u32[]{:S(2)}) collective-permute-start(bf16[2,24,256]{2,1,0:T(8,128)(2,1)S(1)} %dynamic-slice_bitcast_fusion.query), channel_id=1, source_target_pairs={{0,6},{1,7},{2,4},{3,5},{4,2},{5,3},{6,0},{7,1},{8,14},{9,15},{10,... | collective-permute-start | bytes 73736 | tf_op jit(solution)/shard_map/ppermute | solution.py:313
  11.7 5.3 %collective-permute-start.1 = (bf16[2,24,256]{2,1,0:T(8,128)(2,1)S(1)}, bf16[2,24,256]{2,1,0:T(8,128)(2,1)S(1)}, u32[]{:S(2)}, u32[]{:S(2)}) collective-permute-start(bf16[2,24,256]{2,1,0:T(8,128)(2,1)S(1)} %dynamic-slice_bitcast_fusion.query), channel_id=1, source_target_pairs={{0,4},{1,5},{2,6},{3,7},{4,0},{5,1},{6,2},{7,3},{8,12},{9,13},{10,... | collective-permute-start | bytes 73736 | tf_op jit(solution)/shard_map/ppermute | solution.py:313
  11.7 5.3 %collective-permute-start = (bf16[2,24,256]{2,1,0:T(8,128)(2,1)S(1)}, bf16[2,24,256]{2,1,0:T(8,128)(2,1)S(1)}, u32[]{:S(2)}, u32[]{:S(2)}) collective-permute-start(bf16[2,24,256]{2,1,0:T(8,128)(2,1)S(1)} %dynamic-slice_bitcast_fusion.query), channel_id=1, source_target_pairs={{0,2},{1,3},{2,0},{3,1},{4,6},{5,7},{6,4},{7,5},{8,10},{9,11},{10,... | collective-permute-start | bytes 73736 | tf_op jit(solution)/shard_map/ppermute | solution.py:313
  15.5 23.8 %collective-permute-start.10 = (bf16[8,256,256]{2,1,0:T(8,128)(2,1)}, bf16[8,256,256]{2,1,0:T(8,128)(2,1)S(1)}, u32[]{:S(2)}, u32[]{:S(2)}) collective-permute-start(bf16[8,256,256]{2,1,0:T(8,128)(2,1)} %gather_rows.3), channel_id=1, source_target_pairs={{0,1},{1,0},{2,3},{3,2},{4,5},{5,4},{6,7},{7,6},{8,9},{9,8},{10,11... | collective-permute-start | bytes 3145736 | tf_op jit(solution)/shard_map/ppermute | solution.py:313
  17.1 21.1 %copy-start.4 = (bf16[8,24,256]{2,1,0:T(8,128)(2,1)}, bf16[8,24,256]{2,1,0:T(8,128)(2,1)S(1)}, u32[]{:S(2)}) copy-start(bf16[8,24,256]{2,1,0:T(8,128)(2,1)S(1)} %pad_maximum_fusion.query) | copy-start | bytes 294916
  17.1 5.9 %collective-permute-start.3 = (bf16[8,24,256]{2,1,0:T(8,128)(2,1)S(1)}, bf16[8,24,256]{2,1,0:T(8,128)(2,1)S(1)}, u32[]{:S(2)}, u32[]{:S(2)}) collective-permute-start(bf16[8,24,256]{2,1,0:T(8,128)(2,1)S(1)} %pad_maximum_fusion.query), channel_id=1, source_target_pairs={{0,24},{1,25},{2,26},{3,27},{4,28},{5,29},{6,30},{7,31},{8,16},{9,... | collective-permute-start | bytes 294920 | tf_op jit(solution)/shard_map/ppermute | solution.py:313
  22.1 16.6 %copy-start.22 = (f32[2,3,8]{2,0,1:T(2,128)S(1)}, f32[2,3,8]{2,0,1:T(2,128)}, u32[]{:S(2)}) copy-start(f32[2,3,8]{2,0,1:T(2,128)} %param.23) | copy-start | bytes 580
  22.1 16.6 %copy-start.17 = (bf16[2,3,1024]{2,0,1:T(2,128)(2,1)S(1)}, bf16[2,3,1024]{2,0,1:T(2,128)(2,1)}, u32[]{:S(2)}) copy-start(bf16[2,3,1024]{2,0,1:T(2,128)(2,1)} %param.18) | copy-start | bytes 36868
  23.0 0.6 copy-start.13
  27.6 48.6 %all-to-all-start.1 = ((bf16[64,8,4,128]{3,2,1,0:T(4,128)(2,1)}), bf16[64,8,4,128]{3,2,1,0:T(4,128)(2,1)S(1)}, u32[]{:S(2)}, u32[]{:S(2)}) async-start(bf16[64,8,4,128]{3,2,1,0:T(4,128)(2,1)} %gather_fusion), calls=%async_computation.1 | async-start | bytes 1048576 | tf_op jit(solution)/shard_map/all_to_all | solution.py:335
  34.8 14.0 %collective-permute-start.6 = (bf16[8,24,256]{2,1,0:T(8,128)(2,1)S(1)}, bf16[8,24,256]{2,1,0:T(8,128)(2,1)S(1)}, u32[]{:S(2)}, u32[]{:S(2)}) collective-permute-start(bf16[8,24,256]{2,1,0:T(8,128)(2,1)S(1)} %pad_maximum_fusion.query), channel_id=1, source_target_pairs={{0,16},{1,17},{2,18},{3,19},{4,20},{5,21},{6,22},{7,23},{8,24},{9,... | collective-permute-start | bytes 294920 | tf_op jit(solution)/shard_map/ppermute | solution.py:313
  38.2 17.1 %collective-permute-start.8 = (bf16[8,24,256]{2,1,0:T(8,128)(2,1)S(1)}, bf16[8,24,256]{2,1,0:T(8,128)(2,1)S(1)}, u32[]{:S(2)}, u32[]{:S(2)}) collective-permute-start(bf16[8,24,256]{2,1,0:T(8,128)(2,1)S(1)} %pad_maximum_fusion.query), channel_id=1, source_target_pairs={{0,8},{1,9},{2,10},{3,11},{4,12},{5,13},{6,14},{7,15},{8,0},{9,1},... | collective-permute-start | bytes 294920 | tf_op jit(solution)/shard_map/ppermute | solution.py:313
  39.4 8.0 %copy-start.10 = (bf16[24,4224]{1,0:T(8,128)(2,1)S(1)}, bf16[24,4224]{1,0:T(8,128)(2,1)}, u32[]{:S(2)}) copy-start(bf16[24,4224]{1,0:T(8,128)(2,1)} %score_rows.4) | copy-start | bytes 608260
  39.4 1.0 copy-start.1
  44.3 16.8 %collective-permute-start.11 = (bf16[24,4224]{1,0:T(8,128)(2,1)}, bf16[24,4224]{1,0:T(8,128)(2,1)S(1)}, u32[]{:S(2)}, u32[]{:S(2)}) collective-permute-start(bf16[24,4224]{1,0:T(8,128)(2,1)} %score_rows.7), channel_id=1, source_target_pairs={{0,64},{32,96},{1,65},{33,97},{2,66},{34,98},{3,67},{35,99},{4,68}... | collective-permute-start | bytes 608264 | tf_op jit(solution)/shard_map/ppermute | solution.py:331
  47.4 25.0 %collective-permute-start.5 = (bf16[24,4224]{1,0:T(8,128)(2,1)S(1)}, bf16[24,4224]{1,0:T(8,128)(2,1)S(1)}, u32[]{:S(2)}, u32[]{:S(2)}) collective-permute-start(bf16[24,4224]{1,0:T(8,128)(2,1)S(1)} %copy-done.10), channel_id=1, source_target_pairs={{0,64},{32,96},{1,65},{33,97},{2,66},{34,98},{3,67},{35,99},{4,68}... | collective-permute-start | bytes 608264 | tf_op jit(solution)/shard_map/ppermute | solution.py:331
  48.8 0.6 copy-start.12
  53.4 7.7 %copy-start.23 = (f32[2,3,8]{2,0,1:T(2,128)S(1)}, f32[2,3,8]{2,0,1:T(2,128)}, u32[]{:S(2)}) copy-start(f32[2,3,8]{2,0,1:T(2,128)} %param.24) | copy-start | bytes 580
  53.4 15.4 %collective-permute-start.7 = (bf16[24,4224]{1,0:T(8,128)(2,1)}, bf16[24,4224]{1,0:T(8,128)(2,1)S(1)}, u32[]{:S(2)}, u32[]{:S(2)}) collective-permute-start(bf16[24,4224]{1,0:T(8,128)(2,1)} %score_rows.5), channel_id=1, source_target_pairs={{0,64},{32,96},{1,65},{33,97},{2,66},{34,98},{3,67},{35,99},{4,68}... | collective-permute-start | bytes 608264 | tf_op jit(solution)/shard_map/ppermute | solution.py:331
  55.3 0.6 copy-start.11
  59.8 5.2 %collective-permute-start.9 = (bf16[24,4224]{1,0:T(8,128)(2,1)}, bf16[24,4224]{1,0:T(8,128)(2,1)S(1)}, u32[]{:S(2)}, u32[]{:S(2)}) collective-permute-start(bf16[24,4224]{1,0:T(8,128)(2,1)} %score_rows.6), channel_id=1, source_target_pairs={{0,64},{32,96},{1,65},{33,97},{2,66},{34,98},{3,67},{35,99},{4,68}... | collective-permute-start | bytes 608264 | tf_op jit(solution)/shard_map/ppermute | solution.py:331
  61.1 0.7 copy-start.7
  65.0 0.7 copy-start.9
  68.7 0.7 copy-start.8
  72.5 10.3 %copy-start.20 = (bf16[2,3,8,128]{3,2,1,0:T(8,128)(2,1)S(1)}, bf16[2,3,8,128]{3,2,1,0:T(8,128)(2,1)}, u32[]{:S(2)}) copy-start(bf16[2,3,8,128]{3,2,1,0:T(8,128)(2,1)} %param.22) | copy-start | bytes 36868
  72.5 0.7 copy-start.6
  76.2 16.9 %all-to-all-start = ((bf16[16,48,384]{2,1,0:T(8,128)(2,1)}), bf16[16,48,384]{2,1,0:T(8,128)(2,1)S(1)}, u32[]{:S(2)}, u32[]{:S(2)}) async-start(bf16[16,48,384]{2,1,0:T(8,128)(2,1)} %mix_rows.7), calls=%async_computation | async-start | bytes 1179648 | tf_op jit(solution)/shard_map/all_to_all | solution.py:344
  85.3 5.2 %copy-start.19 = (bf16[2,3,8,128]{3,2,1,0:T(8,128)(2,1)S(1)}, bf16[2,3,8,128]{3,2,1,0:T(8,128)(2,1)}, u32[]{:S(2)}) copy-start(bf16[2,3,8,128]{3,2,1,0:T(8,128)(2,1)} %param.25) | copy-start | bytes 36868
  86.7 19.7 %copy-start.21 = (bf16[2,3,1024]{2,0,1:T(2,128)(2,1)S(1)}, bf16[2,3,1024]{2,0,1:T(2,128)(2,1)}, u32[]{:S(2)}) copy-start(bf16[2,3,1024]{2,0,1:T(2,128)(2,1)} %param.19) | copy-start | bytes 36868
  89.3 17.8 %copy-start.2 = (f32[2,8,128,128]{3,2,1,0:T(8,128)}, f32[2,8,128,128]{3,2,1,0:T(8,128)S(1)}, u32[]{:S(2)}) copy-start(f32[2,8,128,128]{3,2,1,0:T(8,128)S(1)} %multiply_add_fusion) | copy-start | bytes 3145732
  93.1 0.8 copy-start.3
  95.6 2.6 %collective-permute-start.12 = (f32[2,3,1024]{2,1,0:T(4,128)}, f32[2,3,1024]{2,1,0:T(4,128)S(1)}, u32[]{:S(2)}, u32[]{:S(2)}) collective-permute-start(f32[2,3,1024]{2,1,0:T(4,128)} %get-tuple-element.6), channel_id=1, source_target_pairs={{64,32},{65,33},{66,34},{67,35},{68,36},{69,37},{70,38},{71,39},{7... | collective-permute-start | bytes 73736 | tf_op jit(solution)/shard_map/ppermute | solution.py:347
  96.3 10.2 %collective-permute-start.13 = (f32[2,3,1024]{2,1,0:T(4,128)}, f32[2,3,1024]{2,1,0:T(4,128)S(1)}, u32[]{:S(2)}, u32[]{:S(2)}) collective-permute-start(f32[2,3,1024]{2,1,0:T(4,128)} %get-tuple-element.7), channel_id=1, source_target_pairs={{64,0},{96,64},{65,1},{97,65},{66,2},{98,66},{67,3},{99,67},{68,4}... | collective-permute-start | bytes 73736 | tf_op jit(solution)/shard_map/ppermute | solution.py:346

commit v2 on v1

v2 whole, which is shorter than its diff:
```python
import functools

import jax
import jax.numpy as jnp
from jax import lax
from jax.experimental import pallas as pl
from jax.experimental.pallas import tpu as pltpu
from jax.sharding import PartitionSpec as P

HQ = 16
KVH = 2
HD = 256
STEPS = 3
GROUP = HQ // KVH
QROWS = STEPS * GROUP
LANES = 128
NEGATIVE = -1e30

CHUNK = 8
CHUNKS = 4
NT = (((1,), (1,)), ((), ()))
LIMIT = 16 * 2**20
VMEM = pl.BlockSpec(memory_space=pltpu.VMEM)
SMEM = pl.BlockSpec(memory_space=pltpu.SMEM)
ANY = pl.BlockSpec(memory_space=pltpu.HBM)
PARAMS = pltpu.CompilerParams(vmem_limit_bytes=LIMIT)
FREE = pl.CostEstimate(flops=0, bytes_accessed=0, transcendentals=0)

ROWS = 64
PLACE = 2 * ROWS


def near(array):
    return pltpu.with_memory_space_constraint(array, pltpu.VMEM)


def far(array):
    return pltpu.with_memory_space_constraint(array, pltpu.HBM)


def prefill_row(info, slot, other=0):
    core = (info[PLACE + 1] & 1) ^ other
    return info[4 * (slot // 2) + 2 * core + slot % 2]


def gather_kernel(info, cache, *refs, first):
    outs, (held, arrived, left) = refs[:-3], refs[-3:]
    size = outs[0].shape[0]
    count = held.shape[0]
    reads = [
        pltpu.make_async_copy(cache.at[prefill_row(info, first + n, 1)], held.at[n], arrived.at[n])
        for n in range(count)
    ]
    writes = [
        pltpu.make_async_copy(held.at[n], outs[n // size].at[n % size], left.at[n])
        for n in range(count)
    ]
    for read in reads:
        read.start()
    for read, write in zip(reads, writes):
        read.wait()
        write.start()
    for write in writes:
        write.wait()


def gather_rows(info, cache, first, count, parts):
    span, dtype = cache.shape[1], cache.dtype
    copies = pltpu.SemaphoreType.DMA((count,))
    return pl.pallas_call(
        functools.partial(gather_kernel, first=first),
        name="gather_rows",
        out_shape=[pltpu.HBM((count // parts, span, HD), dtype)] * parts,
        in_specs=[SMEM, ANY],
        out_specs=[ANY] * parts,
        scratch_shapes=[pltpu.VMEM((count, span, HD), dtype), copies, copies],
        compiler_params=PARAMS,
        cost_estimate=FREE,
    )(info, far(cache))


def hold_kernel(array, out):
    pass


def hold(array, cost):
    return pl.pallas_call(
        hold_kernel,
        name="hold",
        out_shape=pltpu.VMEM(array.shape, array.dtype),
        in_specs=[VMEM],
        out_specs=VMEM,
        input_output_aliases={0: 0},
        compiler_params=PARAMS,
        cost_estimate=pl.CostEstimate(flops=cost, bytes_accessed=0, transcendentals=0),
    )(near(array))


def fetches(info, cache, swapped, own, other, arrived, chunk):
    copies = [
        pltpu.make_async_copy(
            cache.at[prefill_row(info, chunk * CHUNK + n)], own.at[n], arrived.at[n]
        )
        for n in range(CHUNK)
    ]
    if swapped is not None:
        copies.append(pltpu.make_async_copy(swapped, other, arrived.at[CHUNK]))
    return copies


def start(copies):
    for copy in copies:
        copy.start()


def wait(copies):
    for copy in copies:
        copy.wait()


ARRIVED = pltpu.SemaphoreType.DMA((CHUNK + 1,))


def load_kernel(info, cache, own, arrived, *, chunk):
    copies = fetches(info, cache, None, own, None, arrived, chunk)
    start(copies)
    wait(copies)


def load_rows(info, cache, chunk):
    return pl.pallas_call(
        functools.partial(load_kernel, chunk=chunk),
        name="load_rows",
        out_shape=pltpu.VMEM((CHUNK, *cache.shape[1:]), cache.dtype),
        in_specs=[SMEM, ANY],
        out_specs=VMEM,
        scratch_shapes=[ARRIVED],
        compiler_params=PARAMS,
        cost_estimate=FREE,
    )(info, far(cache))


def score_kernel(info, query, own, other, *refs, chunk):
    if chunk + 1 < CHUNKS:
        cache, swapped, out, own_next, other_next, arrived = refs
    else:
        (out,) = refs
    span = own.shape[1]
    width = 2 * span

    @pl.when(info[PLACE] < 2)
    def _():
        if chunk + 1 < CHUNKS:
            copies = fetches(info, cache, swapped, own_next, other_next, arrived, chunk + 1)
            start(copies)
        lane = lax.broadcasted_iota(jnp.int32, (QROWS, LANES), 1)
        column = lax.broadcasted_iota(jnp.int32, (QROWS, span), 1)
        wide = info[PLACE + 1]
        position = jnp.concatenate([column + wide * span, column + (wide ^ 1) * span], axis=1)
        extra = jnp.zeros((QROWS, LANES), jnp.float32)
        for n in range(CHUNK):
            slot = chunk * CHUNK + n
            q = query[slot]
            scores = jnp.concatenate(
                [
                    lax.dot_general(q, own[n], NT, preferred_element_type=jnp.float32),
                    lax.dot_general(q, other[n], NT, preferred_element_type=jnp.float32),
                ],
                axis=1,
            ) * (HD ** (-0.5))
            valid = position < info[ROWS + prefill_row(info, slot)]
            scores = jnp.where(valid, scores, NEGATIVE)
            top = jnp.max(scores, axis=1, keepdims=True)
            top = top.astype(jnp.bfloat16).astype(jnp.float32)
            weights = jnp.where(valid, jnp.exp(scores - top), 0.0)
            total = jnp.sum(weights, axis=1, keepdims=True)
            coarse = total.astype(jnp.bfloat16).astype(jnp.float32)
            out[:, n * width : (n + 1) * width] = weights.astype(out.dtype)
            extra = jnp.where(lane == n, top, extra)
            extra = jnp.where(lane == n + CHUNK, coarse, extra)
            extra = jnp.where(lane == n + 2 * CHUNK, total - coarse, extra)
        out[:, CHUNK * width :] = extra.astype(out.dtype)
        if chunk + 1 < CHUNKS:
            wait(copies)


def score_rows(info, query, own, other, cache, swapped, chunk):
    span, dtype = cache.shape[1], cache.dtype
    last = chunk + 1 == CHUNKS
    rows = pltpu.VMEM((CHUNK, span, HD), dtype)
    made = pl.pallas_call(
        functools.partial(score_kernel, chunk=chunk),
        name="score_rows",
        out_shape=[pltpu.VMEM((QROWS, CHUNK * 2 * span + LANES), jnp.bfloat16)]
        + ([] if last else [rows, rows]),
        in_specs=[SMEM, VMEM, VMEM, VMEM] + ([] if last else [ANY, ANY]),
        out_specs=[VMEM] if last else [VMEM] * 3,
        scratch_shapes=[] if last else [ARRIVED],
        compiler_params=PARAMS,
        cost_estimate=FREE,
    )(
        info, near(query), near(own), near(other),
        *(() if last else (far(cache), far(swapped))),
    )
    return (made[0], None, None) if last else made


LINES = 2 * QROWS
SLAB = 2 * LINES + 16
EXTRAS = 8


def mix_kernel(info, weights, *refs, chunk):
    last = chunk + 1 == CHUNKS
    fetch_last = chunk + 2 == CHUNKS
    made, left = refs[-2:]
    if last:
        own, other, _, out = refs[:4]
    elif fetch_last:
        cache, swapped, swapped_last, _, out, own_last, other_last = refs[:7]
        own, other, arrived, arrived_last = refs[7:11]
    else:
        cache, swapped = refs[:2]
        out, own, other, arrived = refs[-6:-2]
    span = own.shape[1]
    width = 2 * span

    @pl.when(info[PLACE] >= 2)
    def _():
        if not last:
            copies = fetches(info, cache, swapped, own, other, arrived, chunk)
            start(copies)
        if fetch_last:
            copies_last = fetches(
                info, cache, swapped_last, own_last, other_last, arrived_last, chunk + 1
            )
            start(copies_last)
        extra = weights[:, CHUNK * width :].astype(jnp.float32)
        extra = jnp.concatenate([extra, jnp.zeros((LANES - QROWS, LANES), jnp.float32)], axis=0)
        extra = jnp.transpose(extra)
        blank = jnp.zeros((16 - 6, LANES), jnp.float32)
        if not last:
            wait(copies)
        for pair in range(CHUNK // 2):
            rows, lines = [], []
            for n in (2 * pair, 2 * pair + 1):
                at = n * width
                rows.append(
                    jnp.dot(
                        weights[:, at : at + span], own[n], preferred_element_type=jnp.float32
                    )
                    + jnp.dot(
                        weights[:, at + span : at + width],
                        other[n],
                        preferred_element_type=jnp.float32,
                    )
                )
                lines += [extra[n + k * CHUNK : n + k * CHUNK + 1] for k in range(3)]
            slab = [row[:, :LANES] for row in rows] + [row[:, LANES:] for row in rows]
            made[pair] = jnp.concatenate([*slab, *lines, blank], axis=0).astype(made.dtype)
        copy = pltpu.make_async_copy(
            made, out.at[pl.ds(chunk * CHUNK // 2, CHUNK // 2)], left.at[0]
        )
        copy.start()
        copy.wait()
        if fetch_last:
            wait(copies_last)


def mix_rows(info, weights, cache, swapped, chunk, before, rows, cost):
    last = chunk + 1 == CHUNKS
    fetch_last = chunk + 2 == CHUNKS
    held = pltpu.VMEM((CHUNK, *cache.shape[1:]), cache.dtype)
    payload = pltpu.HBM((CHUNK * CHUNKS // 2, SLAB, LANES), jnp.bfloat16)
    if last:
        in_specs = [SMEM, VMEM, VMEM, VMEM]
        operands = [info, near(weights), near(rows[0]), near(rows[1])]
    else:
        in_specs = [SMEM, VMEM, ANY, ANY]
        operands = [info, near(weights), far(cache), far(swapped[chunk])]
    if fetch_last:
        in_specs.append(ANY)
        operands.append(far(swapped[chunk + 1]))
    aliases = {}
    if before is not None:
        in_specs.append(ANY)
        aliases = {len(operands): 0}
        operands.append(far(before))
    made = pl.pallas_call(
        functools.partial(mix_kernel, chunk=chunk),
        name="mix_rows",
        out_shape=[payload] + ([held, held] if fetch_last else []),
        in_specs=in_specs,
        out_specs=[ANY] + ([VMEM, VMEM] if fetch_last else []),
        input_output_aliases=aliases,
        scratch_shapes=([] if last else [held, held, ARRIVED])
        + ([ARRIVED] if fetch_last else [])
        + [pltpu.VMEM((CHUNK // 2, SLAB, LANES), jnp.bfloat16), pltpu.SemaphoreType.DMA((1,))],
        compiler_params=PARAMS,
        cost_estimate=pl.CostEstimate(flops=cost, bytes_accessed=0, transcendentals=0),
    )(*operands)
    return made[0], made[1:]


def combine_kernel(info, parts, query, fresh, low, high):
    @pl.when(info[PLACE] >= 2)
    def _():
        chips = parts.shape[0]
        second = info[PLACE] & 1
        step = lax.broadcasted_iota(jnp.int32, (QROWS, STEPS), 0) // GROUP
        time = lax.broadcasted_iota(jnp.int32, (QROWS, STEPS), 1)
        keep = time <= step
        half = KVH * HD
        extras = [parts[chip, 2 * LINES :].astype(jnp.float32)[:EXTRAS] for chip in range(chips)]
        extras = jnp.transpose(jnp.concatenate(extras, axis=0))

        def line(chip, which):
            at = chip * EXTRAS + which
            return jnp.concatenate(
                [extras[:QROWS, at : at + 1], extras[:QROWS, at + 3 : at + 4]], axis=0
            )

        tops = [line(chip, 0) for chip in range(chips)]
        totals = [line(chip, 1) + line(chip, 2) for chip in range(chips)]
        scores, values = [], []
        for row in range(2):
            news = fresh[row].astype(jnp.float32)
            keys = jnp.where(second == 1, news[:, HD:half], news[:, :HD])
            values.append(jnp.where(second == 1, news[:, half + HD :], news[:, half : half + HD]))
            q = jnp.where(second == 1, query[row, :, GROUP:], query[row, :, :GROUP])
            q = q.reshape(QROWS, HD).astype(jnp.float32)
            columns = [
                jnp.sum(q * keys[t : t + 1], axis=1, keepdims=True) for t in range(STEPS)
            ]
            score = jnp.concatenate(columns, axis=1) * (HD ** (-0.5))
            scores.append(jnp.where(keep, score, NEGATIVE))
        score = jnp.concatenate(scores, axis=0)
        keep = jnp.concatenate([keep, keep], axis=0)
        top = jnp.max(score, axis=1, keepdims=True)
        for chip in range(chips):
            top = jnp.maximum(top, tops[chip])
        probs = jnp.where(keep, jnp.exp(score - top), 0.0)
        total = jnp.sum(probs, axis=1, keepdims=True)
        probs = probs.astype(jnp.bfloat16).astype(jnp.float32)
        mixed = []
        for row in range(2):
            mine = probs[row * QROWS : (row + 1) * QROWS]
            mixed.append(sum(mine[:, t : t + 1] * values[row][t : t + 1] for t in range(STEPS)))
        mixed = jnp.concatenate(mixed, axis=0)
        halves = [mixed[:, :LANES], mixed[:, LANES:]]
        for chip in range(chips):
            factor = jnp.exp(tops[chip] - top)
            total = total + factor * totals[chip]
            for k in range(2):
                part = parts[chip, k * LINES : (k + 1) * LINES].astype(jnp.float32)
                halves[k] = halves[k] + factor * part
        result = jnp.concatenate(halves, axis=1) / total
        heads = GROUP // 2
        for row in range(2):
            for s in range(STEPS):
                for a in range(heads):
                    at = row * QROWS + s * GROUP + a
                    low[row, s : s + 1, a * HD : (a + 1) * HD] = result[at : at + 1]
                    at = at + heads
                    high[row, s : s + 1, a * HD : (a + 1) * HD] = result[at : at + 1]


def combine(info, parts, query, fresh):
    heads = GROUP // 2
    shape = pltpu.VMEM((2, STEPS, heads * HD), jnp.float32)
    return pl.pallas_call(
        combine_kernel,
        name="combine_parts",
        out_shape=(shape, shape),
        in_specs=[SMEM, VMEM, VMEM, VMEM],
        out_specs=(VMEM, VMEM),
        compiler_params=PARAMS,
        cost_estimate=FREE,
    )(info, near(parts), near(query), near(fresh))


def delta_kernel(decay, beta, states, query, key, value, gate, out, final, rows):
    batch, steps, heads_k, width = key.shape
    heads_v = value.shape[2]
    ratio = heads_v // heads_k
    keys_at = batch * steps * heads_k

    def column(row, step, head):
        return (row * steps + step) * heads_k + head

    rows[...] = jnp.zeros_like(rows)
    for row in range(batch):
        for step in range(steps):
            at = column(row, step, 0)
            q = query[row, step].astype(jnp.float32)
            k = key[row, step].astype(jnp.float32)
            q = q * lax.rsqrt(jnp.sum(q * q, -1, keepdims=True) + 1e-06) * width ** (-0.5)
            k = k * lax.rsqrt(jnp.sum(k * k, -1, keepdims=True) + 1e-06)
            rows[at : at + heads_k] = q
            rows[keys_at + at : keys_at + at + heads_k] = k
    columns = jnp.transpose(rows[...])
    for row in range(batch):
        made = [[] for _ in range(steps)]
        values = [value[row, step].astype(jnp.float32) for step in range(steps)]
        for head in range(heads_v):
            state = states[row, head].astype(jnp.float32)
            for step in range(steps):
                at = column(row, step, head // ratio)
                q = columns[:, at : at + 1]
                k = columns[:, keys_at + at : keys_at + at + 1]
                rate = decay[row, step, head]
                recalled = jnp.sum(k * state, axis=0, keepdims=True)
                change = beta[row, step, head] * (values[step][head : head + 1] - rate * recalled)
                state = rate * state + k * change
                made[step].append(jnp.sum(q * state, axis=0, keepdims=True))
            final[row, head] = state
        for step in range(steps):
            read = jnp.concatenate(made[step], axis=0)
            read = read * lax.rsqrt(jnp.mean(read * read, -1, keepdims=True) + 1e-06)
            level = gate[row, step].astype(jnp.float32)
            out[row, step] = (read * (level * jax.nn.sigmoid(level))).astype(out.dtype)


def delta_rule(states, query, key, value, decay, beta, gate):
    width = key.shape[-1]
    return pl.pallas_call(
        delta_kernel,
        name="delta_rule",
        out_shape=(
            jax.ShapeDtypeStruct(value.shape, jnp.bfloat16),
            jax.ShapeDtypeStruct(states.shape, jnp.float32),
        ),
        in_specs=[SMEM, SMEM] + [VMEM] * 5,
        out_specs=(VMEM, VMEM),
        scratch_shapes=[pltpu.VMEM((width, width), jnp.float32)],
        compiler_params=PARAMS,
        cost_estimate=FREE,
    )(decay, beta, states, query, key, value, gate)


def on_device(
    kv_cache,
    lin_states,
    row_order,
    prompt_lengths,
    att_query,
    new_kv,
    att_gate,
    lin_query,
    lin_key,
    lin_value,
    lin_decay,
    lin_beta,
    lin_gate,
):
    wide_count = lax.axis_size("wide")
    chips = wide_count // 2
    head_index = lax.axis_index("head")
    place = jnp.stack([head_index, lax.axis_index("wide")]).astype(jnp.int32)
    info = jnp.concatenate([row_order, prompt_lengths, place])

    def across(array):
        pairs = [(i, i ^ 1) for i in range(wide_count)]
        return lax.ppermute(array, "wide", pairs)

    def after(array, *others):
        return lax.optimization_barrier((array, *others))[0]

    same_core = [[2 * k + c for k in range(chips)] for c in range(2)]

    def between_chips(array):
        return lax.all_to_all(array, "wide", 0, 0, tiled=True, axis_index_groups=same_core)

    mine = lax.dynamic_slice_in_dim(att_query, (head_index % KVH) * GROUP, GROUP, 2)
    copies = jnp.broadcast_to(mine.reshape(1, 2, QROWS, HD), (chips, 2, QROWS, HD))
    query = hold(between_chips(copies.reshape(2 * chips, QROWS, HD)), 30 * 10**9)

    taken = lin_states.at[row_order].get(mode="promise_in_bounds", unique_indices=True)
    taken = taken.astype(jnp.bfloat16)
    made = gather_rows(info, kv_cache, 0, CHUNK, 1)
    made += gather_rows(
        after(info, taken, *made), kv_cache, CHUNK, CHUNK * (CHUNKS - 1), CHUNKS - 1
    )
    swapped = [across(part) for part in made]

    weights = []
    own, other = load_rows(after(info, *made), kv_cache, 0), swapped[0]
    for chunk in range(CHUNKS):
        following = swapped[min(chunk + 1, CHUNKS - 1)]
        made, own, other = score_rows(info, query, own, other, kv_cache, following, chunk)
        weights.append(made)
    moved = [lax.ppermute(made, "head", [(0, 2), (1, 3)]) for made in weights]

    states = lax.all_to_all(
        after(taken, weights[-1]), "wide", split_axis=0, concat_axis=2, tiled=True
    )

    payload, rows = None, None
    for chunk in range(CHUNKS):
        cost = 10 * 10**9 if chunk == CHUNKS - 1 else 100 * 10**6
        payload, rows = mix_rows(
            info, moved[chunk], kv_cache, swapped, chunk, payload, rows, cost
        )
    parts = between_chips(payload)
    lin_out, final_states = delta_rule(
        after(states, payload), lin_query, lin_key, lin_value, lin_decay, lin_beta, lin_gate
    )
    low, high = combine(info, parts, att_query, after(new_kv, lin_out))
    low_here = lax.ppermute(low, "head", [(2, 0), (3, 2)])
    high_here = lax.ppermute(high, "head", [(2, 1)])
    result = jnp.where(
        head_index == 3, high, jnp.where(head_index == 1, high_here, low_here)
    )
    att_out = (result * jax.nn.sigmoid(att_gate.astype(jnp.float32))).astype(jnp.bfloat16)

    return (att_out, lin_out, final_states)


def solution(mesh):
    placed = (
        P(None, "wide", "head"),
        P(None, "head", "wide", None),
        P(),
        P(),
        P("wide", None, None, None),
        P("wide", None, None),
        P("wide", None, "head"),
        P("wide", None, "head", None),
        P("wide", None, "head", None),
        P("wide", None, "head", None),
        P("wide", None, "head"),
        P("wide", None, "head"),
        P("wide", None, "head", None),
    )
    return jax.shard_map(
        on_device,
        mesh=mesh,
        in_specs=placed,
        out_specs=(
            P("wide", None, "head"),
            P("wide", None, "head", None),
            P("wide", "head", None, None),
        ),
        check_vma=False,
    )
```

time: 108 us -> 86.2 us (0.80)
  Pallas kernels: 38.7 us -> 26.6 us
  waiting for transfers between devices: 12.5 us -> 22.8 us
  matrix products: 6.67 us -> 0 us
  local copies, waits for them, and re-layouts: 10.2 us -> 4.44 us
  starting transfers between devices: 34.7 us -> 29.8 us
  other arithmetic: 3.29 us -> 0.8 us
    all_to_all x2 -> x3, waiting for transfers between devices: 2.51 us -> 16.2 us  [the longest x2 8.2 us: between_chips(): lax.all_to_all(array, 'wide', 0, 0, tiled=True, axis_index_groups=same_core)]
    ppermute x8 -> x4, starting transfers between devices: 12.2 us -> 1.15 us  [across(): return lax.ppermute(array, 'wide', pairs)]
    unnamed x50 -> x27, local copies, waits for them, and re-layouts: 7.66 us -> 0.69 us
    pallas_call x6 -> x9, Pallas kernels: 21.2 us -> 14.5 us  [the longest x2 6.48 us: gather_rows(): pl.pallas_call(functools.partial(gather_kernel, first=first), name='gathe...]
    dot_general x6 -> x0, matrix products: 6.67 us -> none  [the longest x3 3.56 us: delta_rule(): jnp.einsum('rhk,rhkv->rhv', queries[:, step], states, precision=lax.Preci...]
    all_to_all x2 -> x3, starting transfers between devices: 12.9 us -> 19.4 us  [the longest x2 11.9 us: between_chips(): lax.all_to_all(array, 'wide', 0, 0, tiled=True, axis_index_groups=same_core)]
    pallas_call x4, Pallas kernels: 15.8 us -> 11.5 us  [score_rows(): pl.pallas_call(functools.partial(score_kernel, chunk=chunk), name='score_...]
    ppermute x1, waiting for transfers between devices: 8.25 us -> 6.38 us  [on_device(): low_here = lax.ppermute(low, 'head', [(2, 0), (3, 2)])]
  transfers between devices with their start and end apart: 16 -> 13, of which waited for: 5 -> 4; matrix products, arithmetic and copies ran while one was open for 12% -> 3% of each run, Pallas kernels for 29% -> 30%
where the time goes in v2:
time: 86.2 us; the launch traced here: 85.5 us
  starting transfers between devices  29.8 us (35%)
  Pallas kernels  26.6 us (31%)
  waiting for transfers between devices  22.8 us (26%)
  local copies, waits for them, and re-layouts  4.44 us (5%)
  between operations  1.09 us (1%)
    all_to_all x2, starting transfers between devices, between_chips(): lax.all_to_all(array, 'wide', 0, 0, tiled=True, axis_index_groups=same_core)  11.9 us
    pallas_call x4, Pallas kernels, score_rows(): pl.pallas_call(functools.partial(score_kernel, chunk=chunk), name='score_...  11.5 us
    all_to_all x2, waiting for transfers between devices, between_chips(): lax.all_to_all(array, 'wide', 0, 0, tiled=True, axis_index_groups=same_core)  8.2 us
    all_to_all x1, waiting for transfers between devices, on_device(): lax.all_to_all(after(taken, weights[-1]), 'wide', split_axis=0, concat_ax...  8.01 us
    all_to_all x1, starting transfers between devices, on_device(): lax.all_to_all(after(taken, weights[-1]), 'wide', split_axis=0, concat_ax...  7.51 us
    ppermute x4, starting transfers between devices, on_device(): moved = [lax.ppermute(made, 'head', [(0, 2), (1, 3)]) for made in weights]  7.29 us
    pallas_call x2, Pallas kernels, gather_rows(): pl.pallas_call(functools.partial(gather_kernel, first=first), name='gathe...  6.48 us
    ppermute x1, waiting for transfers between devices, on_device(): low_here = lax.ppermute(low, 'head', [(2, 0), (3, 2)])  6.38 us
  transfers between devices with their start and end apart: 13, of which 4 were waited for; matrix products, arithmetic and copies ran while one was open for 3% of the time, Pallas kernels for 30%

profile of v2, /device:TPU:0, one launch (start us, length us, event | category | flops | bytes accessed | tf_op | source)
XLA Modules:
  0.0 85.5 jit_solution(10704543757126068477)
XLA Ops:
  0.6 0.0 copy-start
  0.6 0.0 copy-start.11
  0.7 0.8 dynamic-slice_bitcast_fusion
  1.5 0.8 broadcast_in_dim.11
  2.3 8.1 %all-to-all-start = ((bf16[32,24,256]{2,1,0:T(8,128)(2,1)}), bf16[32,24,256]{2,1,0:T(8,128)(2,1)S(1)}, u32[]{:S(2)}, u32[]{:S(2)}) async-start(bf16[32,24,256]{2,1,0:T(8,128)(2,1)} %bitcast.3), calls=%async_computation | async-start | bytes 786432 | tf_op jit(solution)/shard_map/all_to_all | solution.py:472
  10.4 0.8 pad_add_fusion.info
  11.2 2.6 %gather_rows.2 = bf16[8,256,256]{2,1,0:T(8,128)(2,1)} custom-call(s32[130]{0:T(256)S(1)} %pad_add_fusion.info, bf16[64,256,256]{2,1,0:T(8,128)(2,1)} %refs_0_.11), custom_call_target="tpu_custom_call" | custom-call | tf_op jit(solution)/shard_map/gather_rows/pallas_call | solution.py:70
  13.8 0.1 collective-permute-start
  13.9 1.9 %gather_fusion = bf16[64,8,4,128]{3,2,1,0:T(4,128)(2,1)} fusion(f32[64,8,4,128]{3,2,1,0:T(4,128)S(1)} %copy-done, s32[1024]{0:T(1024)S(1)} %pad_clamp_fusion), kind=kCustom, calls=%fused_computation | custom fusion | bytes 1048832 | tf_op jit(solution)/shard_map/gather | solution.py:478
  15.9 3.8 %gather_rows.3 = (bf16[8,256,256]{2,1,0:T(8,128)(2,1)}, bf16[8,256,256]{2,1,0:T(8,128)(2,1)}, bf16[8,256,256]{2,1,0:T(8,128)(2,1)}) custom-call(s32[130]{0:T(256)S(1)} %pad_add_fusion.info, bf16[64,256,256]{2,1,0:T(8,128)(2,1)} %refs_0_.11), custom_call_target="tpu_custom_call" | custom-call | tf_op jit(solution)/shard_map/gather_rows/pallas_call | solution.py:70
  19.7 0.6 collective-permute-start.1
  20.3 0.1 collective-permute-start.2
  20.4 0.4 collective-permute-start.3
  20.8 1.9 %load_rows.1.own = bf16[8,256,256]{2,1,0:T(8,128)(2,1)S(1)} custom-call(s32[130]{0:T(256)S(1)} %pad_add_fusion.info, bf16[64,256,256]{2,1,0:T(8,128)(2,1)} %refs_0_.11), custom_call_target="tpu_custom_call" | custom-call | tf_op jit(solution)/shard_map/load_rows/pallas_call | solution.py:131
  22.7 0.2 collective-permute-done.1.refs_1_
  22.9 3.6 %score_rows.4 = (bf16[24,4224]{1,0:T(8,128)(2,1)}, bf16[8,256,256]{2,1,0:T(8,128)(2,1)S(1)}, bf16[8,256,256]{2,1,0:T(8,128)(2,1)S(1)}) custom-call(s32[130]{0:T(256)S(1)} %pad_add_fusion.info, bf16[32,24,256]{2,1,0:T(8,128)(2,1)S(1)} %hold.1.query, bf16[8,256,256]{2,1,0:T(8,128)(2,1)S(1)} %load_rows.1.own, ...), custom_call_target="tpu_custom_call" | custom-call | tf_op jit(solution)/shard_map/score_rows/pallas_call | solution.py:191
  26.5 3.4 %collective-permute-start.7 = (bf16[24,4224]{1,0:T(8,128)(2,1)}, bf16[24,4224]{1,0:T(8,128)(2,1)}, u32[]{:S(2)}, u32[]{:S(2)}) collective-permute-start(bf16[24,4224]{1,0:T(8,128)(2,1)} %get-tuple-element.40), channel_id=1, source_target_pairs={{0,64},{32,96},{1,65},{33,97},{2,66},{34,98},{3,67},{35,99},{4,68}... | collective-permute-start | bytes 608264 | tf_op jit(solution)/shard_map/ppermute | solution.py:492
  29.9 3.6 %score_rows.5 = (bf16[24,4224]{1,0:T(8,128)(2,1)}, bf16[8,256,256]{2,1,0:T(8,128)(2,1)S(1)}, bf16[8,256,256]{2,1,0:T(8,128)(2,1)S(1)}) custom-call(s32[130]{0:T(256)S(1)} %pad_add_fusion.info, bf16[32,24,256]{2,1,0:T(8,128)(2,1)S(1)} %hold.1.query, bf16[8,256,256]{2,1,0:T(8,128)(2,1)S(1)} %get-tuple-element.32.own, ...), custom_call_target="tpu_custom_call" | custom-call | tf_op jit(solution)/shard_map/score_rows/pallas_call | solution.py:191
  33.5 1.3 %collective-permute-start.6 = (bf16[24,4224]{1,0:T(8,128)(2,1)}, bf16[24,4224]{1,0:T(8,128)(2,1)S(1)}, u32[]{:S(2)}, u32[]{:S(2)}) collective-permute-start(bf16[24,4224]{1,0:T(8,128)(2,1)} %get-tuple-element.39), channel_id=1, source_target_pairs={{0,64},{32,96},{1,65},{33,97},{2,66},{34,98},{3,67},{35,99},{4,68}... | collective-permute-start | bytes 608264 | tf_op jit(solution)/shard_map/ppermute | solution.py:492
  34.8 0.0 collective-permute-done.3.refs_1_.refs_2_
  34.8 2.9 %score_rows.6 = (bf16[24,4224]{1,0:T(8,128)(2,1)S(1)}, bf16[8,256,256]{2,1,0:T(8,128)(2,1)S(1)}, bf16[8,256,256]{2,1,0:T(8,128)(2,1)S(1)}) custom-call(s32[130]{0:T(256)S(1)} %pad_add_fusion.info, bf16[32,24,256]{2,1,0:T(8,128)(2,1)S(1)} %hold.1.query, bf16[8,256,256]{2,1,0:T(8,128)(2,1)S(1)} %get-tuple-element.34.own, ...), custom_call_target="tpu_custom_call" | custom-call | tf_op jit(solution)/shard_map/score_rows/pallas_call | solution.py:191
  37.7 1.3 %collective-permute-start.5 = (bf16[24,4224]{1,0:T(8,128)(2,1)S(1)}, bf16[24,4224]{1,0:T(8,128)(2,1)S(1)}, u32[]{:S(2)}, u32[]{:S(2)}) collective-permute-start(bf16[24,4224]{1,0:T(8,128)(2,1)S(1)} %get-tuple-element.38), channel_id=1, source_target_pairs={{0,64},{32,96},{1,65},{33,97},{2,66},{34,98},{3,67},{35,99},{4,68}... | collective-permute-start | bytes 608264 | tf_op jit(solution)/shard_map/ppermute | solution.py:492
  39.0 1.4 %score_rows.7 = bf16[24,4224]{1,0:T(8,128)(2,1)S(1)} custom-call(s32[130]{0:T(256)S(1)} %pad_add_fusion.info, bf16[32,24,256]{2,1,0:T(8,128)(2,1)S(1)} %hold.1.query, bf16[8,256,256]{2,1,0:T(8,128)(2,1)S(1)} %get-tuple-element.36.own, bf16[8,256,256]{2,1,0:T(8,128)(2,1)S(1)} %get-tuple-element.37.other), custom_call_target="tpu_custom_call" | custom-call | tf_op jit(solution)/shard_map/score_rows/pallas_call | solution.py:191
  40.5 1.3 %collective-permute-start.4 = (bf16[24,4224]{1,0:T(8,128)(2,1)S(1)}, bf16[24,4224]{1,0:T(8,128)(2,1)S(1)}, u32[]{:S(2)}, u32[]{:S(2)}) collective-permute-start(bf16[24,4224]{1,0:T(8,128)(2,1)S(1)} %score_rows.7), channel_id=1, source_target_pairs={{0,64},{32,96},{1,65},{33,97},{2,66},{34,98},{3,67},{35,99},{4,68}... | collective-permute-start | bytes 608264 | tf_op jit(solution)/shard_map/ppermute | solution.py:492
  41.8 7.5 %all-to-all-start.2 = ((bf16[64,8,4,128]{3,2,1,0:T(4,128)(2,1)}), bf16[64,8,4,128]{3,2,1,0:T(4,128)(2,1)S(1)}, u32[]{:S(2)}, u32[]{:S(2)}) async-start(bf16[64,8,4,128]{3,2,1,0:T(4,128)(2,1)} %gather_fusion), calls=%async_computation.2 | async-start | bytes 1048576 | tf_op jit(solution)/shard_map/all_to_all | solution.py:494
  49.3 1.0 %mix_rows.4.refs_2_ = bf16[16,112,128]{2,1,0:T(8,128)(2,1)} custom-call(s32[130]{0:T(256)S(1)} %pad_add_fusion.info, bf16[24,4224]{1,0:T(8,128)(2,1)} %collective-permute-done.7.weights, bf16[64,256,256]{2,1,0:T(8,128)(2,1)} %refs_0_.11, bf16[8,256,256]{2,1,0:T(8,128)(2,1)} %copy-done.1), custom_call_target="tpu_custom_call" | custom-call | flops 100000000 | tf_op jit(solution)/shard_map/mix_rows/pallas_call | solution.py:289
  50.3 0.6 mix_rows.5.refs_3_
  51.0 0.7 mix_rows.6
  51.8 0.0 copy-start.9
  51.8 0.0 copy-start.10
  51.8 0.0 copy-start.3
  51.8 0.0 copy-start.4
  51.8 0.0 copy-start.5
  51.8 0.0 copy-start.6
  51.8 0.0 copy-start.7
  51.8 0.0 copy-start.2
  51.9 0.0 copy-start.8
  51.9 0.6 mix_rows.7
  52.4 8.0 %all-to-all-done.2 = bf16[64,8,4,128]{3,2,1,0:T(4,128)(2,1)S(1)} async-done(((bf16[64,8,4,128]{3,2,1,0:T(4,128)(2,1)}), bf16[64,8,4,128]{3,2,1,0:T(4,128)(2,1)S(1)}, u32[]{:S(2)}, u32[]{:S(2)}) %all-to-all-start.2) | async-done | bytes 524320 | tf_op jit(solution)/shard_map/all_to_all | solution.py:494
  60.5 3.8 %all-to-all-start.1 = ((bf16[16,112,128]{2,1,0:T(8,128)(2,1)}), bf16[16,112,128]{2,1,0:T(8,128)(2,1)S(1)}, u32[]{:S(2)}, u32[]{:S(2)}) async-start(bf16[16,112,128]{2,1,0:T(8,128)(2,1)} %mix_rows.7), calls=%async_computation.1 | async-start | bytes 917504 | tf_op jit(solution)/shard_map/all_to_all | solution.py:472
  64.3 0.2 copy.20
  64.6 3.2 %delta_rule.1 = (bf16[2,3,8,128]{3,2,1,0:T(8,128)(2,1)}, f32[2,8,128,128]{3,2,1,0:T(8,128)}) custom-call(f32[2,3,8]{2,1,0:T(4,128)S(1)} %copy.21.decay, f32[2,3,8]{2,1,0:T(4,128)S(1)} %copy.22.beta, bf16[2,8,128,128]{3,2,1,0:T(8,128)(2,1)S(1)} %bitcast.9, bf16[2,3,4,128]{3,2,1,0:T(4,128)(2,1)S(1)} %copy-done.5, bf16[2,3,4,128]{3,2,1,0:T(4,128)(2,1)S(1)} %copy-done.6, ...), custom_call_target="tpu_custom_call" | custom-call | tf_op jit(solution)/shard_map/delta_rule/pallas_call | solution.py:426
  67.7 8.2 %all-to-all-done.1.parts = bf16[16,112,128]{2,1,0:T(8,128)(2,1)S(1)} async-done(((bf16[16,112,128]{2,1,0:T(8,128)(2,1)}), bf16[16,112,128]{2,1,0:T(8,128)(2,1)S(1)}, u32[]{:S(2)}, u32[]{:S(2)}) %all-to-all-start.1) | async-done | bytes 458784 | tf_op jit(solution)/shard_map/all_to_all | solution.py:472
  75.9 0.6 combine_parts.1
  76.5 0.7 collective-permute-start.8
  77.2 1.3 %collective-permute-start.9 = (f32[2,3,1024]{2,1,0:T(4,128)S(1)}, f32[2,3,1024]{2,1,0:T(4,128)S(1)}, u32[]{:S(2)}, u32[]{:S(2)}) collective-permute-start(f32[2,3,1024]{2,1,0:T(4,128)S(1)} %get-tuple-element.49), channel_id=1, source_target_pairs={{64,0},{96,64},{65,1},{97,65},{66,2},{98,66},{67,3},{99,67},{68,4}... | collective-permute-start | bytes 73736 | tf_op jit(solution)/shard_map/ppermute | solution.py:509
  78.5 6.4 %collective-permute-done.9 = f32[2,3,1024]{2,1,0:T(4,128)S(1)} collective-permute-done((f32[2,3,1024]{2,1,0:T(4,128)S(1)}, f32[2,3,1024]{2,1,0:T(4,128)S(1)}, u32[]{:S(2)}, u32[]{:S(2)}) %collective-permute-start.9) | collective-permute-done | bytes 24608 | tf_op jit(solution)/shard_map/ppermute | solution.py:509
  84.9 0.6 copy.25
  (28 shorter events, 0.1 us)
Async XLA Ops:
  0.6 13.3 %copy-start = (f32[64,8,4,128]{3,2,1,0:T(4,128)S(1)}, f32[64,8,4,128]{3,2,1,0:T(4,128)}, u32[]{:S(2)}) copy-start(f32[64,8,4,128]{3,2,1,0:T(4,128)} %param.14) | copy-start | bytes 3145732
  0.6 13.3 %copy-start.11 = (s32[64]{0:T(128)S(1)}, s32[64]{0:T(128)}, u32[]{:S(2)}) copy-start(s32[64]{0:T(128)} %param.15) | copy-start | bytes 772
  2.3 20.4 %all-to-all-start = ((bf16[32,24,256]{2,1,0:T(8,128)(2,1)}), bf16[32,24,256]{2,1,0:T(8,128)(2,1)S(1)}, u32[]{:S(2)}, u32[]{:S(2)}) async-start(bf16[32,24,256]{2,1,0:T(8,128)(2,1)} %bitcast.3), calls=%async_computation | async-start | bytes 786432 | tf_op jit(solution)/shard_map/all_to_all | solution.py:472
  13.8 9.1 %collective-permute-start = (bf16[8,256,256]{2,1,0:T(8,128)(2,1)}, bf16[8,256,256]{2,1,0:T(8,128)(2,1)S(1)}, u32[]{:S(2)}, u32[]{:S(2)}) collective-permute-start(bf16[8,256,256]{2,1,0:T(8,128)(2,1)} %gather_rows.2), channel_id=1, source_target_pairs={{0,1},{1,0},{2,3},{3,2},{4,5},{5,4},{6,7},{7,6},{8,9},{9,8},{10,11... | collective-permute-start | bytes 3145736 | tf_op jit(solution)/shard_map/ppermute | solution.py:464
  19.7 3.2 %collective-permute-start.1 = (bf16[8,256,256]{2,1,0:T(8,128)(2,1)}, bf16[8,256,256]{2,1,0:T(8,128)(2,1)}, u32[]{:S(2)}, u32[]{:S(2)}) collective-permute-start(bf16[8,256,256]{2,1,0:T(8,128)(2,1)} %get-tuple-element.28), channel_id=1, source_target_pairs={{0,1},{1,0},{2,3},{3,2},{4,5},{5,4},{6,7},{7,6},{8,9},{9,8},{10,11... | collective-permute-start | bytes 3145736 | tf_op jit(solution)/shard_map/ppermute | solution.py:464
  20.3 9.6 %collective-permute-start.2 = (bf16[8,256,256]{2,1,0:T(8,128)(2,1)}, bf16[8,256,256]{2,1,0:T(8,128)(2,1)}, u32[]{:S(2)}, u32[]{:S(2)}) collective-permute-start(bf16[8,256,256]{2,1,0:T(8,128)(2,1)} %get-tuple-element.29), channel_id=1, source_target_pairs={{0,1},{1,0},{2,3},{3,2},{4,5},{5,4},{6,7},{7,6},{8,9},{9,8},{10,11... | collective-permute-start | bytes 3145736 | tf_op jit(solution)/shard_map/ppermute | solution.py:464
  20.4 14.4 %collective-permute-start.3 = (bf16[8,256,256]{2,1,0:T(8,128)(2,1)}, bf16[8,256,256]{2,1,0:T(8,128)(2,1)}, u32[]{:S(2)}, u32[]{:S(2)}) collective-permute-start(bf16[8,256,256]{2,1,0:T(8,128)(2,1)} %get-tuple-element.30), channel_id=1, source_target_pairs={{0,1},{1,0},{2,3},{3,2},{4,5},{5,4},{6,7},{7,6},{8,9},{9,8},{10,11... | collective-permute-start | bytes 3145736 | tf_op jit(solution)/shard_map/ppermute | solution.py:464
  22.9 10.6 %copy-start.1 = (bf16[8,256,256]{2,1,0:T(8,128)(2,1)}, bf16[8,256,256]{2,1,0:T(8,128)(2,1)S(1)}, u32[]{:S(2)}) copy-start(bf16[8,256,256]{2,1,0:T(8,128)(2,1)S(1)} %collective-permute-done.other.refs_1_) | copy-start | bytes 3145732
  26.5 22.8 %collective-permute-start.7 = (bf16[24,4224]{1,0:T(8,128)(2,1)}, bf16[24,4224]{1,0:T(8,128)(2,1)}, u32[]{:S(2)}, u32[]{:S(2)}) collective-permute-start(bf16[24,4224]{1,0:T(8,128)(2,1)} %get-tuple-element.40), channel_id=1, source_target_pairs={{0,64},{32,96},{1,65},{33,97},{2,66},{34,98},{3,67},{35,99},{4,68}... | collective-permute-start | bytes 608264 | tf_op jit(solution)/shard_map/ppermute | solution.py:492
  33.5 16.9 %collective-permute-start.6 = (bf16[24,4224]{1,0:T(8,128)(2,1)}, bf16[24,4224]{1,0:T(8,128)(2,1)S(1)}, u32[]{:S(2)}, u32[]{:S(2)}) collective-permute-start(bf16[24,4224]{1,0:T(8,128)(2,1)} %get-tuple-element.39), channel_id=1, source_target_pairs={{0,64},{32,96},{1,65},{33,97},{2,66},{34,98},{3,67},{35,99},{4,68}... | collective-permute-start | bytes 608264 | tf_op jit(solution)/shard_map/ppermute | solution.py:492
  37.7 13.3 %collective-permute-start.5 = (bf16[24,4224]{1,0:T(8,128)(2,1)S(1)}, bf16[24,4224]{1,0:T(8,128)(2,1)S(1)}, u32[]{:S(2)}, u32[]{:S(2)}) collective-permute-start(bf16[24,4224]{1,0:T(8,128)(2,1)S(1)} %get-tuple-element.38), channel_id=1, source_target_pairs={{0,64},{32,96},{1,65},{33,97},{2,66},{34,98},{3,67},{35,99},{4,68}... | collective-permute-start | bytes 608264 | tf_op jit(solution)/shard_map/ppermute | solution.py:492
  40.5 11.3 %collective-permute-start.4 = (bf16[24,4224]{1,0:T(8,128)(2,1)S(1)}, bf16[24,4224]{1,0:T(8,128)(2,1)S(1)}, u32[]{:S(2)}, u32[]{:S(2)}) collective-permute-start(bf16[24,4224]{1,0:T(8,128)(2,1)S(1)} %score_rows.7), channel_id=1, source_target_pairs={{0,64},{32,96},{1,65},{33,97},{2,66},{34,98},{3,67},{35,99},{4,68}... | collective-permute-start | bytes 608264 | tf_op jit(solution)/shard_map/ppermute | solution.py:492
  41.8 18.7 %all-to-all-start.2 = ((bf16[64,8,4,128]{3,2,1,0:T(4,128)(2,1)}), bf16[64,8,4,128]{3,2,1,0:T(4,128)(2,1)S(1)}, u32[]{:S(2)}, u32[]{:S(2)}) async-start(bf16[64,8,4,128]{3,2,1,0:T(4,128)(2,1)} %gather_fusion), calls=%async_computation.2 | async-start | bytes 1048576 | tf_op jit(solution)/shard_map/all_to_all | solution.py:494
  51.8 12.5 %copy-start.9 = (f32[2,3,8]{2,0,1:T(2,128)S(1)}, f32[2,3,8]{2,0,1:T(2,128)}, u32[]{:S(2)}) copy-start(f32[2,3,8]{2,0,1:T(2,128)} %param.23) | copy-start | bytes 580
  51.8 12.5 %copy-start.10 = (f32[2,3,8]{2,0,1:T(2,128)S(1)}, f32[2,3,8]{2,0,1:T(2,128)}, u32[]{:S(2)}) copy-start(f32[2,3,8]{2,0,1:T(2,128)} %param.24) | copy-start | bytes 580
  51.8 12.8 %copy-start.3 = (bf16[2,3,8,128]{3,2,1,0:T(8,128)(2,1)S(1)}, bf16[2,3,8,128]{3,2,1,0:T(8,128)(2,1)}, u32[]{:S(2)}) copy-start(bf16[2,3,8,128]{3,2,1,0:T(8,128)(2,1)} %value.1) | copy-start | bytes 36868
  51.8 12.7 %copy-start.4 = (bf16[2,3,8,128]{3,2,1,0:T(8,128)(2,1)S(1)}, bf16[2,3,8,128]{3,2,1,0:T(8,128)(2,1)}, u32[]{:S(2)}) copy-start(bf16[2,3,8,128]{3,2,1,0:T(8,128)(2,1)} %gate.1) | copy-start | bytes 36868
  51.8 12.7 %copy-start.5 = (bf16[2,3,4,128]{3,2,1,0:T(4,128)(2,1)S(1)}, bf16[2,3,4,128]{3,2,1,0:T(4,128)(2,1)}, u32[]{:S(2)}) copy-start(bf16[2,3,4,128]{3,2,1,0:T(4,128)(2,1)} %query.2) | copy-start | bytes 18436
  51.8 12.7 %copy-start.6 = (bf16[2,3,4,128]{3,2,1,0:T(4,128)(2,1)S(1)}, bf16[2,3,4,128]{3,2,1,0:T(4,128)(2,1)}, u32[]{:S(2)}) copy-start(bf16[2,3,4,128]{3,2,1,0:T(4,128)(2,1)} %key.1) | copy-start | bytes 18436
  51.8 15.9 %copy-start.7 = (bf16[2,3,1024]{2,0,1:T(2,128)(2,1)S(1)}, bf16[2,3,1024]{2,0,1:T(2,128)(2,1)}, u32[]{:S(2)}) copy-start(bf16[2,3,1024]{2,0,1:T(2,128)(2,1)} %param.18) | copy-start | bytes 36868
  51.8 24.1 %copy-start.2 = (bf16[2,3,16,256]{3,2,1,0:T(8,128)(2,1)S(1)}, bf16[2,3,16,256]{3,2,1,0:T(8,128)(2,1)}, u32[]{:S(2)}) copy-start(bf16[2,3,16,256]{3,2,1,0:T(8,128)(2,1)} %query.3) | copy-start | bytes 147460
  51.9 33.0 %copy-start.8 = (bf16[2,3,1024]{2,0,1:T(2,128)(2,1)S(1)}, bf16[2,3,1024]{2,0,1:T(2,128)(2,1)}, u32[]{:S(2)}) copy-start(bf16[2,3,1024]{2,0,1:T(2,128)(2,1)} %param.19) | copy-start | bytes 36868
  60.5 15.5 %all-to-all-start.1 = ((bf16[16,112,128]{2,1,0:T(8,128)(2,1)}), bf16[16,112,128]{2,1,0:T(8,128)(2,1)S(1)}, u32[]{:S(2)}, u32[]{:S(2)}) async-start(bf16[16,112,128]{2,1,0:T(8,128)(2,1)} %mix_rows.7), calls=%async_computation.1 | async-start | bytes 917504 | tf_op jit(solution)/shard_map/all_to_all | solution.py:472
  76.5 2.0 %collective-permute-start.8 = (f32[2,3,1024]{2,1,0:T(4,128)S(1)}, f32[2,3,1024]{2,1,0:T(4,128)S(1)}, u32[]{:S(2)}, u32[]{:S(2)}) collective-permute-start(f32[2,3,1024]{2,1,0:T(4,128)S(1)} %get-tuple-element.48), channel_id=1, source_target_pairs={{64,32},{65,33},{66,34},{67,35},{68,36},{69,37},{70,38},{71,39},{7... | collective-permute-start | bytes 73736 | tf_op jit(solution)/shard_map/ppermute | solution.py:510
  77.2 7.7 %collective-permute-start.9 = (f32[2,3,1024]{2,1,0:T(4,128)S(1)}, f32[2,3,1024]{2,1,0:T(4,128)S(1)}, u32[]{:S(2)}, u32[]{:S(2)}) collective-permute-start(f32[2,3,1024]{2,1,0:T(4,128)S(1)} %get-tuple-element.49), channel_id=1, source_target_pairs={{64,0},{96,64},{65,1},{97,65},{66,2},{98,66},{67,3},{99,67},{68,4}... | collective-permute-start | bytes 73736 | tf_op jit(solution)/shard_map/ppermute | solution.py:509

commit v3 on v2

--- a/solution.py
+++ b/solution.py
@@ -16,8 +16,9 @@
 LANES = 128
 NEGATIVE = -1e30
 
-CHUNK = 8
-CHUNKS = 4
+CHUNK = 16
+CHUNKS = 2
+GROUP_ROWS = 4
 NT = (((1,), (1,)), ((), ()))
 LIMIT = 16 * 2**20
 VMEM = pl.BlockSpec(memory_space=pltpu.VMEM)
@@ -97,68 +98,55 @@
 
 
 def fetches(info, cache, swapped, own, other, arrived, chunk):
-    copies = [
-        pltpu.make_async_copy(
-            cache.at[prefill_row(info, chunk * CHUNK + n)], own.at[n], arrived.at[n]
+    groups = []
+    for first in range(0, CHUNK, GROUP_ROWS):
+        copies = [
+            pltpu.make_async_copy(
+                cache.at[prefill_row(info, chunk * CHUNK + n)], own.at[n], arrived.at[n]
+            )
+            for n in range(first, first + GROUP_ROWS)
+        ]
+        span = pl.ds(first, GROUP_ROWS)
+        copies.append(
+            pltpu.make_async_copy(
+                swapped.at[span], other.at[span], arrived.at[CHUNK + first // GROUP_ROWS]
+            )
         )
-        for n in range(CHUNK)
-    ]
-    if swapped is not None:
-        copies.append(pltpu.make_async_copy(swapped, other, arrived.at[CHUNK]))
-    return copies
-
-
-def start(copies):
-    for copy in copies:
-        copy.start()
-
-
-def wait(copies):
-    for copy in copies:
-        copy.wait()
-
-
-ARRIVED = pltpu.SemaphoreType.DMA((CHUNK + 1,))
-
-
-def load_kernel(info, cache, own, arrived, *, chunk):
-    copies = fetches(info, cache, None, own, None, arrived, chunk)
-    start(copies)
-    wait(copies)
-
-
-def load_rows(info, cache, chunk):
-    return pl.pallas_call(
-        functools.partial(load_kernel, chunk=chunk),
-        name="load_rows",
-        out_shape=pltpu.VMEM((CHUNK, *cache.shape[1:]), cache.dtype),
-        in_specs=[SMEM, ANY],
-        out_specs=VMEM,
-        scratch_shapes=[ARRIVED],
-        compiler_params=PARAMS,
-        cost_estimate=FREE,
-    )(info, far(cache))
-
-
-def score_kernel(info, query, own, other, *refs, chunk):
-    if chunk + 1 < CHUNKS:
-        cache, swapped, out, own_next, other_next, arrived = refs
-    else:
-        (out,) = refs
+        groups.append(copies)
+    return groups
+
+
+def start(groups):
+    for copies in groups:
+        for copy in copies:
+            copy.start()
+
+
+def wait(groups):
+    for copies in groups:
+        for copy in copies:
+            copy.wait()
+
+
+ARRIVED = pltpu.SemaphoreType.DMA((CHUNK + CHUNK // GROUP_ROWS,))
+
+
+def score_kernel(info, query, cache, swapped, out, own, other, arrived, *, chunk):
     span = own.shape[1]
     width = 2 * span
 
     @pl.when(info[PLACE] < 2)
     def _():
-        if chunk + 1 < CHUNKS:
-            copies = fetches(info, cache, swapped, own_next, other_next, arrived, chunk + 1)
-            start(copies)
+        groups = fetches(info, cache, swapped, own, other, arrived, chunk)
+        start(groups)
         lane = lax.broadcasted_iota(jnp.int32, (QROWS, LANES), 1)
         column = lax.broadcasted_iota(jnp.int32, (QROWS, span), 1)
         wide = info[PLACE + 1]
         position = jnp.concatenate([column + wide * span, column + (wide ^ 1) * span], axis=1)
         extra = jnp.zeros((QROWS, LANES), jnp.float32)
         for n in range(CHUNK):
+            if n % GROUP_ROWS == 0:
+                wait(groups[n // GROUP_ROWS : n // GROUP_ROWS + 1])
             slot = chunk * CHUNK + n
             q = query[slot]
             scores = jnp.concatenate(
@@ -180,29 +168,24 @@
             extra = jnp.where(lane == n + CHUNK, coarse, extra)
             extra = jnp.where(lane == n + 2 * CHUNK, total - coarse, extra)
         out[:, CHUNK * width :] = extra.astype(out.dtype)
-        if chunk + 1 < CHUNKS:
-            wait(copies)
-
-
-def score_rows(info, query, own, other, cache, swapped, chunk):
-    span, dtype = cache.shape[1], cache.dtype
-    last = chunk + 1 == CHUNKS
-    rows = pltpu.VMEM((CHUNK, span, HD), dtype)
-    made = pl.pallas_call(
+
+
+def held_rows(cache):
+    return pltpu.VMEM((CHUNK, *cache.shape[1:]), cache.dtype)
+
+
+def score_rows(info, query, cache, swapped, chunk):
+    width = CHUNK * 2 * cache.shape[1] + LANES
+    return pl.pallas_call(
         functools.partial(score_kernel, chunk=chunk),
         name="score_rows",
-        out_shape=[pltpu.VMEM((QROWS, CHUNK * 2 * span + LANES), jnp.bfloat16)]
-        + ([] if last else [rows, rows]),
-        in_specs=[SMEM, VMEM, VMEM, VMEM] + ([] if last else [ANY, ANY]),
-        out_specs=[VMEM] if last else [VMEM] * 3,
-        scratch_shapes=[] if last else [ARRIVED],
+        out_shape=pltpu.VMEM((QROWS, width), jnp.bfloat16),
+        in_specs=[SMEM, VMEM, ANY, ANY],
+        out_specs=VMEM,
+        scratch_shapes=[held_rows(cache), held_rows(cache), ARRIVED],
         compiler_params=PARAMS,
         cost_estimate=FREE,
-    )(
-        info, near(query), near(own), near(other),
-        *(() if last else (far(cache), far(swapped))),
-    )
-    return (made[0], None, None) if last else made
+    )(info, near(query), far(cache), far(swapped))
 
 
 LINES = 2 * QROWS
@@ -215,10 +198,11 @@
     fetch_last = chunk + 2 == CHUNKS
     made, left = refs[-2:]
     if last:
-        own, other, _, out = refs[:4]
+        own, other = refs[:2]
+        out = refs[-3]
     elif fetch_last:
-        cache, swapped, swapped_last, _, out, own_last, other_last = refs[:7]
-        own, other, arrived, arrived_last = refs[7:11]
+        cache, swapped, swapped_last = refs[:3]
+        out, own_last, other_last, own, other, arrived, arrived_last = refs[-9:-2]
     else:
         cache, swapped = refs[:2]
         out, own, other, arrived = refs[-6:-2]
@@ -239,9 +223,9 @@
         extra = jnp.concatenate([extra, jnp.zeros((LANES - QROWS, LANES), jnp.float32)], axis=0)
         extra = jnp.transpose(extra)
         blank = jnp.zeros((16 - 6, LANES), jnp.float32)
-        if not last:
-            wait(copies)
         for pair in range(CHUNK // 2):
+            if not last and (2 * pair) % GROUP_ROWS == 0:
+                wait(copies[2 * pair // GROUP_ROWS : 2 * pair // GROUP_ROWS + 1])
             rows, lines = [], []
             for n in (2 * pair, 2 * pair + 1):
                 at = n * width
@@ -270,7 +254,7 @@
 def mix_rows(info, weights, cache, swapped, chunk, before, rows, cost):
     last = chunk + 1 == CHUNKS
     fetch_last = chunk + 2 == CHUNKS
-    held = pltpu.VMEM((CHUNK, *cache.shape[1:]), cache.dtype)
+    held = held_rows(cache)
     payload = pltpu.HBM((CHUNK * CHUNKS // 2, SLAB, LANES), jnp.bfloat16)
     if last:
         in_specs = [SMEM, VMEM, VMEM, VMEM]
@@ -484,11 +468,9 @@
     swapped = [across(part) for part in made]
 
     weights = []
-    own, other = load_rows(after(info, *made), kv_cache, 0), swapped[0]
     for chunk in range(CHUNKS):
-        following = swapped[min(chunk + 1, CHUNKS - 1)]
-        made, own, other = score_rows(info, query, own, other, kv_cache, following, chunk)
-        weights.append(made)
+        held = after(info, *weights)
+        weights.append(score_rows(held, query, kv_cache, swapped[chunk], chunk))
     moved = [lax.ppermute(made, "head", [(0, 2), (1, 3)]) for made in weights]
 
     states = lax.all_to_all(

time: 86.2 us -> 75.1 us (0.87)
  Pallas kernels: 26.6 us -> 20.5 us
  starting transfers between devices: 29.8 us -> 24.6 us
    ppermute x4 -> x2, starting transfers between devices: 7.29 us -> 2.63 us  [on_device(): moved = [lax.ppermute(made, 'head', [(0, 2), (1, 3)]) for made in weights]]
    ppermute x4 -> x2, waiting for transfers between devices: 0.01 us -> 3.27 us  [on_device(): moved = [lax.ppermute(made, 'head', [(0, 2), (1, 3)]) for made in weights]]
    pallas_call x4 -> x2, Pallas kernels: 11.5 us -> 8.87 us  [score_rows(): pl.pallas_call(functools.partial(score_kernel, chunk=chunk), name='score_...]
    pallas_call x1 -> x0, Pallas kernels: 1.92 us -> none  [load_rows(): pl.pallas_call(functools.partial(load_kernel, chunk=chunk), name='load_ro...]
    all_to_all x1, waiting for transfers between devices: 8.01 us -> 6.33 us  [on_device(): lax.all_to_all(after(taken, weights[-1]), 'wide', split_axis=0, concat_ax...]
    pallas_call x4 -> x2, Pallas kernels: 2.99 us -> 1.49 us  [mix_rows(): pl.pallas_call(functools.partial(mix_kernel, chunk=chunk), name='mix_rows...]
    ppermute x1, waiting for transfers between devices: 6.38 us -> 5.34 us  [on_device(): low_here = lax.ppermute(low, 'head', [(2, 0), (3, 2)])]
  transfers between devices with their start and end apart: 13 -> 9, of which waited for: 4 -> 4; matrix products, arithmetic and copies ran while one was open for 3% -> 4% of each run, Pallas kernels for 30% -> 27%
where the time goes in v3:
time: 75.1 us; the launch traced here: 74.5 us
  starting transfers between devices  24.6 us (33%)
  waiting for transfers between devices  23.2 us (31%)
  Pallas kernels  20.5 us (27%)
  local copies, waits for them, and re-layouts  4.46 us (6%)
  between operations  0.96 us (1%)
  other arithmetic  0.8 us (1%)
    all_to_all x2, starting transfers between devices, between_chips(): lax.all_to_all(array, 'wide', 0, 0, tiled=True, axis_index_groups=same_core)  11.9 us
    pallas_call x2, Pallas kernels, score_rows(): pl.pallas_call(functools.partial(score_kernel, chunk=chunk), name='score_...  8.87 us
    all_to_all x2, waiting for transfers between devices, between_chips(): lax.all_to_all(array, 'wide', 0, 0, tiled=True, axis_index_groups=same_core)  8.23 us
    all_to_all x1, starting transfers between devices, on_device(): lax.all_to_all(after(taken, weights[-1]), 'wide', split_axis=0, concat_ax...  7.48 us
    pallas_call x2, Pallas kernels, gather_rows(): pl.pallas_call(functools.partial(gather_kernel, first=first), name='gathe...  6.42 us
    all_to_all x1, waiting for transfers between devices, on_device(): lax.all_to_all(after(taken, weights[-1]), 'wide', split_axis=0, concat_ax...  6.33 us
    ppermute x1, waiting for transfers between devices, on_device(): low_here = lax.ppermute(low, 'head', [(2, 0), (3, 2)])  5.34 us
    ppermute x2, waiting for transfers between devices, on_device(): moved = [lax.ppermute(made, 'head', [(0, 2), (1, 3)]) for made in weights]  3.27 us
  transfers between devices with their start and end apart: 9, of which 4 were waited for; matrix products, arithmetic and copies ran while one was open for 4% of the time, Pallas kernels for 27%

profile of v3, /device:TPU:0, one launch (start us, length us, event | category | flops | bytes accessed | tf_op | source)
XLA Modules:
  0.0 74.5 jit_solution(10368652159626045194)
XLA Ops:
  0.6 0.0 copy-start
  0.7 0.8 %dynamic-slice_bitcast_fusion = bf16[2,24,256]{2,1,0:T(8,128)(2,1)S(1)} fusion(bf16[2,3,16,256]{3,2,1,0:T(8,128)(2,1)} %query.3, s32[]{:T(128)S(6)} %select_n.31), kind=kLoop, calls=%fused_computation.3 | loop fusion | bytes 49156 | tf_op jit(solution)/shard_map/broadcast_in_dim | solution.py:459
  1.5 0.8 %broadcast_in_dim.11 = bf16[16,2,24,256]{3,2,1,0:T(8,128)(2,1)} broadcast(bf16[2,24,256]{2,1,0:T(8,128)(2,1)S(1)} %dynamic-slice_bitcast_fusion), dimensions={1,2,3} | broadcast | bytes 417792 | tf_op jit(solution)/shard_map/broadcast_in_dim | solution.py:459
  2.3 8.1 %all-to-all-start = ((bf16[32,24,256]{2,1,0:T(8,128)(2,1)}), bf16[32,24,256]{2,1,0:T(8,128)(2,1)S(1)}, u32[]{:S(2)}, u32[]{:S(2)}) async-start(bf16[32,24,256]{2,1,0:T(8,128)(2,1)} %bitcast.3), calls=%async_computation | async-start | bytes 786432 | tf_op jit(solution)/shard_map/all_to_all | solution.py:456
  10.5 0.8 %pad_add_fusion.info = s32[130]{0:T(256)S(1)} fusion(s32[1]{0:T(128)} %bitcast.1, s32[1]{0:T(128)} %bitcast, s32[64]{0:T(128)} %param.16, s32[64]{0:T(128)} %param.15), kind=kLoop, calls=%fused_computation.6 | loop fusion | flops 390 | bytes 1040 | tf_op jit(solution)/shard_map/concatenate | solution.py:444
  11.2 3.2 %gather_rows.2 = bf16[16,256,256]{2,1,0:T(8,128)(2,1)} custom-call(s32[130]{0:T(256)S(1)} %pad_add_fusion.info, bf16[64,256,256]{2,1,0:T(8,128)(2,1)} %refs_0_.1), custom_call_target="tpu_custom_call" | custom-call | tf_op jit(solution)/shard_map/gather_rows/pallas_call | solution.py:71
  14.4 0.1 collective-permute-start
  14.5 0.0 copy-done.10
  14.5 0.0 copy-done
  14.5 1.9 %gather_fusion = bf16[64,8,4,128]{3,2,1,0:T(4,128)(2,1)} fusion(f32[64,8,4,128]{3,2,1,0:T(4,128)S(1)} %copy-done, s32[1024]{0:T(1024)S(1)} %pad_clamp_fusion), kind=kCustom, calls=%fused_computation | custom fusion | bytes 1048832 | tf_op jit(solution)/shard_map/gather | solution.py:462
  16.4 3.2 %gather_rows.3 = bf16[16,256,256]{2,1,0:T(8,128)(2,1)} custom-call(s32[130]{0:T(256)S(1)} %pad_add_fusion.info, bf16[64,256,256]{2,1,0:T(8,128)(2,1)} %refs_0_.1), custom_call_target="tpu_custom_call" | custom-call | tf_op jit(solution)/shard_map/gather_rows/pallas_call | solution.py:71
  19.7 0.6 collective-permute-start.1
  20.2 0.0 all-to-all-done.array
  20.3 0.0 collective-permute-done.swapped.refs_1_
  20.3 4.4 %score_rows.2 = bf16[24,8320]{1,0:T(8,128)(2,1)S(1)} custom-call(s32[130]{0:T(256)S(1)} %pad_add_fusion.info, bf16[32,24,256]{2,1,0:T(8,128)(2,1)S(1)} %hold.1.query, bf16[64,256,256]{2,1,0:T(8,128)(2,1)} %refs_0_.1, bf16[16,256,256]{2,1,0:T(8,128)(2,1)} %collective-permute-done.swapped.refs_1_), custom_call_target="tpu_custom_call" | custom-call | tf_op jit(solution)/shard_map/score_rows/pallas_call | solution.py:179
  24.7 1.3 %collective-permute-start.3 = (bf16[24,8320]{1,0:T(8,128)(2,1)S(1)}, bf16[24,8320]{1,0:T(8,128)(2,1)S(1)}, u32[]{:S(2)}, u32[]{:S(2)}) collective-permute-start(bf16[24,8320]{1,0:T(8,128)(2,1)S(1)} %score_rows.2), channel_id=1, source_target_pairs={{0,64},{32,96},{1,65},{33,97},{2,66},{34,98},{3,67},{35,99},{4,68}... | collective-permute-start | bytes 1198088 | tf_op jit(solution)/shard_map/ppermute | solution.py:474
  26.0 0.0 collective-permute-done.1.swapped.refs_2_
  26.0 4.4 %score_rows.3 = bf16[24,8320]{1,0:T(8,128)(2,1)S(1)} custom-call(s32[130]{0:T(256)S(1)} %pad_add_fusion.info, bf16[32,24,256]{2,1,0:T(8,128)(2,1)S(1)} %hold.1.query, bf16[64,256,256]{2,1,0:T(8,128)(2,1)} %refs_0_.1, bf16[16,256,256]{2,1,0:T(8,128)(2,1)} %collective-permute-done.1.swapped.refs_2_), custom_call_target="tpu_custom_call" | custom-call | tf_op jit(solution)/shard_map/score_rows/pallas_call | solution.py:179
  30.5 1.3 %collective-permute-start.2 = (bf16[24,8320]{1,0:T(8,128)(2,1)S(1)}, bf16[24,8320]{1,0:T(8,128)(2,1)S(1)}, u32[]{:S(2)}, u32[]{:S(2)}) collective-permute-start(bf16[24,8320]{1,0:T(8,128)(2,1)S(1)} %score_rows.3), channel_id=1, source_target_pairs={{0,64},{32,96},{1,65},{33,97},{2,66},{34,98},{3,67},{35,99},{4,68}... | collective-permute-start | bytes 1198088 | tf_op jit(solution)/shard_map/ppermute | solution.py:474
  31.8 7.5 %all-to-all-start.2 = ((bf16[64,8,4,128]{3,2,1,0:T(4,128)(2,1)}), bf16[64,8,4,128]{3,2,1,0:T(4,128)(2,1)S(1)}, u32[]{:S(2)}, u32[]{:S(2)}) async-start(bf16[64,8,4,128]{3,2,1,0:T(4,128)(2,1)} %gather_fusion), calls=%async_computation.2 | async-start | bytes 1048576 | tf_op jit(solution)/shard_map/all_to_all | solution.py:476
  39.3 0.0 collective-permute-done.3.weights
  39.3 0.9 %mix_rows.2 = (bf16[16,112,128]{2,1,0:T(8,128)(2,1)}, bf16[16,256,256]{2,1,0:T(8,128)(2,1)S(1)}, bf16[16,256,256]{2,1,0:T(8,128)(2,1)S(1)}) custom-call(s32[130]{0:T(256)S(1)} %pad_add_fusion.info, bf16[24,8320]{1,0:T(8,128)(2,1)S(1)} %collective-permute-done.3.weights, bf16[64,256,256]{2,1,0:T(8,128)(2,1)} %refs_0_.1, ...), custom_call_target="tpu_custom_call" | custom-call | flops 100000000 | tf_op jit(solution)/shard_map/mix_rows/pallas_call | solution.py:273
  40.2 3.3 %collective-permute-done.2.weights = bf16[24,8320]{1,0:T(8,128)(2,1)S(1)} collective-permute-done((bf16[24,8320]{1,0:T(8,128)(2,1)S(1)}, bf16[24,8320]{1,0:T(8,128)(2,1)S(1)}, u32[]{:S(2)}, u32[]{:S(2)}) %collective-permute-start.2) | collective-permute-done | bytes 399392 | tf_op jit(solution)/shard_map/ppermute | solution.py:474
  43.5 0.0 copy-start.5
  43.5 0.6 mix_rows.3
  44.1 0.0 copy-start.6
  44.1 0.0 copy-start.1
  44.1 0.0 copy-start.7
  44.2 6.3 %all-to-all-done.2 = bf16[64,8,4,128]{3,2,1,0:T(4,128)(2,1)S(1)} async-done(((bf16[64,8,4,128]{3,2,1,0:T(4,128)(2,1)}), bf16[64,8,4,128]{3,2,1,0:T(4,128)(2,1)S(1)}, u32[]{:S(2)}, u32[]{:S(2)}) %all-to-all-start.2) | async-done | bytes 524320 | tf_op jit(solution)/shard_map/all_to_all | solution.py:476
  50.5 3.8 %all-to-all-start.1 = ((bf16[16,112,128]{2,1,0:T(8,128)(2,1)}), bf16[16,112,128]{2,1,0:T(8,128)(2,1)S(1)}, u32[]{:S(2)}, u32[]{:S(2)}) async-start(bf16[16,112,128]{2,1,0:T(8,128)(2,1)} %mix_rows.3), calls=%async_computation.1 | async-start | bytes 917504 | tf_op jit(solution)/shard_map/all_to_all | solution.py:456
  54.3 0.0 copy-done.8
  54.3 0.0 copy-done.9
  54.3 0.2 copy.18
  54.6 0.0 copy-done.2
  54.6 0.0 copy-done.3
  54.6 0.0 copy-done.4
  54.6 0.0 copy-done.5
  54.6 3.2 %delta_rule.1 = (bf16[2,3,8,128]{3,2,1,0:T(8,128)(2,1)}, f32[2,8,128,128]{3,2,1,0:T(8,128)}) custom-call(f32[2,3,8]{2,1,0:T(4,128)S(1)} %copy.19.decay, f32[2,3,8]{2,1,0:T(4,128)S(1)} %copy.20.beta, bf16[2,8,128,128]{3,2,1,0:T(8,128)(2,1)S(1)} %bitcast.9, bf16[2,3,4,128]{3,2,1,0:T(4,128)(2,1)S(1)} %copy-done.4, bf16[2,3,4,128]{3,2,1,0:T(4,128)(2,1)S(1)} %copy-done.5, ...), custom_call_target="tpu_custom_call" | custom-call | tf_op jit(solution)/shard_map/delta_rule/pallas_call | solution.py:410
  57.7 0.0 copy-done.6
  57.8 8.2 %all-to-all-done.1.parts = bf16[16,112,128]{2,1,0:T(8,128)(2,1)S(1)} async-done(((bf16[16,112,128]{2,1,0:T(8,128)(2,1)}), bf16[16,112,128]{2,1,0:T(8,128)(2,1)S(1)}, u32[]{:S(2)}, u32[]{:S(2)}) %all-to-all-start.1) | async-done | bytes 458784 | tf_op jit(solution)/shard_map/all_to_all | solution.py:456
  66.0 0.0 copy-done.1
  66.0 0.6 combine_parts.1
  66.5 1.3 %collective-permute-start.5 = (f32[2,3,1024]{2,1,0:T(4,128)S(1)}, f32[2,3,1024]{2,1,0:T(4,128)S(1)}, u32[]{:S(2)}, u32[]{:S(2)}) collective-permute-start(f32[2,3,1024]{2,1,0:T(4,128)S(1)} %get-tuple-element.25), channel_id=1, source_target_pairs={{64,0},{96,64},{65,1},{97,65},{66,2},{98,66},{67,3},{99,67},{68,4}... | collective-permute-start | bytes 73736 | tf_op jit(solution)/shard_map/ppermute | solution.py:491
  67.8 0.7 collective-permute-start.4
  68.5 5.3 %collective-permute-done.5 = f32[2,3,1024]{2,1,0:T(4,128)S(1)} collective-permute-done((f32[2,3,1024]{2,1,0:T(4,128)S(1)}, f32[2,3,1024]{2,1,0:T(4,128)S(1)}, u32[]{:S(2)}, u32[]{:S(2)}) %collective-permute-start.5) | collective-permute-done | bytes 24608 | tf_op jit(solution)/shard_map/ppermute | solution.py:491
  73.8 0.0 collective-permute-done.4
  73.8 0.0 copy-done.7
  73.9 0.6 copy.23
  (13 shorter events, 0.1 us)
Async XLA Ops:
  0.6 13.9 %copy-start = (f32[64,8,4,128]{3,2,1,0:T(4,128)S(1)}, f32[64,8,4,128]{3,2,1,0:T(4,128)}, u32[]{:S(2)}) copy-start(f32[64,8,4,128]{3,2,1,0:T(4,128)} %param.14) | copy-start | bytes 3145732
  2.3 18.0 %all-to-all-start = ((bf16[32,24,256]{2,1,0:T(8,128)(2,1)}), bf16[32,24,256]{2,1,0:T(8,128)(2,1)S(1)}, u32[]{:S(2)}, u32[]{:S(2)}) async-start(bf16[32,24,256]{2,1,0:T(8,128)(2,1)} %bitcast.3), calls=%async_computation | async-start | bytes 786432 | tf_op jit(solution)/shard_map/all_to_all | solution.py:456
  11.2 3.3 %copy-start.10 = (s32[64]{0:T(128)S(1)}, s32[64]{0:T(128)}, u32[]{:S(2)}) copy-start(s32[64]{0:T(128)} %param.15) | copy-start | bytes 772
  14.4 5.9 %collective-permute-start = (bf16[16,256,256]{2,1,0:T(8,128)(2,1)}, bf16[16,256,256]{2,1,0:T(8,128)(2,1)}, u32[]{:S(2)}, u32[]{:S(2)}) collective-permute-start(bf16[16,256,256]{2,1,0:T(8,128)(2,1)} %gather_rows.2), channel_id=1, source_target_pairs={{0,1},{1,0},{2,3},{3,2},{4,5},{5,4},{6,7},{7,6},{8,9},{9,8},{10,11... | collective-permute-start | bytes 6291464 | tf_op jit(solution)/shard_map/ppermute | solution.py:448
  19.7 6.4 %collective-permute-start.1 = (bf16[16,256,256]{2,1,0:T(8,128)(2,1)}, bf16[16,256,256]{2,1,0:T(8,128)(2,1)}, u32[]{:S(2)}, u32[]{:S(2)}) collective-permute-start(bf16[16,256,256]{2,1,0:T(8,128)(2,1)} %gather_rows.3), channel_id=1, source_target_pairs={{0,1},{1,0},{2,3},{3,2},{4,5},{5,4},{6,7},{7,6},{8,9},{9,8},{10,11... | collective-permute-start | bytes 6291464 | tf_op jit(solution)/shard_map/ppermute | solution.py:448
  24.7 14.6 %collective-permute-start.3 = (bf16[24,8320]{1,0:T(8,128)(2,1)S(1)}, bf16[24,8320]{1,0:T(8,128)(2,1)S(1)}, u32[]{:S(2)}, u32[]{:S(2)}) collective-permute-start(bf16[24,8320]{1,0:T(8,128)(2,1)S(1)} %score_rows.2), channel_id=1, source_target_pairs={{0,64},{32,96},{1,65},{33,97},{2,66},{34,98},{3,67},{35,99},{4,68}... | collective-permute-start | bytes 1198088 | tf_op jit(solution)/shard_map/ppermute | solution.py:474
  30.5 13.0 %collective-permute-start.2 = (bf16[24,8320]{1,0:T(8,128)(2,1)S(1)}, bf16[24,8320]{1,0:T(8,128)(2,1)S(1)}, u32[]{:S(2)}, u32[]{:S(2)}) collective-permute-start(bf16[24,8320]{1,0:T(8,128)(2,1)S(1)} %score_rows.3), channel_id=1, source_target_pairs={{0,64},{32,96},{1,65},{33,97},{2,66},{34,98},{3,67},{35,99},{4,68}... | collective-permute-start | bytes 1198088 | tf_op jit(solution)/shard_map/ppermute | solution.py:474
  31.8 18.7 %all-to-all-start.2 = ((bf16[64,8,4,128]{3,2,1,0:T(4,128)(2,1)}), bf16[64,8,4,128]{3,2,1,0:T(4,128)(2,1)S(1)}, u32[]{:S(2)}, u32[]{:S(2)}) async-start(bf16[64,8,4,128]{3,2,1,0:T(4,128)(2,1)} %gather_fusion), calls=%async_computation.2 | async-start | bytes 1048576 | tf_op jit(solution)/shard_map/all_to_all | solution.py:476
  43.5 10.8 %copy-start.8 = (f32[2,3,8]{2,0,1:T(2,128)S(1)}, f32[2,3,8]{2,0,1:T(2,128)}, u32[]{:S(2)}) copy-start(f32[2,3,8]{2,0,1:T(2,128)} %param.23) | copy-start | bytes 580
  43.5 10.8 %copy-start.9 = (f32[2,3,8]{2,0,1:T(2,128)S(1)}, f32[2,3,8]{2,0,1:T(2,128)}, u32[]{:S(2)}) copy-start(f32[2,3,8]{2,0,1:T(2,128)} %param.24) | copy-start | bytes 580
  43.5 11.0 %copy-start.2 = (bf16[2,3,8,128]{3,2,1,0:T(8,128)(2,1)S(1)}, bf16[2,3,8,128]{3,2,1,0:T(8,128)(2,1)}, u32[]{:S(2)}) copy-start(bf16[2,3,8,128]{3,2,1,0:T(8,128)(2,1)} %value.1) | copy-start | bytes 36868
  43.5 11.0 %copy-start.3 = (bf16[2,3,8,128]{3,2,1,0:T(8,128)(2,1)S(1)}, bf16[2,3,8,128]{3,2,1,0:T(8,128)(2,1)}, u32[]{:S(2)}) copy-start(bf16[2,3,8,128]{3,2,1,0:T(8,128)(2,1)} %gate.1) | copy-start | bytes 36868
  43.5 11.1 %copy-start.4 = (bf16[2,3,4,128]{3,2,1,0:T(4,128)(2,1)S(1)}, bf16[2,3,4,128]{3,2,1,0:T(4,128)(2,1)}, u32[]{:S(2)}) copy-start(bf16[2,3,4,128]{3,2,1,0:T(4,128)(2,1)} %query.2) | copy-start | bytes 18436
  43.5 11.1 %copy-start.5 = (bf16[2,3,4,128]{3,2,1,0:T(4,128)(2,1)S(1)}, bf16[2,3,4,128]{3,2,1,0:T(4,128)(2,1)}, u32[]{:S(2)}) copy-start(bf16[2,3,4,128]{3,2,1,0:T(4,128)(2,1)} %key.1) | copy-start | bytes 18436
  44.1 13.6 %copy-start.6 = (bf16[2,3,1024]{2,0,1:T(2,128)(2,1)S(1)}, bf16[2,3,1024]{2,0,1:T(2,128)(2,1)}, u32[]{:S(2)}) copy-start(bf16[2,3,1024]{2,0,1:T(2,128)(2,1)} %param.18) | copy-start | bytes 36868
  44.1 21.8 %copy-start.1 = (bf16[2,3,16,256]{3,2,1,0:T(8,128)(2,1)S(1)}, bf16[2,3,16,256]{3,2,1,0:T(8,128)(2,1)}, u32[]{:S(2)}) copy-start(bf16[2,3,16,256]{3,2,1,0:T(8,128)(2,1)} %query.3) | copy-start | bytes 147460
  44.1 29.7 %copy-start.7 = (bf16[2,3,1024]{2,0,1:T(2,128)(2,1)S(1)}, bf16[2,3,1024]{2,0,1:T(2,128)(2,1)}, u32[]{:S(2)}) copy-start(bf16[2,3,1024]{2,0,1:T(2,128)(2,1)} %param.19) | copy-start | bytes 36868
  50.5 15.5 %all-to-all-start.1 = ((bf16[16,112,128]{2,1,0:T(8,128)(2,1)}), bf16[16,112,128]{2,1,0:T(8,128)(2,1)S(1)}, u32[]{:S(2)}, u32[]{:S(2)}) async-start(bf16[16,112,128]{2,1,0:T(8,128)(2,1)} %mix_rows.3), calls=%async_computation.1 | async-start | bytes 917504 | tf_op jit(solution)/shard_map/all_to_all | solution.py:456
  66.5 7.3 %collective-permute-start.5 = (f32[2,3,1024]{2,1,0:T(4,128)S(1)}, f32[2,3,1024]{2,1,0:T(4,128)S(1)}, u32[]{:S(2)}, u32[]{:S(2)}) collective-permute-start(f32[2,3,1024]{2,1,0:T(4,128)S(1)} %get-tuple-element.25), channel_id=1, source_target_pairs={{64,0},{96,64},{65,1},{97,65},{66,2},{98,66},{67,3},{99,67},{68,4}... | collective-permute-start | bytes 73736 | tf_op jit(solution)/shard_map/ppermute | solution.py:491
  67.8 6.0 %collective-permute-start.4 = (f32[2,3,1024]{2,1,0:T(4,128)S(1)}, f32[2,3,1024]{2,1,0:T(4,128)S(1)}, u32[]{:S(2)}, u32[]{:S(2)}) collective-permute-start(f32[2,3,1024]{2,1,0:T(4,128)S(1)} %get-tuple-element.24), channel_id=1, source_target_pairs={{64,32},{65,33},{66,34},{67,35},{68,36},{69,37},{70,38},{71,39},{7... | collective-permute-start | bytes 73736 | tf_op jit(solution)/shard_map/ppermute | solution.py:492

commit v4 on v3

v4 whole, which is shorter than its diff:
```python
import functools

import jax
import jax.numpy as jnp
from jax import lax
from jax.experimental import pallas as pl
from jax.experimental.pallas import tpu as pltpu
from jax.sharding import PartitionSpec as P

HQ = 16
KVH = 2
HD = 256
STEPS = 3
GROUP = HQ // KVH
QROWS = STEPS * GROUP
LANES = 128
NEGATIVE = -1e30

SLOTS = 32
SIZES = (8, 12, 12)
FIRSTS = (0, 8, 20)
CHUNKS = 3
GROUPS = ((8,), (4, 8), (4, 8))
NT = (((1,), (1,)), ((), ()))
LIMIT = 16 * 2**20
VMEM = pl.BlockSpec(memory_space=pltpu.VMEM)
SMEM = pl.BlockSpec(memory_space=pltpu.SMEM)
ANY = pl.BlockSpec(memory_space=pltpu.HBM)
PARAMS = pltpu.CompilerParams(vmem_limit_bytes=LIMIT)
FREE = pl.CostEstimate(flops=0, bytes_accessed=0, transcendentals=0)

def near(array):
    return pltpu.with_memory_space_constraint(array, pltpu.VMEM)


def far(array):
    return pltpu.with_memory_space_constraint(array, pltpu.HBM)


def prefill_row(order, slot, other=0):
    core = (lax.axis_index("wide") & 1) ^ other
    return order[4 * (slot // 2) + 2 * core + slot % 2]


def gather_kernel(order, cache, *refs, chunks):
    outs, (held, arrived, left) = refs[:-3], refs[-3:]
    reads, writes = [], []
    for chunk, out in zip(chunks, outs):
        for n in range(SIZES[chunk]):
            at = len(reads)
            reads.append(
                pltpu.make_async_copy(
                    cache.at[prefill_row(order, FIRSTS[chunk] + n, 1)], held.at[at], arrived.at[at]
                )
            )
            writes.append(pltpu.make_async_copy(held.at[at], out.at[n], left.at[at]))
    for read in reads:
        read.start()
    for read, write in zip(reads, writes):
        read.wait()
        write.start()
    for write in writes:
        write.wait()


def gather_rows(order, cache, chunks):
    count = sum(SIZES[chunk] for chunk in chunks)
    copies = pltpu.SemaphoreType.DMA((count,))
    return pl.pallas_call(
        functools.partial(gather_kernel, chunks=chunks),
        name="gather_rows",
        out_shape=[pltpu.HBM((SIZES[c], *cache.shape[1:]), cache.dtype) for c in chunks],
        in_specs=[SMEM, ANY],
        out_specs=[ANY] * len(chunks),
        scratch_shapes=[held_rows(cache, count), copies, copies],
        compiler_params=PARAMS,
        cost_estimate=FREE,
    )(far(order), far(cache))


def hold_kernel(array, out):
    pass


def hold(array, cost):
    return pl.pallas_call(
        hold_kernel,
        name="hold",
        out_shape=pltpu.VMEM(array.shape, array.dtype),
        in_specs=[VMEM],
        out_specs=VMEM,
        input_output_aliases={0: 0},
        compiler_params=PARAMS,
        cost_estimate=pl.CostEstimate(flops=cost, bytes_accessed=0, transcendentals=0),
    )(near(array))


def fetches(order, cache, swapped, own, other, arrived, chunk):
    groups, first = {}, 0
    for at, size in enumerate(GROUPS[chunk]):
        span = pl.ds(first, size)
        copies = [
            pltpu.make_async_copy(
                swapped.at[span], other.at[span], arrived.at[SIZES[chunk] + at]
            )
        ] + [
            pltpu.make_async_copy(
                cache.at[prefill_row(order, FIRSTS[chunk] + n)], own.at[n], arrived.at[n]
            )
            for n in range(first, first + size)
        ]
        groups[first] = copies
        first += size
    return groups


def start(groups):
    for copies in groups.values():
        for copy in copies:
            copy.start()


def wait(groups, first):
    for copy in groups.get(first, ()):
        copy.wait()


def held_rows(cache, size):
    return pltpu.VMEM((size, *cache.shape[1:]), cache.dtype)


def arrivals(chunk):
    return pltpu.SemaphoreType.DMA((SIZES[chunk] + len(GROUPS[chunk]),))


def score_kernel(order, lengths, query, cache, swapped, out, own, other, arrived, *, chunk):
    size = SIZES[chunk]
    span = own.shape[1]
    width = 2 * span

    @pl.when(lax.axis_index("head") < 2)
    def _():
        groups = fetches(order, cache, swapped, own, other, arrived, chunk)
        start(groups)
        lane = lax.broadcasted_iota(jnp.int32, (QROWS, LANES), 1)
        column = lax.broadcasted_iota(jnp.int32, (QROWS, span), 1)
        wide = lax.axis_index("wide")
        position = jnp.concatenate([column + wide * span, column + (wide ^ 1) * span], axis=1)
        extra = jnp.zeros((QROWS, LANES), jnp.float32)
        for n in range(size):
            wait(groups, n)
            slot = FIRSTS[chunk] + n
            q = query[slot]
            scores = jnp.concatenate(
                [
                    lax.dot_general(q, own[n], NT, preferred_element_type=jnp.float32),
                    lax.dot_general(q, other[n], NT, preferred_element_type=jnp.float32),
                ],
                axis=1,
            ) * (HD ** (-0.5))
            valid = position < lengths[prefill_row(order, slot)]
            scores = jnp.where(valid, scores, NEGATIVE)
            top = jnp.max(scores, axis=1, keepdims=True)
            top = top.astype(jnp.bfloat16).astype(jnp.float32)
            weights = jnp.where(valid, jnp.exp(scores - top), 0.0)
            total = jnp.sum(weights, axis=1, keepdims=True)
            coarse = total.astype(jnp.bfloat16).astype(jnp.float32)
            out[:, n * width : (n + 1) * width] = weights.astype(out.dtype)
            extra = jnp.where(lane == n, top, extra)
            extra = jnp.where(lane == n + size, coarse, extra)
            extra = jnp.where(lane == n + 2 * size, total - coarse, extra)
        out[:, size * width :] = extra.astype(out.dtype)


def score_rows(order, lengths, query, cache, swapped, chunk):
    size = SIZES[chunk]
    rows = held_rows(cache, size)
    return pl.pallas_call(
        functools.partial(score_kernel, chunk=chunk),
        name="score_rows",
        out_shape=pltpu.VMEM((QROWS, size * 2 * cache.shape[1] + LANES), jnp.bfloat16),
        in_specs=[SMEM, SMEM, VMEM, ANY, ANY],
        out_specs=VMEM,
        scratch_shapes=[rows, rows, arrivals(chunk)],
        compiler_params=PARAMS,
        cost_estimate=FREE,
    )(far(order), far(lengths), near(query), far(cache), far(swapped))


LINES = 2 * QROWS
SLAB = 2 * LINES + 16
EXTRAS = 8


def mix_kernel(order, weights, *refs, chunk):
    last = chunk + 1 == CHUNKS
    fetch_last = chunk + 2 == CHUNKS
    made, left = refs[-2:]
    if last:
        own, other = refs[:2]
        out = refs[-3]
    elif fetch_last:
        cache, swapped, swapped_last = refs[:3]
        out, own_last, other_last, own, other, arrived, arrived_last = refs[-9:-2]
    else:
        cache, swapped = refs[:2]
        out, own, other, arrived = refs[-6:-2]
    size = SIZES[chunk]
    span = own.shape[1]
    width = 2 * span

    @pl.when(lax.axis_index("head") >= 2)
    def _():
        if not last:
            groups = fetches(order, cache, swapped, own, other, arrived, chunk)
            start(groups)
        if fetch_last:
            groups_last = fetches(
                order, cache, swapped_last, own_last, other_last, arrived_last, chunk + 1
            )
            start(groups_last)
        extra = weights[:, size * width :].astype(jnp.float32)
        extra = jnp.concatenate([extra, jnp.zeros((LANES - QROWS, LANES), jnp.float32)], axis=0)
        extra = jnp.transpose(extra)
        blank = jnp.zeros((16 - 6, LANES), jnp.float32)
        for pair in range(size // 2):
            if not last:
                wait(groups, 2 * pair)
            rows, lines = [], []
            for n in (2 * pair, 2 * pair + 1):
                at = n * width
                rows.append(
                    jnp.dot(
                        weights[:, at : at + span], own[n], preferred_element_type=jnp.float32
                    )
                    + jnp.dot(
                        weights[:, at + span : at + width],
                        other[n],
                        preferred_element_type=jnp.float32,
                    )
                )
                lines += [extra[n + k * size : n + k * size + 1] for k in range(3)]
            slab = [row[:, :LANES] for row in rows] + [row[:, LANES:] for row in rows]
            made[pair] = jnp.concatenate([*slab, *lines, blank], axis=0).astype(made.dtype)
        copy = pltpu.make_async_copy(
            made, out.at[pl.ds(FIRSTS[chunk] // 2, size // 2)], left.at[0]
        )
        copy.start()
        copy.wait()
        if fetch_last:
            for first in groups_last:
                wait(groups_last, first)


def mix_rows(order, weights, cache, swapped, chunk, before, rows, cost):
    last = chunk + 1 == CHUNKS
    fetch_last = chunk + 2 == CHUNKS
    size = SIZES[chunk]
    held, held_last = held_rows(cache, size), held_rows(cache, SIZES[-1])
    payload = pltpu.HBM((SLOTS // 2, SLAB, LANES), jnp.bfloat16)
    if last:
        in_specs = [SMEM, VMEM, VMEM, VMEM]
        operands = [far(order), near(weights), near(rows[0]), near(rows[1])]
    else:
        in_specs = [SMEM, VMEM, ANY, ANY]
        operands = [far(order), near(weights), far(cache), far(swapped[chunk])]
    if fetch_last:
        in_specs.append(ANY)
        operands.append(far(swapped[chunk + 1]))
    aliases = {}
    if before is not None:
        in_specs.append(ANY)
        aliases = {len(operands): 0}
        operands.append(far(before))
    made = pl.pallas_call(
        functools.partial(mix_kernel, chunk=chunk),
        name="mix_rows",
        out_shape=[payload] + ([held_last, held_last] if fetch_last else []),
        in_specs=in_specs,
        out_specs=[ANY] + ([VMEM, VMEM] if fetch_last else []),
        input_output_aliases=aliases,
        scratch_shapes=([] if last else [held, held, arrivals(chunk)])
        + ([arrivals(CHUNKS - 1)] if fetch_last else [])
        + [pltpu.VMEM((size // 2, SLAB, LANES), jnp.bfloat16), pltpu.SemaphoreType.DMA((1,))],
        compiler_params=PARAMS,
        cost_estimate=pl.CostEstimate(flops=cost, bytes_accessed=0, transcendentals=0),
    )(*operands)
    return made[0], made[1:]


def combine_kernel(parts, query, fresh, low, high):
    @pl.when(lax.axis_index("head") >= 2)
    def _():
        chips = parts.shape[0]
        second = lax.axis_index("head") & 1
        half = KVH * HD
        extras = jnp.stack(
            [parts[chip, 2 * LINES :].astype(jnp.float32)[:EXTRAS] for chip in range(chips)]
        )
        tops = [extras[:, 3 * row] for row in range(2)]
        totals = [extras[:, 3 * row + 1] + extras[:, 3 * row + 2] for row in range(2)]
        step = lax.broadcasted_iota(jnp.int32, (QROWS, STEPS), 0) // GROUP
        time = lax.broadcasted_iota(jnp.int32, (QROWS, STEPS), 1)
        keep = time <= step
        scores, values = [], []
        for row in range(2):
            news = fresh[row].astype(jnp.float32)
            keys = jnp.where(second == 1, news[:, HD:half], news[:, :HD])
            values.append(jnp.where(second == 1, news[:, half + HD :], news[:, half : half + HD]))
            q = jnp.where(second == 1, query[row, :, GROUP:], query[row, :, :GROUP])
            q = q.reshape(QROWS, HD).astype(jnp.float32)
            columns = [
                jnp.sum(q * keys[t : t + 1], axis=1, keepdims=True) for t in range(STEPS)
            ]
            score = jnp.concatenate(columns, axis=1) * (HD ** (-0.5))
            scores.append(jnp.where(keep, score, NEGATIVE))
        lines, marks = [], []
        for row in range(2):
            top = jnp.max(tops[row], axis=0, keepdims=True)
            factors = jnp.exp(tops[row] - top)
            lines += [top, jnp.sum(factors * totals[row], axis=0, keepdims=True)]
            marks.append(factors)
        blank = jnp.zeros((LANES - 4 - 2 * chips, LANES), jnp.float32)
        columns = jnp.transpose(jnp.concatenate([*marks, *lines, blank], axis=0))[:QROWS]
        halves = []
        for row in range(2):
            at = 2 * chips + 2 * row
            cached = columns[:, at : at + 1]
            top = jnp.maximum(cached, jnp.max(scores[row], axis=1, keepdims=True))
            scale = jnp.exp(cached - top)
            probs = jnp.where(keep, jnp.exp(scores[row] - top), 0.0)
            total = columns[:, at + 1 : at + 2] * scale + jnp.sum(probs, axis=1, keepdims=True)
            probs = probs.astype(jnp.bfloat16).astype(jnp.float32)
            mixed = sum(probs[:, t : t + 1] * values[row][t : t + 1] for t in range(STEPS))
            first = row * QROWS
            sides = []
            for k in range(2):
                acc = jnp.zeros((QROWS, LANES), jnp.float32)
                for chip in range(chips):
                    span = slice(k * LINES + first, k * LINES + first + QROWS)
                    part = parts[chip, span].astype(jnp.float32)
                    at = row * chips + chip
                    acc = acc + columns[:, at : at + 1] * part
                sides.append(acc * scale + mixed[:, k * LANES : (k + 1) * LANES])
            halves.append(jnp.concatenate(sides, axis=1) / total)
        heads = GROUP // 2
        for row in range(2):
            for s in range(STEPS):
                for a in range(heads):
                    at = s * GROUP + a
                    span = slice(a * HD, (a + 1) * HD)
                    low[s, row : row + 1, span] = halves[row][at : at + 1]
                    high[s, row : row + 1, span] = halves[row][at + heads : at + heads + 1]


def combine(parts, query, fresh):
    heads = GROUP // 2
    shape = pltpu.VMEM((STEPS, 2, heads * HD), jnp.float32)
    return pl.pallas_call(
        combine_kernel,
        name="combine_parts",
        out_shape=(shape, shape),
        in_specs=[VMEM, VMEM, VMEM],
        out_specs=(VMEM, VMEM),
        compiler_params=PARAMS,
        cost_estimate=FREE,
    )(near(parts), near(query), near(fresh))


NEAR = 4


def block_kernel(*refs, moves):
    for target, at, source, place in moves:
        refs[target][at] = refs[source][place].astype(refs[target].dtype)


def move_blocks(name, arrays, shapes, moves):
    count = len(arrays)
    return pl.pallas_call(
        functools.partial(
            block_kernel, moves=[(count + t, at, source, place) for t, at, source, place in moves]
        ),
        name=name,
        out_shape=[pltpu.VMEM(shape, jnp.bfloat16) for shape in shapes],
        in_specs=[VMEM] * count,
        out_specs=[VMEM] * len(shapes),
        compiler_params=PARAMS,
        cost_estimate=FREE,
    )(*[near(array) for array in arrays])


def split_kernel(order, states, mine, theirs):
    wide = lax.axis_index("wide")
    for z in range(NEAR):
        for y in range(NEAR):
            chip = (wide >> 1) ^ (4 * y + z)
            for row in range(2):
                at = 4 * chip + 2 * (wide & 1) + row
                mine[z, y, row] = states[order[at]].astype(mine.dtype)
                theirs[z, y, row] = states[order[at ^ 2]].astype(theirs.dtype)


def split_states(order, states):
    shape = pltpu.VMEM((NEAR, NEAR, 2, *states.shape[1:]), jnp.bfloat16)
    return pl.pallas_call(
        split_kernel,
        name="split_states",
        out_shape=(shape, shape),
        in_specs=[SMEM, VMEM],
        out_specs=(VMEM, VMEM),
        compiler_params=PARAMS,
        cost_estimate=FREE,
    )(far(order), near(states))


def along_z(mine, other):
    shape = (2, *mine.shape[1:])
    moves = [(z, core, core, z) for z in range(NEAR) for core in range(2)]
    return move_blocks("pack_z", [mine, other], [shape] * NEAR, moves)


def along_y(blocks):
    shape = (NEAR, 2, *blocks[0].shape[2:])
    moves = [
        (y, (z, core), z, (core, y)) for y in range(NEAR) for z in range(NEAR) for core in range(2)
    ]
    return move_blocks("pack_y", blocks, [shape] * NEAR, moves)


def join_kernel(*refs):
    blocks, out = refs[:NEAR], refs[NEAR]
    wide = lax.axis_index("wide")
    for y in range(NEAR):
        for z in range(NEAR):
            for core in range(2):
                out[wide ^ (8 * y + 2 * z + core)] = blocks[y][z, core]


def join_states(blocks):
    shape = (2 * NEAR * NEAR, *blocks[0].shape[2:])
    return pl.pallas_call(
        join_kernel,
        name="join_states",
        out_shape=pltpu.VMEM(shape, jnp.bfloat16),
        in_specs=[VMEM] * NEAR,
        out_specs=VMEM,
        compiler_params=PARAMS,
        cost_estimate=FREE,
    )(*[near(block) for block in blocks])


def delta_kernel(decay, beta, states, query, key, value, gate, out, final, rows):
    batch, steps, heads_k, width = key.shape
    heads_v = value.shape[2]
    ratio = heads_v // heads_k
    keys_at = batch * steps * heads_k

    def column(row, step, head):
        return (row * steps + step) * heads_k + head

    rows[...] = jnp.zeros_like(rows)
    for row in range(batch):
        for step in range(steps):
            at = column(row, step, 0)
            q = query[row, step].astype(jnp.float32)
            k = key[row, step].astype(jnp.float32)
            q = q * lax.rsqrt(jnp.sum(q * q, -1, keepdims=True) + 1e-06) * width ** (-0.5)
            k = k * lax.rsqrt(jnp.sum(k * k, -1, keepdims=True) + 1e-06)
            rows[at : at + heads_k] = q
            rows[keys_at + at : keys_at + at + heads_k] = k
    columns = jnp.transpose(rows[...])
    for row in range(batch):
        made = [[] for _ in range(steps)]
        values = [value[row, step].astype(jnp.float32) for step in range(steps)]
        for head in range(heads_v):
            state = states[row, head].astype(jnp.float32)
            for step in range(steps):
                at = column(row, step, head // ratio)
                q = columns[:, at : at + 1]
                k = columns[:, keys_at + at : keys_at + at + 1]
                rate = decay[row, step, head]
                recalled = jnp.sum(k * state, axis=0, keepdims=True)
                change = beta[row, step, head] * (values[step][head : head + 1] - rate * recalled)
                state = rate * state + k * change
                made[step].append(jnp.sum(q * state, axis=0, keepdims=True))
            final[row, head] = state
        for step in range(steps):
            read = jnp.concatenate(made[step], axis=0)
            read = read * lax.rsqrt(jnp.mean(read * read, -1, keepdims=True) + 1e-06)
            level = gate[row, step].astype(jnp.float32)
            out[row, step] = (read * (level * jax.nn.sigmoid(level))).astype(out.dtype)


def delta_rule(states, query, key, value, decay, beta, gate):
    width = key.shape[-1]
    return pl.pallas_call(
        delta_kernel,
        name="delta_rule",
        out_shape=(
            jax.ShapeDtypeStruct(value.shape, jnp.bfloat16),
            jax.ShapeDtypeStruct(states.shape, jnp.float32),
        ),
        in_specs=[SMEM, SMEM] + [VMEM] * 5,
        out_specs=(VMEM, VMEM),
        scratch_shapes=[pltpu.VMEM((width, width), jnp.float32)],
        compiler_params=PARAMS,
        cost_estimate=FREE,
    )(decay, beta, states, query, key, value, gate)


def on_device(
    kv_cache,
    lin_states,
    row_order,
    prompt_lengths,
    att_query,
    new_kv,
    att_gate,
    lin_query,
    lin_key,
    lin_value,
    lin_decay,
    lin_beta,
    lin_gate,
):
    wide_count = lax.axis_size("wide")
    chips = wide_count // 2
    head_index = lax.axis_index("head")
    def across(array, distance=1):
        pairs = [(i, i ^ distance) for i in range(wide_count)]
        return lax.ppermute(array, "wide", pairs)

    def after(array, *others):
        return lax.optimization_barrier((array, *others))[0]

    same_core = [[2 * k + c for k in range(chips)] for c in range(2)]

    def between_chips(array):
        return lax.all_to_all(array, "wide", 0, 0, tiled=True, axis_index_groups=same_core)

    sides = [
        jnp.broadcast_to(side.reshape(1, 2, QROWS, HD), (chips, 2, QROWS, HD))
        for side in (att_query[:, :, :GROUP], att_query[:, :, GROUP:])
    ]
    copies = jnp.where(head_index % KVH == 1, sides[1], sides[0])
    query = hold(between_chips(copies.reshape(2 * chips, QROWS, HD)), 30 * 10**9)

    made = gather_rows(row_order, kv_cache, (0,))
    made += gather_rows(after(row_order, *made), kv_cache, tuple(range(1, CHUNKS)))
    rows_all, heads, depth, width = lin_states.shape
    mine, theirs = split_states(
        after(row_order, *made), lin_states.reshape(rows_all, heads * depth, width)
    )
    swapped = [across(part) for part in made]
    other = across(theirs)

    weights = []
    for chunk in range(CHUNKS):
        order = after(row_order, theirs, *weights)
        weights.append(
            score_rows(order, prompt_lengths, query, kv_cache, swapped[chunk], chunk)
        )
    moved = [lax.ppermute(made, "head", [(0, 2), (1, 3)]) for made in weights]

    blocks = along_z(after(mine, weights[-1]), other)
    blocks = [blocks[0]] + [across(block, 2 * z) for z, block in enumerate(blocks[1:], 1)]
    blocks = along_y(blocks)

    payload, rows = None, None
    for chunk in range(CHUNKS):
        cost = 10 * 10**9 if chunk + 1 == CHUNKS else 10**8
        payload, rows = mix_rows(
            after(row_order, weights[-1]), moved[chunk], kv_cache, swapped, chunk, payload, rows,
            cost,
        )
    parts = between_chips(after(payload, *blocks))
    blocks = [blocks[0]] + [across(block, 8 * y) for y, block in enumerate(blocks[1:], 1)]
    states = join_states(blocks).reshape(wide_count, 2, heads, depth, width)
    states = states.transpose(1, 2, 0, 3, 4).reshape(2, heads, wide_count * depth, width)
    lin_out, final_states = delta_rule(
        states, lin_query, lin_key, lin_value, lin_decay, lin_beta, lin_gate
    )
    low, high = combine(parts, att_query, after(new_kv, lin_out))
    low_here = lax.ppermute(low, "head", [(2, 0), (3, 2)])
    high_here = lax.ppermute(high, "head", [(2, 1)])
    result = jnp.where(
        head_index == 3, high, jnp.where(head_index == 1, high_here, low_here)
    )
    gate = jnp.transpose(att_gate, (1, 0, 2)).astype(jnp.float32)
    att_out = (result * jax.nn.sigmoid(gate)).astype(jnp.bfloat16)
    att_out = jnp.transpose(att_out, (1, 0, 2))
    return (att_out, lin_out, final_states)


def solution(mesh):
    placed = (
        P(None, "wide", "head"),
        P(None, "head", "wide", None),
        P(),
        P(),
        P("wide", None, None, None),
        P("wide", None, None),
        P("wide", None, "head"),
        P("wide", None, "head", None),
        P("wide", None, "head", None),
        P("wide", None, "head", None),
        P("wide", None, "head"),
        P("wide", None, "head"),
        P("wide", None, "head", None),
    )
    return jax.shard_map(
        on_device,
        mesh=mesh,
        in_specs=placed,
        out_specs=(
            P("wide", None, "head"),
            P("wide", None, "head", None),
            P("wide", "head", None, None),
        ),
        check_vma=False,
    )
```

time: 75.1 us -> 81.4 us (1.084)
  starting transfers between devices: 24.6 us -> 30.6 us
  Pallas kernels: 20.5 us -> 23.6 us
  local copies, waits for them, and re-layouts: 4.46 us -> 2.23 us
  waiting for transfers between devices: 23.2 us -> 21.8 us
    ppermute x2 -> x10, waiting for transfers between devices: 0.01 us -> 15.5 us  [across(): return lax.ppermute(array, 'wide', pairs)]
    ppermute x2 -> x10, starting transfers between devices: 0.64 us -> 10.7 us  [across(): return lax.ppermute(array, 'wide', pairs)]
    all_to_all x1 -> x0, starting transfers between devices: 7.48 us -> none  [on_device(): lax.all_to_all(after(taken, weights[-1]), 'wide', split_axis=0, concat_ax...]
    all_to_all x2, waiting for transfers between devices: 8.23 us -> 1.03 us  [between_chips(): lax.all_to_all(array, 'wide', 0, 0, tiled=True, axis_index_groups=same_core)]
    all_to_all x1 -> x0, waiting for transfers between devices: 6.33 us -> none  [on_device(): lax.all_to_all(after(taken, weights[-1]), 'wide', split_axis=0, concat_ax...]
    ppermute x2 -> x3, waiting for transfers between devices: 3.27 us -> 0.01 us  [on_device(): moved = [lax.ppermute(made, 'head', [(0, 2), (1, 3)]) for made in weights]]
    ppermute x2 -> x3, starting transfers between devices: 2.63 us -> 5.17 us  [on_device(): moved = [lax.ppermute(made, 'head', [(0, 2), (1, 3)]) for made in weights]]
    gather x1 -> x0, local copies, waits for them, and re-layouts: 1.9 us -> none  [on_device(): lin_states.at[row_order].get(mode='promise_in_bounds', unique_indices=True)]
  transfers between devices with their start and end apart: 9 -> 17, of which waited for: 4 -> 7; matrix products, arithmetic and copies ran while one was open for 4% -> 0% of each run, Pallas kernels for 27% -> 28%
where the time goes in v4:
time: 81.4 us; the launch traced here: 80.7 us
  starting transfers between devices  30.6 us (38%)
  Pallas kernels  23.6 us (29%)
  waiting for transfers between devices  21.8 us (27%)
  local copies, waits for them, and re-layouts  2.23 us (3%)
  other arithmetic  1.41 us (2%)
  between operations  1.01 us (1%)
    ppermute x10, waiting for transfers between devices, across(): return lax.ppermute(array, 'wide', pairs)  15.5 us
    all_to_all x2, starting transfers between devices, between_chips(): lax.all_to_all(array, 'wide', 0, 0, tiled=True, axis_index_groups=same_core)  12.8 us
    ppermute x10, starting transfers between devices, across(): return lax.ppermute(array, 'wide', pairs)  10.7 us
    pallas_call x3, Pallas kernels, score_rows(): pl.pallas_call(functools.partial(score_kernel, chunk=chunk), name='score_...  10.2 us
    pallas_call x2, Pallas kernels, gather_rows(): pl.pallas_call(functools.partial(gather_kernel, chunks=chunks), name='gat...  6.88 us
    ppermute x1, waiting for transfers between devices, on_device(): low_here = lax.ppermute(low, 'head', [(2, 0), (3, 2)])  5.25 us
    ppermute x3, starting transfers between devices, on_device(): moved = [lax.ppermute(made, 'head', [(0, 2), (1, 3)]) for made in weights]  5.17 us
    pallas_call x1, Pallas kernels, delta_rule(): pl.pallas_call(delta_kernel, name='delta_rule', out_shape=(jax.ShapeDtype...  3.15 us
  transfers between devices with their start and end apart: 17, of which 7 were waited for; matrix products, arithmetic and copies ran while one was open for 0% of the time, Pallas kernels for 28%

profile of v4, /device:TPU:0, one launch (start us, length us, event | category | flops | bytes accessed | tf_op | source)
XLA Modules:
  0.0 80.7 jit_solution(3171273468757592944)
XLA Ops:
  0.6 0.8 select_bitcast_fusion
  1.4 0.8 broadcast_in_dim.2
  2.2 8.1 %all-to-all-start = ((bf16[32,24,256]{2,1,0:T(8,128)(2,1)}), bf16[32,24,256]{2,1,0:T(8,128)(2,1)S(1)}, u32[]{:S(2)}, u32[]{:S(2)}) async-start(bf16[32,24,256]{2,1,0:T(8,128)(2,1)} %bitcast.2), calls=%async_computation | async-start | bytes 786432 | tf_op jit(solution)/shard_map/all_to_all | solution.py:540
  10.3 2.8 %gather_rows.2 = bf16[8,256,256]{2,1,0:T(8,128)(2,1)} custom-call(s32[64]{0:T(128)} %order.9, bf16[64,256,256]{2,1,0:T(8,128)(2,1)} %refs_0_.3), custom_call_target="tpu_custom_call" | custom-call | tf_op jit(solution)/shard_map/gather_rows/pallas_call | solution.py:69
  13.1 0.0 copy-start
  13.1 0.1 collective-permute-start
  13.2 4.1 %gather_rows.3 = (bf16[12,256,256]{2,1,0:T(8,128)(2,1)}, bf16[12,256,256]{2,1,0:T(8,128)(2,1)}) custom-call(s32[64]{0:T(128)} %order.9, bf16[64,256,256]{2,1,0:T(8,128)(2,1)} %refs_0_.3), custom_call_target="tpu_custom_call" | custom-call | tf_op jit(solution)/shard_map/gather_rows/pallas_call | solution.py:69
  17.3 0.4 collective-permute-start.1
  17.8 0.2 collective-permute-start.2
  17.9 0.8 split_states.1
  18.7 0.4 collective-permute-start.6
  19.1 1.0 %all-to-all-done.array = bf16[32,24,256]{2,1,0:T(8,128)(2,1)S(1)} async-done(((bf16[32,24,256]{2,1,0:T(8,128)(2,1)}), bf16[32,24,256]{2,1,0:T(8,128)(2,1)S(1)}, u32[]{:S(2)}, u32[]{:S(2)}) %all-to-all-start) | async-done | bytes 393248 | tf_op jit(solution)/shard_map/all_to_all | solution.py:540
  20.2 3.1 %score_rows.3 = bf16[24,4224]{1,0:T(8,128)(2,1)S(1)} custom-call(s32[64]{0:T(128)} %order.9, s32[64]{0:T(128)} %lengths.5, bf16[32,24,256]{2,1,0:T(8,128)(2,1)S(1)} %hold.1.query, bf16[64,256,256]{2,1,0:T(8,128)(2,1)} %refs_0_.3, bf16[8,256,256]{2,1,0:T(8,128)(2,1)} %collective-permute-done.swapped.refs_1_), custom_call_target="tpu_custom_call" | custom-call | tf_op jit(solution)/shard_map/score_rows/pallas_call | solution.py:178
  23.3 2.6 %collective-permute-start.5 = (bf16[24,4224]{1,0:T(8,128)(2,1)S(1)}, bf16[24,4224]{1,0:T(8,128)(2,1)S(1)}, u32[]{:S(2)}, u32[]{:S(2)}) collective-permute-start(bf16[24,4224]{1,0:T(8,128)(2,1)S(1)} %score_rows.3), channel_id=1, source_target_pairs={{0,64},{32,96},{1,65},{33,97},{2,66},{34,98},{3,67},{35,99},{4,68}... | collective-permute-start | bytes 608264 | tf_op jit(solution)/shard_map/ppermute | solution.py:564
  25.9 1.1 %copy-done.6 = bf16[12,256,256]{2,1,0:T(8,128)(2,1)} copy-done((bf16[12,256,256]{2,1,0:T(8,128)(2,1)}, bf16[12,256,256]{2,1,0:T(8,128)(2,1)S(1)}, u32[]{:S(2)}) %copy-start.6) | copy-done | bytes 1572888
  27.0 3.5 %score_rows.4 = bf16[24,6272]{1,0:T(8,128)(2,1)S(1)} custom-call(s32[64]{0:T(128)} %order.9, s32[64]{0:T(128)} %lengths.5, bf16[32,24,256]{2,1,0:T(8,128)(2,1)S(1)} %hold.1.query, bf16[64,256,256]{2,1,0:T(8,128)(2,1)} %refs_0_.3, bf16[12,256,256]{2,1,0:T(8,128)(2,1)} %copy-done.6), custom_call_target="tpu_custom_call" | custom-call | tf_op jit(solution)/shard_map/score_rows/pallas_call | solution.py:178
  30.6 1.3 %collective-permute-start.4 = (bf16[24,6272]{1,0:T(8,128)(2,1)S(1)}, bf16[24,6272]{1,0:T(8,128)(2,1)S(1)}, u32[]{:S(2)}, u32[]{:S(2)}) collective-permute-start(bf16[24,6272]{1,0:T(8,128)(2,1)S(1)} %score_rows.4), channel_id=1, source_target_pairs={{0,64},{32,96},{1,65},{33,97},{2,66},{34,98},{3,67},{35,99},{4,68}... | collective-permute-start | bytes 903176 | tf_op jit(solution)/shard_map/ppermute | solution.py:564
  31.9 3.5 %score_rows.5 = bf16[24,6272]{1,0:T(8,128)(2,1)S(1)} custom-call(s32[64]{0:T(128)} %order.9, s32[64]{0:T(128)} %lengths.5, bf16[32,24,256]{2,1,0:T(8,128)(2,1)S(1)} %hold.1.query, bf16[64,256,256]{2,1,0:T(8,128)(2,1)} %refs_0_.3, bf16[12,256,256]{2,1,0:T(8,128)(2,1)} %collective-permute-done.2.swapped.refs_2_), custom_call_target="tpu_custom_call" | custom-call | tf_op jit(solution)/shard_map/score_rows/pallas_call | solution.py:178
  35.4 1.3 %collective-permute-start.3 = (bf16[24,6272]{1,0:T(8,128)(2,1)S(1)}, bf16[24,6272]{1,0:T(8,128)(2,1)S(1)}, u32[]{:S(2)}, u32[]{:S(2)}) collective-permute-start(bf16[24,6272]{1,0:T(8,128)(2,1)S(1)} %score_rows.5), channel_id=1, source_target_pairs={{0,64},{32,96},{1,65},{33,97},{2,66},{34,98},{3,67},{35,99},{4,68}... | collective-permute-start | bytes 903176 | tf_op jit(solution)/shard_map/ppermute | solution.py:564
  36.8 1.0 %collective-permute-start.7 = (bf16[2,4,2,32,128]{4,3,2,1,0:T(8,128)(2,1)S(1)}, bf16[2,4,2,32,128]{4,3,2,1,0:T(8,128)(2,1)S(1)}, u32[]{:S(2)}, u32[]{:S(2)}) collective-permute-start(bf16[2,4,2,32,128]{4,3,2,1,0:T(8,128)(2,1)S(1)} %get-tuple-element.46), channel_id=1, source_target_pairs={{0,2},{1,3},{2,0},{3,1},{4,6},{5,7},{6,4},{7,5},{8,10},{9,11},{10,... | collective-permute-start | bytes 393224 | tf_op jit(solution)/shard_map/ppermute | solution.py:532
  37.7 2.7 %collective-permute-start.8 = (bf16[2,4,2,32,128]{4,3,2,1,0:T(8,128)(2,1)S(1)}, bf16[2,4,2,32,128]{4,3,2,1,0:T(8,128)(2,1)S(1)}, u32[]{:S(2)}, u32[]{:S(2)}) collective-permute-start(bf16[2,4,2,32,128]{4,3,2,1,0:T(8,128)(2,1)S(1)} %get-tuple-element.47), channel_id=1, source_target_pairs={{0,4},{1,5},{2,6},{3,7},{4,0},{5,1},{6,2},{7,3},{8,12},{9,13},{10,... | collective-permute-start | bytes 393224 | tf_op jit(solution)/shard_map/ppermute | solution.py:532
  40.4 1.1 %collective-permute-start.9 = (bf16[2,4,2,32,128]{4,3,2,1,0:T(8,128)(2,1)S(1)}, bf16[2,4,2,32,128]{4,3,2,1,0:T(8,128)(2,1)S(1)}, u32[]{:S(2)}, u32[]{:S(2)}) collective-permute-start(bf16[2,4,2,32,128]{4,3,2,1,0:T(8,128)(2,1)S(1)} %get-tuple-element.48), channel_id=1, source_target_pairs={{0,6},{1,7},{2,4},{3,5},{4,2},{5,3},{6,0},{7,1},{8,14},{9,15},{10,... | collective-permute-start | bytes 393224 | tf_op jit(solution)/shard_map/ppermute | solution.py:532
  41.6 0.8 mix_rows.3.refs_3_
  42.3 0.6 collective-permute-done.7.refs_1_
  42.9 3.7 %collective-permute-done.8.refs_2_ = bf16[2,4,2,32,128]{4,3,2,1,0:T(8,128)(2,1)S(1)} collective-permute-done((bf16[2,4,2,32,128]{4,3,2,1,0:T(8,128)(2,1)S(1)}, bf16[2,4,2,32,128]{4,3,2,1,0:T(8,128)(2,1)S(1)}, u32[]{:S(2)}, u32[]{:S(2)}) %collective-permute-start.8) | collective-permute-done | bytes 131104 | tf_op jit(solution)/shard_map/ppermute | solution.py:532
  46.6 2.1 %collective-permute-done.9.refs_3_ = bf16[2,4,2,32,128]{4,3,2,1,0:T(8,128)(2,1)S(1)} collective-permute-done((bf16[2,4,2,32,128]{4,3,2,1,0:T(8,128)(2,1)S(1)}, bf16[2,4,2,32,128]{4,3,2,1,0:T(8,128)(2,1)S(1)}, u32[]{:S(2)}, u32[]{:S(2)}) %collective-permute-start.9) | collective-permute-done | bytes 131104 | tf_op jit(solution)/shard_map/ppermute | solution.py:532
  48.7 0.9 %mix_rows.4 = (bf16[16,112,128]{2,1,0:T(8,128)(2,1)}, bf16[12,256,256]{2,1,0:T(8,128)(2,1)S(1)}, bf16[12,256,256]{2,1,0:T(8,128)(2,1)S(1)}) custom-call(s32[64]{0:T(128)} %order.9, bf16[24,6272]{1,0:T(8,128)(2,1)S(1)} %collective-permute-done.4.weights, bf16[64,256,256]{2,1,0:T(8,128)(2,1)} %refs_0_.3, ...), custom_call_target="tpu_custom_call", output_to_operand_aliasing={{0}: (5, {})} | custom-call | flops 100000000 | tf_op jit(solution)/shard_map/mix_rows/pallas_call | solution.py:275
  49.7 0.0 copy-start.9
  49.7 0.0 copy-start.10
  49.7 0.8 %mix_rows.5 = bf16[16,112,128]{2,1,0:T(8,128)(2,1)} custom-call(s32[64]{0:T(128)} %order.9, bf16[24,6272]{1,0:T(8,128)(2,1)S(1)} %collective-permute-done.3.weights, bf16[12,256,256]{2,1,0:T(8,128)(2,1)S(1)} %get-tuple-element.40.refs_0_, bf16[12,256,256]{2,1,0:T(8,128)(2,1)S(1)} %get-tuple-element.41.refs_1_, ...), custom_call_target="tpu_custom_call", output_to_operand_aliasing={{}: (4, {})} | custom-call | flops 10000000000 | tf_op jit(solution)/shard_map/mix_rows/pallas_call | solution.py:275
  50.5 0.0 copy-start.2
  50.5 0.0 copy-start.3
  50.6 0.0 copy-start.4
  50.6 0.0 copy-start.5
  50.6 0.0 copy-start.7
  50.6 4.7 %all-to-all-start.1 = ((bf16[16,112,128]{2,1,0:T(8,128)(2,1)}), bf16[16,112,128]{2,1,0:T(8,128)(2,1)S(1)}, u32[]{:S(2)}, u32[]{:S(2)}) async-start(bf16[16,112,128]{2,1,0:T(8,128)(2,1)} %mix_rows.5), calls=%async_computation.1 | async-start | bytes 917504 | tf_op jit(solution)/shard_map/all_to_all | solution.py:540
  55.3 2.0 %collective-permute-start.10 = (bf16[4,2,2,32,128]{4,3,2,1,0:T(8,128)(2,1)S(1)}, bf16[4,2,2,32,128]{4,3,2,1,0:T(8,128)(2,1)S(1)}, u32[]{:S(2)}, u32[]{:S(2)}) collective-permute-start(bf16[4,2,2,32,128]{4,3,2,1,0:T(8,128)(2,1)S(1)} %get-tuple-element.50), channel_id=1, source_target_pairs={{0,8},{1,9},{2,10},{3,11},{4,12},{5,13},{6,14},{7,15},{8,0},{9,1},... | collective-permute-start | bytes 393224 | tf_op jit(solution)/shard_map/ppermute | solution.py:532
  57.3 2.7 %collective-permute-start.11 = (bf16[4,2,2,32,128]{4,3,2,1,0:T(8,128)(2,1)S(1)}, bf16[4,2,2,32,128]{4,3,2,1,0:T(8,128)(2,1)S(1)}, u32[]{:S(2)}, u32[]{:S(2)}) collective-permute-start(bf16[4,2,2,32,128]{4,3,2,1,0:T(8,128)(2,1)S(1)} %get-tuple-element.51), channel_id=1, source_target_pairs={{0,16},{1,17},{2,18},{3,19},{4,20},{5,21},{6,22},{7,23},{8,24},{9,... | collective-permute-start | bytes 393224 | tf_op jit(solution)/shard_map/ppermute | solution.py:532
  60.0 0.1 collective-permute-start.12
  60.1 0.0 copy-start.8
  60.1 6.2 %collective-permute-done.10.refs_1_ = bf16[4,2,2,32,128]{4,3,2,1,0:T(8,128)(2,1)S(1)} collective-permute-done((bf16[4,2,2,32,128]{4,3,2,1,0:T(8,128)(2,1)S(1)}, bf16[4,2,2,32,128]{4,3,2,1,0:T(8,128)(2,1)S(1)}, u32[]{:S(2)}, u32[]{:S(2)}) %collective-permute-start.10) | collective-permute-done | bytes 131104 | tf_op jit(solution)/shard_map/ppermute | solution.py:532
  66.3 2.9 %collective-permute-done.11.refs_2_ = bf16[4,2,2,32,128]{4,3,2,1,0:T(8,128)(2,1)S(1)} collective-permute-done((bf16[4,2,2,32,128]{4,3,2,1,0:T(8,128)(2,1)S(1)}, bf16[4,2,2,32,128]{4,3,2,1,0:T(8,128)(2,1)S(1)}, u32[]{:S(2)}, u32[]{:S(2)}) %collective-permute-start.11) | collective-permute-done | bytes 131104 | tf_op jit(solution)/shard_map/ppermute | solution.py:532
  69.3 0.2 copy.19
  69.6 3.2 %delta_rule.1 = (bf16[2,3,8,128]{3,2,1,0:T(8,128)(2,1)}, f32[2,8,128,128]{3,2,1,0:T(8,128)}) custom-call(f32[2,3,8]{2,1,0:T(4,128)S(1)} %copy.20.decay, f32[2,3,8]{2,1,0:T(4,128)S(1)} %copy.21.beta, bf16[2,8,128,128]{3,2,1,0:T(8,128)(2,1)S(1)} %bitcast.16, bf16[2,3,4,128]{3,2,1,0:T(4,128)(2,1)S(1)} %copy-done.4, bf16[2,3,4,128]{3,2,1,0:T(4,128)(2,1)S(1)} %copy-done.5, ...), custom_call_target="tpu_custom_call" | custom-call | tf_op jit(solution)/shard_map/delta_rule/pallas_call | solution.py:497
  72.8 1.3 %collective-permute-start.14 = (f32[3,2,1024]{2,1,0:T(2,128)S(1)}, f32[3,2,1024]{2,1,0:T(2,128)S(1)}, u32[]{:S(2)}, u32[]{:S(2)}) collective-permute-start(f32[3,2,1024]{2,1,0:T(2,128)S(1)} %get-tuple-element.57), channel_id=1, source_target_pairs={{64,0},{96,64},{65,1},{97,65},{66,2},{98,66},{67,3},{99,67},{68,4}... | collective-permute-start | bytes 73736 | tf_op jit(solution)/shard_map/ppermute | solution.py:585
  74.1 0.7 collective-permute-start.13
  74.8 5.2 %collective-permute-done.14 = f32[3,2,1024]{2,1,0:T(2,128)S(1)} collective-permute-done((f32[3,2,1024]{2,1,0:T(2,128)S(1)}, f32[3,2,1024]{2,1,0:T(2,128)S(1)}, u32[]{:S(2)}, u32[]{:S(2)}) %collective-permute-start.14) | collective-permute-done | bytes 24608 | tf_op jit(solution)/shard_map/ppermute | solution.py:585
  80.0 0.6 fusion.1
  (30 shorter events, 0.2 us)
Async XLA Ops:
  2.2 18.0 %all-to-all-start = ((bf16[32,24,256]{2,1,0:T(8,128)(2,1)}), bf16[32,24,256]{2,1,0:T(8,128)(2,1)S(1)}, u32[]{:S(2)}, u32[]{:S(2)}) async-start(bf16[32,24,256]{2,1,0:T(8,128)(2,1)} %bitcast.2), calls=%async_computation | async-start | bytes 786432 | tf_op jit(solution)/shard_map/all_to_all | solution.py:540
  13.1 4.8 %copy-start = (f32[64,8,4,128]{3,2,1,0:T(4,128)S(1)}, f32[64,8,4,128]{3,2,1,0:T(4,128)}, u32[]{:S(2)}) copy-start(f32[64,8,4,128]{3,2,1,0:T(4,128)} %param.14) | copy-start | bytes 3145732
  13.1 7.0 %collective-permute-start = (bf16[8,256,256]{2,1,0:T(8,128)(2,1)}, bf16[8,256,256]{2,1,0:T(8,128)(2,1)}, u32[]{:S(2)}, u32[]{:S(2)}) collective-permute-start(bf16[8,256,256]{2,1,0:T(8,128)(2,1)} %gather_rows.2), channel_id=1, source_target_pairs={{0,1},{1,0},{2,3},{3,2},{4,5},{5,4},{6,7},{7,6},{8,9},{9,8},{10,11... | collective-permute-start | bytes 3145736 | tf_op jit(solution)/shard_map/ppermute | solution.py:532
  17.3 8.6 %collective-permute-start.1 = (bf16[12,256,256]{2,1,0:T(8,128)(2,1)}, bf16[12,256,256]{2,1,0:T(8,128)(2,1)S(1)}, u32[]{:S(2)}, u32[]{:S(2)}) collective-permute-start(bf16[12,256,256]{2,1,0:T(8,128)(2,1)} %get-tuple-element.32), channel_id=1, source_target_pairs={{0,1},{1,0},{2,3},{3,2},{4,5},{5,4},{6,7},{7,6},{8,9},{9,8},{10,11... | collective-permute-start | bytes 4718600 | tf_op jit(solution)/shard_map/ppermute | solution.py:532
  17.8 14.1 %collective-permute-start.2 = (bf16[12,256,256]{2,1,0:T(8,128)(2,1)}, bf16[12,256,256]{2,1,0:T(8,128)(2,1)}, u32[]{:S(2)}, u32[]{:S(2)}) collective-permute-start(bf16[12,256,256]{2,1,0:T(8,128)(2,1)} %get-tuple-element.33), channel_id=1, source_target_pairs={{0,1},{1,0},{2,3},{3,2},{4,5},{5,4},{6,7},{7,6},{8,9},{9,8},{10,11... | collective-permute-start | bytes 4718600 | tf_op jit(solution)/shard_map/ppermute | solution.py:532
  18.7 18.0 %collective-permute-start.6 = (bf16[4,4,2,32,128]{4,3,2,1,0:T(8,128)(2,1)S(1)}, bf16[4,4,2,32,128]{4,3,2,1,0:T(8,128)(2,1)S(1)}, u32[]{:S(2)}, u32[]{:S(2)}) collective-permute-start(bf16[4,4,2,32,128]{4,3,2,1,0:T(8,128)(2,1)S(1)} %get-tuple-element.35), channel_id=1, source_target_pairs={{0,1},{1,0},{2,3},{3,2},{4,5},{5,4},{6,7},{7,6},{8,9},{9,8},{10,11... | collective-permute-start | bytes 786440 | tf_op jit(solution)/shard_map/ppermute | solution.py:532
  23.3 17.1 %collective-permute-start.5 = (bf16[24,4224]{1,0:T(8,128)(2,1)S(1)}, bf16[24,4224]{1,0:T(8,128)(2,1)S(1)}, u32[]{:S(2)}, u32[]{:S(2)}) collective-permute-start(bf16[24,4224]{1,0:T(8,128)(2,1)S(1)} %score_rows.3), channel_id=1, source_target_pairs={{0,64},{32,96},{1,65},{33,97},{2,66},{34,98},{3,67},{35,99},{4,68}... | collective-permute-start | bytes 608264 | tf_op jit(solution)/shard_map/ppermute | solution.py:564
  25.9 1.1 %copy-start.6 = (bf16[12,256,256]{2,1,0:T(8,128)(2,1)}, bf16[12,256,256]{2,1,0:T(8,128)(2,1)S(1)}, u32[]{:S(2)}) copy-start(bf16[12,256,256]{2,1,0:T(8,128)(2,1)S(1)} %collective-permute-done.1.swapped.refs_1_) | copy-start | bytes 4718596
  30.6 18.1 %collective-permute-start.4 = (bf16[24,6272]{1,0:T(8,128)(2,1)S(1)}, bf16[24,6272]{1,0:T(8,128)(2,1)S(1)}, u32[]{:S(2)}, u32[]{:S(2)}) collective-permute-start(bf16[24,6272]{1,0:T(8,128)(2,1)S(1)} %score_rows.4), channel_id=1, source_target_pairs={{0,64},{32,96},{1,65},{33,97},{2,66},{34,98},{3,67},{35,99},{4,68}... | collective-permute-start | bytes 903176 | tf_op jit(solution)/shard_map/ppermute | solution.py:564
  35.4 14.3 %collective-permute-start.3 = (bf16[24,6272]{1,0:T(8,128)(2,1)S(1)}, bf16[24,6272]{1,0:T(8,128)(2,1)S(1)}, u32[]{:S(2)}, u32[]{:S(2)}) collective-permute-start(bf16[24,6272]{1,0:T(8,128)(2,1)S(1)} %score_rows.5), channel_id=1, source_target_pairs={{0,64},{32,96},{1,65},{33,97},{2,66},{34,98},{3,67},{35,99},{4,68}... | collective-permute-start | bytes 903176 | tf_op jit(solution)/shard_map/ppermute | solution.py:564
  36.8 6.1 %collective-permute-start.7 = (bf16[2,4,2,32,128]{4,3,2,1,0:T(8,128)(2,1)S(1)}, bf16[2,4,2,32,128]{4,3,2,1,0:T(8,128)(2,1)S(1)}, u32[]{:S(2)}, u32[]{:S(2)}) collective-permute-start(bf16[2,4,2,32,128]{4,3,2,1,0:T(8,128)(2,1)S(1)} %get-tuple-element.46), channel_id=1, source_target_pairs={{0,2},{1,3},{2,0},{3,1},{4,6},{5,7},{6,4},{7,5},{8,10},{9,11},{10,... | collective-permute-start | bytes 393224 | tf_op jit(solution)/shard_map/ppermute | solution.py:532
  37.7 8.8 %collective-permute-start.8 = (bf16[2,4,2,32,128]{4,3,2,1,0:T(8,128)(2,1)S(1)}, bf16[2,4,2,32,128]{4,3,2,1,0:T(8,128)(2,1)S(1)}, u32[]{:S(2)}, u32[]{:S(2)}) collective-permute-start(bf16[2,4,2,32,128]{4,3,2,1,0:T(8,128)(2,1)S(1)} %get-tuple-element.47), channel_id=1, source_target_pairs={{0,4},{1,5},{2,6},{3,7},{4,0},{5,1},{6,2},{7,3},{8,12},{9,13},{10,... | collective-permute-start | bytes 393224 | tf_op jit(solution)/shard_map/ppermute | solution.py:532
  40.4 8.2 %collective-permute-start.9 = (bf16[2,4,2,32,128]{4,3,2,1,0:T(8,128)(2,1)S(1)}, bf16[2,4,2,32,128]{4,3,2,1,0:T(8,128)(2,1)S(1)}, u32[]{:S(2)}, u32[]{:S(2)}) collective-permute-start(bf16[2,4,2,32,128]{4,3,2,1,0:T(8,128)(2,1)S(1)} %get-tuple-element.48), channel_id=1, source_target_pairs={{0,6},{1,7},{2,4},{3,5},{4,2},{5,3},{6,0},{7,1},{8,14},{9,15},{10,... | collective-permute-start | bytes 393224 | tf_op jit(solution)/shard_map/ppermute | solution.py:532
  49.7 10.4 %copy-start.9 = (f32[2,3,8]{2,0,1:T(2,128)S(1)}, f32[2,3,8]{2,0,1:T(2,128)}, u32[]{:S(2)}) copy-start(f32[2,3,8]{2,0,1:T(2,128)} %param.23) | copy-start | bytes 580
  49.7 10.4 %copy-start.10 = (f32[2,3,8]{2,0,1:T(2,128)S(1)}, f32[2,3,8]{2,0,1:T(2,128)}, u32[]{:S(2)}) copy-start(f32[2,3,8]{2,0,1:T(2,128)} %param.24) | copy-start | bytes 580
  50.5 19.0 %copy-start.2 = (bf16[2,3,8,128]{3,2,1,0:T(8,128)(2,1)S(1)}, bf16[2,3,8,128]{3,2,1,0:T(8,128)(2,1)}, u32[]{:S(2)}) copy-start(bf16[2,3,8,128]{3,2,1,0:T(8,128)(2,1)} %value.1) | copy-start | bytes 36868
  50.5 19.0 %copy-start.3 = (bf16[2,3,8,128]{3,2,1,0:T(8,128)(2,1)S(1)}, bf16[2,3,8,128]{3,2,1,0:T(8,128)(2,1)}, u32[]{:S(2)}) copy-start(bf16[2,3,8,128]{3,2,1,0:T(8,128)(2,1)} %gate.1) | copy-start | bytes 36868
  50.6 19.0 %copy-start.4 = (bf16[2,3,4,128]{3,2,1,0:T(4,128)(2,1)S(1)}, bf16[2,3,4,128]{3,2,1,0:T(4,128)(2,1)}, u32[]{:S(2)}) copy-start(bf16[2,3,4,128]{3,2,1,0:T(4,128)(2,1)} %query.2) | copy-start | bytes 18436
  50.6 19.0 %copy-start.5 = (bf16[2,3,4,128]{3,2,1,0:T(4,128)(2,1)S(1)}, bf16[2,3,4,128]{3,2,1,0:T(4,128)(2,1)}, u32[]{:S(2)}) copy-start(bf16[2,3,4,128]{3,2,1,0:T(4,128)(2,1)} %key.1) | copy-start | bytes 18436
  50.6 22.2 %copy-start.7 = (bf16[2,3,1024]{2,0,1:T(2,128)(2,1)S(1)}, bf16[2,3,1024]{2,0,1:T(2,128)(2,1)}, u32[]{:S(2)}) copy-start(bf16[2,3,1024]{2,0,1:T(2,128)(2,1)} %param.18) | copy-start | bytes 36868
  50.6 22.2 %all-to-all-start.1 = ((bf16[16,112,128]{2,1,0:T(8,128)(2,1)}), bf16[16,112,128]{2,1,0:T(8,128)(2,1)S(1)}, u32[]{:S(2)}, u32[]{:S(2)}) async-start(bf16[16,112,128]{2,1,0:T(8,128)(2,1)} %mix_rows.5), calls=%async_computation.1 | async-start | bytes 917504 | tf_op jit(solution)/shard_map/all_to_all | solution.py:540
  55.3 17.5 %copy-start.1 = (bf16[2,3,16,256]{3,2,1,0:T(8,128)(2,1)S(1)}, bf16[2,3,16,256]{3,2,1,0:T(8,128)(2,1)}, u32[]{:S(2)}) copy-start(bf16[2,3,16,256]{3,2,1,0:T(8,128)(2,1)} %query.3) | copy-start | bytes 147460
  55.3 11.1 %collective-permute-start.10 = (bf16[4,2,2,32,128]{4,3,2,1,0:T(8,128)(2,1)S(1)}, bf16[4,2,2,32,128]{4,3,2,1,0:T(8,128)(2,1)S(1)}, u32[]{:S(2)}, u32[]{:S(2)}) collective-permute-start(bf16[4,2,2,32,128]{4,3,2,1,0:T(8,128)(2,1)S(1)} %get-tuple-element.50), channel_id=1, source_target_pairs={{0,8},{1,9},{2,10},{3,11},{4,12},{5,13},{6,14},{7,15},{8,0},{9,1},... | collective-permute-start | bytes 393224 | tf_op jit(solution)/shard_map/ppermute | solution.py:532
  57.3 12.0 %collective-permute-start.11 = (bf16[4,2,2,32,128]{4,3,2,1,0:T(8,128)(2,1)S(1)}, bf16[4,2,2,32,128]{4,3,2,1,0:T(8,128)(2,1)S(1)}, u32[]{:S(2)}, u32[]{:S(2)}) collective-permute-start(bf16[4,2,2,32,128]{4,3,2,1,0:T(8,128)(2,1)S(1)} %get-tuple-element.51), channel_id=1, source_target_pairs={{0,16},{1,17},{2,18},{3,19},{4,20},{5,21},{6,22},{7,23},{8,24},{9,... | collective-permute-start | bytes 393224 | tf_op jit(solution)/shard_map/ppermute | solution.py:532
  60.0 9.3 %collective-permute-start.12 = (bf16[4,2,2,32,128]{4,3,2,1,0:T(8,128)(2,1)S(1)}, bf16[4,2,2,32,128]{4,3,2,1,0:T(8,128)(2,1)S(1)}, u32[]{:S(2)}, u32[]{:S(2)}) collective-permute-start(bf16[4,2,2,32,128]{4,3,2,1,0:T(8,128)(2,1)S(1)} %get-tuple-element.52), channel_id=1, source_target_pairs={{0,24},{1,25},{2,26},{3,27},{4,28},{5,29},{6,30},{7,31},{8,16},{9,... | collective-permute-start | bytes 393224 | tf_op jit(solution)/shard_map/ppermute | solution.py:532
  60.1 19.9 %copy-start.8 = (bf16[2,3,1024]{2,0,1:T(2,128)(2,1)S(1)}, bf16[2,3,1024]{2,0,1:T(2,128)(2,1)}, u32[]{:S(2)}) copy-start(bf16[2,3,1024]{2,0,1:T(2,128)(2,1)} %param.19) | copy-start | bytes 36868
  72.8 7.2 %collective-permute-start.14 = (f32[3,2,1024]{2,1,0:T(2,128)S(1)}, f32[3,2,1024]{2,1,0:T(2,128)S(1)}, u32[]{:S(2)}, u32[]{:S(2)}) collective-permute-start(f32[3,2,1024]{2,1,0:T(2,128)S(1)} %get-tuple-element.57), channel_id=1, source_target_pairs={{64,0},{96,64},{65,1},{97,65},{66,2},{98,66},{67,3},{99,67},{68,4}... | collective-permute-start | bytes 73736 | tf_op jit(solution)/shard_map/ppermute | solution.py:585
  74.1 5.9 %collective-permute-start.13 = (f32[3,2,1024]{2,1,0:T(2,128)S(1)}, f32[3,2,1024]{2,1,0:T(2,128)S(1)}, u32[]{:S(2)}, u32[]{:S(2)}) collective-permute-start(f32[3,2,1024]{2,1,0:T(2,128)S(1)} %get-tuple-element.56), channel_id=1, source_target_pairs={{64,32},{65,33},{66,34},{67,35},{68,36},{69,37},{70,38},{71,39},{7... | collective-permute-start | bytes 73736 | tf_op jit(solution)/shard_map/ppermute | solution.py:586

commit v5 on v4

--- a/solution.py
+++ b/solution.py
@@ -42,18 +42,13 @@
     return order[4 * (slot // 2) + 2 * core + slot % 2]
 
 
-def gather_kernel(order, cache, *refs, chunks):
-    outs, (held, arrived, left) = refs[:-3], refs[-3:]
-    reads, writes = [], []
-    for chunk, out in zip(chunks, outs):
-        for n in range(SIZES[chunk]):
-            at = len(reads)
-            reads.append(
-                pltpu.make_async_copy(
-                    cache.at[prefill_row(order, FIRSTS[chunk] + n, 1)], held.at[at], arrived.at[at]
-                )
-            )
-            writes.append(pltpu.make_async_copy(held.at[at], out.at[n], left.at[at]))
+def gather_kernel(order, cache, out, held, arrived, left, *, first):
+    count = out.shape[0]
+    reads = [
+        pltpu.make_async_copy(cache.at[prefill_row(order, first + n, 1)], held.at[n], arrived.at[n])
+        for n in range(count)
+    ]
+    writes = [pltpu.make_async_copy(held.at[n], out.at[n], left.at[n]) for n in range(count)]
     for read in reads:
         read.start()
     for read, write in zip(reads, writes):
@@ -63,52 +58,57 @@
         write.wait()
 
 
-def gather_rows(order, cache, chunks):
-    count = sum(SIZES[chunk] for chunk in chunks)
+def gather_rows(order, cache, first, count):
     copies = pltpu.SemaphoreType.DMA((count,))
     return pl.pallas_call(
-        functools.partial(gather_kernel, chunks=chunks),
+        functools.partial(gather_kernel, first=first),
         name="gather_rows",
-        out_shape=[pltpu.HBM((SIZES[c], *cache.shape[1:]), cache.dtype) for c in chunks],
+        out_shape=pltpu.HBM((count, *cache.shape[1:]), cache.dtype),
         in_specs=[SMEM, ANY],
-        out_specs=[ANY] * len(chunks),
+        out_specs=ANY,
         scratch_shapes=[held_rows(cache, count), copies, copies],
         compiler_params=PARAMS,
         cost_estimate=FREE,
     )(far(order), far(cache))
 
 
-def hold_kernel(array, out):
+def hold_kernel(*refs):
     pass
 
 
-def hold(array, cost):
+def hold(arrays, cost):
+    count = len(arrays)
     return pl.pallas_call(
         hold_kernel,
         name="hold",
-        out_shape=pltpu.VMEM(array.shape, array.dtype),
-        in_specs=[VMEM],
-        out_specs=VMEM,
-        input_output_aliases={0: 0},
+        out_shape=[pltpu.VMEM(array.shape, array.dtype) for array in arrays],
+        in_specs=[VMEM] * count,
+        out_specs=[VMEM] * count,
+        input_output_aliases={n: n for n in range(count)},
         compiler_params=PARAMS,
         cost_estimate=pl.CostEstimate(flops=cost, bytes_accessed=0, transcendentals=0),
-    )(near(array))
+    )(*[near(array) for array in arrays])
 
 
 def fetches(order, cache, swapped, own, other, arrived, chunk):
     groups, first = {}, 0
+    base = FIRSTS[chunk] - FIRSTS[1]
     for at, size in enumerate(GROUPS[chunk]):
-        span = pl.ds(first, size)
         copies = [
-            pltpu.make_async_copy(
-                swapped.at[span], other.at[span], arrived.at[SIZES[chunk] + at]
-            )
-        ] + [
             pltpu.make_async_copy(
                 cache.at[prefill_row(order, FIRSTS[chunk] + n)], own.at[n], arrived.at[n]
             )
             for n in range(first, first + size)
         ]
+        if chunk:
+            copies.insert(
+                0,
+                pltpu.make_async_copy(
+                    swapped.at[pl.ds(base + first, size)],
+                    other.at[pl.ds(first, size)],
+                    arrived.at[SIZES[chunk] + at],
+                ),
+            )
         groups[first] = copies
         first += size
     return groups
@@ -134,6 +134,8 @@
 
 
 def score_kernel(order, lengths, query, cache, swapped, out, own, other, arrived, *, chunk):
+    if not chunk:
+        other = swapped
     size = SIZES[chunk]
     span = own.shape[1]
     width = 2 * span
@@ -179,12 +181,12 @@
         functools.partial(score_kernel, chunk=chunk),
         name="score_rows",
         out_shape=pltpu.VMEM((QROWS, size * 2 * cache.shape[1] + LANES), jnp.bfloat16),
-        in_specs=[SMEM, SMEM, VMEM, ANY, ANY],
+        in_specs=[SMEM, SMEM, VMEM, ANY, ANY if chunk else VMEM],
         out_specs=VMEM,
         scratch_shapes=[rows, rows, arrivals(chunk)],
         compiler_params=PARAMS,
         cost_estimate=FREE,
-    )(far(order), far(lengths), near(query), far(cache), far(swapped))
+    )(far(order), far(lengths), near(query), far(cache), (far if chunk else near)(swapped))
 
 
 LINES = 2 * QROWS
@@ -203,8 +205,9 @@
         cache, swapped, swapped_last = refs[:3]
         out, own_last, other_last, own, other, arrived, arrived_last = refs[-9:-2]
     else:
-        cache, swapped = refs[:2]
-        out, own, other, arrived = refs[-6:-2]
+        cache, other = refs[:2]
+        swapped = None
+        out, own, _, arrived = refs[-6:-2]
     size = SIZES[chunk]
     span = own.shape[1]
     width = 2 * span
@@ -262,8 +265,10 @@
         in_specs = [SMEM, VMEM, VMEM, VMEM]
         operands = [far(order), near(weights), near(rows[0]), near(rows[1])]
     else:
-        in_specs = [SMEM, VMEM, ANY, ANY]
-        operands = [far(order), near(weights), far(cache), far(swapped[chunk])]
+        in_specs = [SMEM, VMEM, ANY, ANY if chunk else VMEM]
+        operands = [
+            far(order), near(weights), far(cache), (far if chunk else near)(swapped[chunk])
+        ]
     if fetch_last:
         in_specs.append(ANY)
         operands.append(far(swapped[chunk + 1]))
@@ -470,21 +475,27 @@
             rows[at : at + heads_k] = q
             rows[keys_at + at : keys_at + at + heads_k] = k
     columns = jnp.transpose(rows[...])
+    shape = (width, value.shape[3])
     for row in range(batch):
         made = [[] for _ in range(steps)]
         values = [value[row, step].astype(jnp.float32) for step in range(steps)]
-        for head in range(heads_v):
-            state = states[row, head].astype(jnp.float32)
+        for head in range(heads_k):
+            both = range(head * ratio, (head + 1) * ratio)
+            held = [states[row, one].astype(jnp.float32) for one in both]
             for step in range(steps):
-                at = column(row, step, head // ratio)
-                q = columns[:, at : at + 1]
-                k = columns[:, keys_at + at : keys_at + at + 1]
-                rate = decay[row, step, head]
-                recalled = jnp.sum(k * state, axis=0, keepdims=True)
-                change = beta[row, step, head] * (values[step][head : head + 1] - rate * recalled)
-                state = rate * state + k * change
-                made[step].append(jnp.sum(q * state, axis=0, keepdims=True))
-            final[row, head] = state
+                at = column(row, step, head)
+                q = jnp.broadcast_to(columns[:, at : at + 1], shape)
+                k = jnp.broadcast_to(columns[:, keys_at + at : keys_at + at + 1], shape)
+                for n, one in enumerate(both):
+                    rate = decay[row, step, one]
+                    recalled = jnp.sum(k * held[n], axis=0, keepdims=True)
+                    change = beta[row, step, one] * (
+                        values[step][one : one + 1] - rate * recalled
+                    )
+                    held[n] = rate * held[n] + k * change
+                    made[step].append(jnp.sum(q * held[n], axis=0, keepdims=True))
+            for n, one in enumerate(both):
+                final[row, one] = held[n]
         for step in range(steps):
             read = jnp.concatenate(made[step], axis=0)
             read = read * lax.rsqrt(jnp.mean(read * read, -1, keepdims=True) + 1e-06)
@@ -544,16 +555,17 @@
         for side in (att_query[:, :, :GROUP], att_query[:, :, GROUP:])
     ]
     copies = jnp.where(head_index % KVH == 1, sides[1], sides[0])
-    query = hold(between_chips(copies.reshape(2 * chips, QROWS, HD)), 30 * 10**9)
-
-    made = gather_rows(row_order, kv_cache, (0,))
-    made += gather_rows(after(row_order, *made), kv_cache, tuple(range(1, CHUNKS)))
+    (query,) = hold([between_chips(copies.reshape(2 * chips, QROWS, HD))], 30 * 10**9)
+
+    first = gather_rows(row_order, kv_cache, 0, FIRSTS[1])
+    made = [first, gather_rows(after(row_order, first), kv_cache, FIRSTS[1], SLOTS - FIRSTS[1])]
     rows_all, heads, depth, width = lin_states.shape
     mine, theirs = split_states(
         after(row_order, *made), lin_states.reshape(rows_all, heads * depth, width)
     )
-    swapped = [across(part) for part in made]
-    other = across(theirs)
+    query, first = hold([query, across(made[0])], 30 * 10**9)
+    swapped = [first] + [across(made[1])] * (CHUNKS - 1)
+    (other,) = hold([across(theirs)], 30 * 10**9)
 
     weights = []
     for chunk in range(CHUNKS):
@@ -564,24 +576,25 @@
     moved = [lax.ppermute(made, "head", [(0, 2), (1, 3)]) for made in weights]
 
     blocks = along_z(after(mine, weights[-1]), other)
-    blocks = [blocks[0]] + [across(block, 2 * z) for z, block in enumerate(blocks[1:], 1)]
-    blocks = along_y(blocks)
-
+    crossed = [across(block, 2 * z) for z, block in enumerate(blocks[1:], 1)]
+    blocks = [blocks[0], *hold(crossed, 10 * 10**9)]
     payload, rows = None, None
     for chunk in range(CHUNKS):
-        cost = 10 * 10**9 if chunk + 1 == CHUNKS else 10**8
+        cost = 10 * 10**9 if chunk + 1 == CHUNKS else 3 * 10**9
         payload, rows = mix_rows(
             after(row_order, weights[-1]), moved[chunk], kv_cache, swapped, chunk, payload, rows,
             cost,
         )
-    parts = between_chips(after(payload, *blocks))
+    parts = between_chips(payload)
+    blocks = along_y([after(blocks[0], payload), *blocks[1:]])
     blocks = [blocks[0]] + [across(block, 8 * y) for y, block in enumerate(blocks[1:], 1)]
-    states = join_states(blocks).reshape(wide_count, 2, heads, depth, width)
+    low, high = combine(parts, att_query, new_kv)
+    states = join_states([after(blocks[0], low), *blocks[1:]])
+    states = states.reshape(wide_count, 2, heads, depth, width)
     states = states.transpose(1, 2, 0, 3, 4).reshape(2, heads, wide_count * depth, width)
     lin_out, final_states = delta_rule(
         states, lin_query, lin_key, lin_value, lin_decay, lin_beta, lin_gate
     )
-    low, high = combine(parts, att_query, after(new_kv, lin_out))
     low_here = lax.ppermute(low, "head", [(2, 0), (3, 2)])
     high_here = lax.ppermute(high, "head", [(2, 1)])
     result = jnp.where(

time: 81.4 us -> 73.9 us (0.908)
  waiting for transfers between devices: 21.8 us -> 13.4 us
  starting transfers between devices: 30.6 us -> 33 us
  local copies, waits for them, and re-layouts: 2.23 us -> 1.1 us
    ppermute x10 -> x9, waiting for transfers between devices: 15.5 us -> 0.97 us  [across(): return lax.ppermute(array, 'wide', pairs)]
    all_to_all x2, waiting for transfers between devices: 1.03 us -> 7.48 us  [between_chips(): lax.all_to_all(array, 'wide', 0, 0, tiled=True, axis_index_groups=same_core)]
    all_to_all x2, starting transfers between devices: 12.8 us -> 15.4 us  [between_chips(): lax.all_to_all(array, 'wide', 0, 0, tiled=True, axis_index_groups=same_core)]
    unnamed x24 -> x23, local copies, waits for them, and re-layouts: 1.2 us -> 0.08 us
    ppermute x10 -> x9, starting transfers between devices: 10.7 us -> 10.3 us  [across(): return lax.ppermute(array, 'wide', pairs)]
    pallas_call x3 -> x6, Pallas kernels: 6.88 us -> 6.85 us  [the longest x2 6.84 us: gather_rows(): pl.pallas_call(functools.partial(gather_kernel, first=first), name='gathe...]
  transfers between devices with their start and end apart: 17 -> 16, of which waited for: 7 -> 5; matrix products, arithmetic and copies ran while one was open for 0% -> 0% of each run, Pallas kernels for 28% -> 32%
where the time goes in v5:
time: 73.9 us; the launch traced here: 73.2 us
  starting transfers between devices  33 us (45%)
  Pallas kernels  23.2 us (31%)
  waiting for transfers between devices  13.4 us (18%)
  other arithmetic  1.41 us (2%)
  local copies, waits for them, and re-layouts  1.1 us (1%)
  between operations  1.05 us (1%)
    all_to_all x2, starting transfers between devices, between_chips(): lax.all_to_all(array, 'wide', 0, 0, tiled=True, axis_index_groups=same_core)  15.4 us
    ppermute x9, starting transfers between devices, across(): return lax.ppermute(array, 'wide', pairs)  10.3 us
    pallas_call x3, Pallas kernels, score_rows(): pl.pallas_call(functools.partial(score_kernel, chunk=chunk), name='score_...  9.98 us
    all_to_all x2, waiting for transfers between devices, between_chips(): lax.all_to_all(array, 'wide', 0, 0, tiled=True, axis_index_groups=same_core)  7.48 us
    pallas_call x2, Pallas kernels, gather_rows(): pl.pallas_call(functools.partial(gather_kernel, first=first), name='gathe...  6.84 us
    ppermute x3, starting transfers between devices, on_device(): moved = [lax.ppermute(made, 'head', [(0, 2), (1, 3)]) for made in weights]  5.38 us
    ppermute x1, waiting for transfers between devices, on_device(): low_here = lax.ppermute(low, 'head', [(2, 0), (3, 2)])  4.49 us
    pallas_call x1, Pallas kernels, delta_rule(): pl.pallas_call(delta_kernel, name='delta_rule', out_shape=(jax.ShapeDtype...  3.14 us
  transfers between devices with their start and end apart: 16, of which 5 were waited for; matrix products, arithmetic and copies ran while one was open for 0% of the time, Pallas kernels for 32%

profile of v5, /device:TPU:0, one launch (start us, length us, event | category | flops | bytes accessed | tf_op | source)
XLA Modules:
  0.0 73.2 jit_solution(4243567746343340866)
XLA Ops:
  0.6 0.8 %select_bitcast_fusion = bf16[2,24,256]{2,1,0:T(8,128)(2,1)S(1)} fusion(bf16[2,3,16,256]{3,2,1,0:T(8,128)(2,1)} %query.2, pred[]{:T(512)S(6)} %eq.12), kind=kLoop, calls=%fused_computation.2 | loop fusion | flops 12288 | bytes 73729 | tf_op jit(solution)/shard_map/jit(_where)/select_n | solution.py:557
  1.4 0.8 %broadcast_in_dim.2 = bf16[16,2,24,256]{3,2,1,0:T(8,128)(2,1)} broadcast(bf16[2,24,256]{2,1,0:T(8,128)(2,1)S(1)} %select_bitcast_fusion), dimensions={1,2,3} | broadcast | bytes 417792 | tf_op jit(solution)/shard_map/broadcast_in_dim | solution.py:554
  2.2 8.1 %all-to-all-start = ((bf16[32,24,256]{2,1,0:T(8,128)(2,1)}), bf16[32,24,256]{2,1,0:T(8,128)(2,1)S(1)}, u32[]{:S(2)}, u32[]{:S(2)}) async-start(bf16[32,24,256]{2,1,0:T(8,128)(2,1)} %bitcast.2), calls=%async_computation | async-start | bytes 786432 | tf_op jit(solution)/shard_map/all_to_all | solution.py:551
  10.3 2.8 %gather_rows.2 = bf16[8,256,256]{2,1,0:T(8,128)(2,1)} custom-call(s32[64]{0:T(128)} %order.9, bf16[64,256,256]{2,1,0:T(8,128)(2,1)} %refs_0_.3), custom_call_target="tpu_custom_call" | custom-call | tf_op jit(solution)/shard_map/gather_rows/pallas_call | solution.py:63
  13.1 0.0 copy-start
  13.1 0.1 collective-permute-start
  13.2 4.1 %gather_rows.3 = bf16[24,256,256]{2,1,0:T(8,128)(2,1)} custom-call(s32[64]{0:T(128)} %order.9, bf16[64,256,256]{2,1,0:T(8,128)(2,1)} %refs_0_.3), custom_call_target="tpu_custom_call" | custom-call | tf_op jit(solution)/shard_map/gather_rows/pallas_call | solution.py:63
  17.3 0.4 collective-permute-start.1
  17.7 0.8 %split_states.1 = (bf16[4,4,2,32,128]{4,3,2,1,0:T(8,128)(2,1)S(1)}, bf16[4,4,2,32,128]{4,3,2,1,0:T(8,128)(2,1)S(1)}) custom-call(s32[64]{0:T(128)} %order.9, f32[64,32,128]{2,1,0:T(8,128)S(1)} %bitcast.18), custom_call_target="tpu_custom_call" | custom-call | tf_op jit(solution)/shard_map/split_states/pallas_call | solution.py:411
  18.5 0.2 collective-permute-start.7
  18.7 1.4 %all-to-all-done.refs_0_ = bf16[32,24,256]{2,1,0:T(8,128)(2,1)S(1)} async-done(((bf16[32,24,256]{2,1,0:T(8,128)(2,1)}), bf16[32,24,256]{2,1,0:T(8,128)(2,1)S(1)}, u32[]{:S(2)}, u32[]{:S(2)}) %all-to-all-start) | async-done | bytes 393248 | tf_op jit(solution)/shard_map/all_to_all | solution.py:551
  20.2 0.0 collective-permute-done.refs_1_
  20.2 2.9 %score_rows.3 = bf16[24,4224]{1,0:T(8,128)(2,1)S(1)} custom-call(s32[64]{0:T(128)} %order.9, s32[64]{0:T(128)} %lengths.5, bf16[32,24,256]{2,1,0:T(8,128)(2,1)S(1)} %get-tuple-element.38.query, bf16[64,256,256]{2,1,0:T(8,128)(2,1)} %refs_0_.3, bf16[8,256,256]{2,1,0:T(8,128)(2,1)S(1)} %get-tuple-element.39.swapped.refs_1_), custom_call_target="tpu_custom_call" | custom-call | tf_op jit(solution)/shard_map/score_rows/pallas_call | solution.py:180
  23.1 2.8 %collective-permute-start.4 = (bf16[24,4224]{1,0:T(8,128)(2,1)S(1)}, bf16[24,4224]{1,0:T(8,128)(2,1)S(1)}, u32[]{:S(2)}, u32[]{:S(2)}) collective-permute-start(bf16[24,4224]{1,0:T(8,128)(2,1)S(1)} %score_rows.3), channel_id=1, source_target_pairs={{0,64},{32,96},{1,65},{33,97},{2,66},{34,98},{3,67},{35,99},{4,68}... | collective-permute-start | bytes 608264 | tf_op jit(solution)/shard_map/ppermute | solution.py:576
  25.9 3.5 %score_rows.4 = bf16[24,6272]{1,0:T(8,128)(2,1)S(1)} custom-call(s32[64]{0:T(128)} %order.9, s32[64]{0:T(128)} %lengths.5, bf16[32,24,256]{2,1,0:T(8,128)(2,1)S(1)} %get-tuple-element.38.query, bf16[64,256,256]{2,1,0:T(8,128)(2,1)} %refs_0_.3, bf16[24,256,256]{2,1,0:T(8,128)(2,1)} %collective-permute-done.1.swapped.refs_1_.refs_2_), custom_call_target="tpu_custom_call" | custom-call | tf_op jit(solution)/shard_map/score_rows/pallas_call | solution.py:180
  29.4 1.3 %collective-permute-start.3 = (bf16[24,6272]{1,0:T(8,128)(2,1)S(1)}, bf16[24,6272]{1,0:T(8,128)(2,1)S(1)}, u32[]{:S(2)}, u32[]{:S(2)}) collective-permute-start(bf16[24,6272]{1,0:T(8,128)(2,1)S(1)} %score_rows.4), channel_id=1, source_target_pairs={{0,64},{32,96},{1,65},{33,97},{2,66},{34,98},{3,67},{35,99},{4,68}... | collective-permute-start | bytes 903176 | tf_op jit(solution)/shard_map/ppermute | solution.py:576
  30.8 3.5 %score_rows.5 = bf16[24,6272]{1,0:T(8,128)(2,1)S(1)} custom-call(s32[64]{0:T(128)} %order.9, s32[64]{0:T(128)} %lengths.5, bf16[32,24,256]{2,1,0:T(8,128)(2,1)S(1)} %get-tuple-element.38.query, bf16[64,256,256]{2,1,0:T(8,128)(2,1)} %refs_0_.3, bf16[24,256,256]{2,1,0:T(8,128)(2,1)} %collective-permute-done.1.swapped.refs_1_.refs_2_), custom_call_target="tpu_custom_call" | custom-call | tf_op jit(solution)/shard_map/score_rows/pallas_call | solution.py:180
  34.3 1.3 %collective-permute-start.2 = (bf16[24,6272]{1,0:T(8,128)(2,1)S(1)}, bf16[24,6272]{1,0:T(8,128)(2,1)S(1)}, u32[]{:S(2)}, u32[]{:S(2)}) collective-permute-start(bf16[24,6272]{1,0:T(8,128)(2,1)S(1)} %score_rows.5), channel_id=1, source_target_pairs={{0,64},{32,96},{1,65},{33,97},{2,66},{34,98},{3,67},{35,99},{4,68}... | collective-permute-start | bytes 903176 | tf_op jit(solution)/shard_map/ppermute | solution.py:576
  35.6 1.8 %collective-permute-start.10 = (bf16[2,4,2,32,128]{4,3,2,1,0:T(8,128)(2,1)S(1)}, bf16[2,4,2,32,128]{4,3,2,1,0:T(8,128)(2,1)S(1)}, u32[]{:S(2)}, u32[]{:S(2)}) collective-permute-start(bf16[2,4,2,32,128]{4,3,2,1,0:T(8,128)(2,1)S(1)} %get-tuple-element.54), channel_id=1, source_target_pairs={{0,6},{1,7},{2,4},{3,5},{4,2},{5,3},{6,0},{7,1},{8,14},{9,15},{10,... | collective-permute-start | bytes 393224 | tf_op jit(solution)/shard_map/ppermute | solution.py:543
  37.4 0.3 collective-permute-start.8
  37.7 0.0 collective-permute-done.4.weights
  37.7 2.7 %collective-permute-start.9 = (bf16[2,4,2,32,128]{4,3,2,1,0:T(8,128)(2,1)S(1)}, bf16[2,4,2,32,128]{4,3,2,1,0:T(8,128)(2,1)S(1)}, u32[]{:S(2)}, u32[]{:S(2)}) collective-permute-start(bf16[2,4,2,32,128]{4,3,2,1,0:T(8,128)(2,1)S(1)} %get-tuple-element.53), channel_id=1, source_target_pairs={{0,4},{1,5},{2,6},{3,7},{4,0},{5,1},{6,2},{7,3},{8,12},{9,13},{10,... | collective-permute-start | bytes 393224 | tf_op jit(solution)/shard_map/ppermute | solution.py:543
  40.4 0.8 %mix_rows.3.refs_3_ = bf16[16,112,128]{2,1,0:T(8,128)(2,1)} custom-call(s32[64]{0:T(128)} %order.9, bf16[24,4224]{1,0:T(8,128)(2,1)S(1)} %collective-permute-done.4.weights, bf16[64,256,256]{2,1,0:T(8,128)(2,1)} %refs_0_.3, bf16[8,256,256]{2,1,0:T(8,128)(2,1)S(1)} %get-tuple-element.39.swapped.refs_1_), custom_call_target="tpu_custom_call" | custom-call | flops 3000000000 | tf_op jit(solution)/shard_map/mix_rows/pallas_call | solution.py:280
  41.2 0.9 %mix_rows.4 = (bf16[16,112,128]{2,1,0:T(8,128)(2,1)}, bf16[12,256,256]{2,1,0:T(8,128)(2,1)S(1)}, bf16[12,256,256]{2,1,0:T(8,128)(2,1)S(1)}) custom-call(s32[64]{0:T(128)} %order.9, bf16[24,6272]{1,0:T(8,128)(2,1)S(1)} %collective-permute-done.3.weights, bf16[64,256,256]{2,1,0:T(8,128)(2,1)} %refs_0_.3, ...), custom_call_target="tpu_custom_call", output_to_operand_aliasing={{0}: (5, {})} | custom-call | flops 3000000000 | tf_op jit(solution)/shard_map/mix_rows/pallas_call | solution.py:280
  42.2 0.5 collective-permute-done.2.weights
  42.7 0.7 mix_rows.5
  43.3 7.2 %all-to-all-start.1 = ((bf16[16,112,128]{2,1,0:T(8,128)(2,1)}), bf16[16,112,128]{2,1,0:T(8,128)(2,1)S(1)}, u32[]{:S(2)}, u32[]{:S(2)}) async-start(bf16[16,112,128]{2,1,0:T(8,128)(2,1)} %mix_rows.5), calls=%async_computation.1 | async-start | bytes 917504 | tf_op jit(solution)/shard_map/all_to_all | solution.py:551
  50.6 0.0 copy-start.6
  50.6 0.0 copy-start.1
  50.6 0.0 copy-start.8
  50.6 0.0 copy-start.9
  50.6 0.0 collective-permute-done.8.refs_0_
  50.7 0.0 copy-start.2
  50.7 0.0 copy-start.3
  50.7 0.0 copy-start.4
  50.7 0.0 copy-start.5
  50.7 0.0 copy-start.7
  50.8 2.0 %collective-permute-start.11 = (bf16[4,2,2,32,128]{4,3,2,1,0:T(8,128)(2,1)S(1)}, bf16[4,2,2,32,128]{4,3,2,1,0:T(8,128)(2,1)S(1)}, u32[]{:S(2)}, u32[]{:S(2)}) collective-permute-start(bf16[4,2,2,32,128]{4,3,2,1,0:T(8,128)(2,1)S(1)} %get-tuple-element.60), channel_id=1, source_target_pairs={{0,8},{1,9},{2,10},{3,11},{4,12},{5,13},{6,14},{7,15},{8,0},{9,1},... | collective-permute-start | bytes 393224 | tf_op jit(solution)/shard_map/ppermute | solution.py:543
  52.8 2.7 %collective-permute-start.12 = (bf16[4,2,2,32,128]{4,3,2,1,0:T(8,128)(2,1)S(1)}, bf16[4,2,2,32,128]{4,3,2,1,0:T(8,128)(2,1)S(1)}, u32[]{:S(2)}, u32[]{:S(2)}) collective-permute-start(bf16[4,2,2,32,128]{4,3,2,1,0:T(8,128)(2,1)S(1)} %get-tuple-element.61), channel_id=1, source_target_pairs={{0,16},{1,17},{2,18},{3,19},{4,20},{5,21},{6,22},{7,23},{8,24},{9,... | collective-permute-start | bytes 393224 | tf_op jit(solution)/shard_map/ppermute | solution.py:543
  55.5 0.1 collective-permute-start.13
  55.6 6.0 %all-to-all-done.1.parts = bf16[16,112,128]{2,1,0:T(8,128)(2,1)S(1)} async-done(((bf16[16,112,128]{2,1,0:T(8,128)(2,1)}), bf16[16,112,128]{2,1,0:T(8,128)(2,1)S(1)}, u32[]{:S(2)}, u32[]{:S(2)}) %all-to-all-start.1) | async-done | bytes 458784 | tf_op jit(solution)/shard_map/all_to_all | solution.py:551
  61.6 0.7 collective-permute-start.5
  62.3 1.3 %collective-permute-start.6 = (f32[3,2,1024]{2,1,0:T(2,128)S(1)}, f32[3,2,1024]{2,1,0:T(2,128)S(1)}, u32[]{:S(2)}, u32[]{:S(2)}) collective-permute-start(f32[3,2,1024]{2,1,0:T(2,128)S(1)} %get-tuple-element.47), channel_id=1, source_target_pairs={{64,0},{96,64},{65,1},{97,65},{66,2},{98,66},{67,3},{99,67},{68,4}... | collective-permute-start | bytes 73736 | tf_op jit(solution)/shard_map/ppermute | solution.py:598
  63.7 0.9 %collective-permute-done.12.refs_2_ = bf16[4,2,2,32,128]{4,3,2,1,0:T(8,128)(2,1)S(1)} collective-permute-done((bf16[4,2,2,32,128]{4,3,2,1,0:T(8,128)(2,1)S(1)}, bf16[4,2,2,32,128]{4,3,2,1,0:T(8,128)(2,1)S(1)}, u32[]{:S(2)}, u32[]{:S(2)}) %collective-permute-start.12) | collective-permute-done | bytes 131104 | tf_op jit(solution)/shard_map/ppermute | solution.py:543
  64.6 0.2 copy.26
  64.9 3.1 %delta_rule.1 = (bf16[2,3,8,128]{3,2,1,0:T(8,128)(2,1)}, f32[2,8,128,128]{3,2,1,0:T(8,128)}) custom-call(f32[2,3,8]{2,1,0:T(4,128)S(1)} %copy.27.decay, f32[2,3,8]{2,1,0:T(4,128)S(1)} %copy.28.beta, bf16[2,8,128,128]{3,2,1,0:T(8,128)(2,1)S(1)} %bitcast.16, bf16[2,3,4,128]{3,2,1,0:T(4,128)(2,1)S(1)} %copy-done.4, bf16[2,3,4,128]{3,2,1,0:T(4,128)(2,1)S(1)} %copy-done.5, ...), custom_call_target="tpu_custom_call" | custom-call | tf_op jit(solution)/shard_map/delta_rule/pallas_call | solution.py:508
  68.1 4.5 %collective-permute-done.6 = f32[3,2,1024]{2,1,0:T(2,128)S(1)} collective-permute-done((f32[3,2,1024]{2,1,0:T(2,128)S(1)}, f32[3,2,1024]{2,1,0:T(2,128)S(1)}, u32[]{:S(2)}, u32[]{:S(2)}) %collective-permute-start.6) | collective-permute-done | bytes 24608 | tf_op jit(solution)/shard_map/ppermute | solution.py:598
  72.6 0.6 fusion.1
  (29 shorter events, 0.2 us)
Async XLA Ops:
  2.2 18.0 %all-to-all-start = ((bf16[32,24,256]{2,1,0:T(8,128)(2,1)}), bf16[32,24,256]{2,1,0:T(8,128)(2,1)S(1)}, u32[]{:S(2)}, u32[]{:S(2)}) async-start(bf16[32,24,256]{2,1,0:T(8,128)(2,1)} %bitcast.2), calls=%async_computation | async-start | bytes 786432 | tf_op jit(solution)/shard_map/all_to_all | solution.py:551
  13.1 4.6 %copy-start = (f32[64,8,4,128]{3,2,1,0:T(4,128)S(1)}, f32[64,8,4,128]{3,2,1,0:T(4,128)}, u32[]{:S(2)}) copy-start(f32[64,8,4,128]{3,2,1,0:T(4,128)} %param.14) | copy-start | bytes 3145732
  13.1 7.0 %collective-permute-start = (bf16[8,256,256]{2,1,0:T(8,128)(2,1)}, bf16[8,256,256]{2,1,0:T(8,128)(2,1)S(1)}, u32[]{:S(2)}, u32[]{:S(2)}) collective-permute-start(bf16[8,256,256]{2,1,0:T(8,128)(2,1)} %gather_rows.2), channel_id=1, source_target_pairs={{0,1},{1,0},{2,3},{3,2},{4,5},{5,4},{6,7},{7,6},{8,9},{9,8},{10,11... | collective-permute-start | bytes 3145736 | tf_op jit(solution)/shard_map/ppermute | solution.py:543
  17.3 8.6 %collective-permute-start.1 = (bf16[24,256,256]{2,1,0:T(8,128)(2,1)}, bf16[24,256,256]{2,1,0:T(8,128)(2,1)}, u32[]{:S(2)}, u32[]{:S(2)}) collective-permute-start(bf16[24,256,256]{2,1,0:T(8,128)(2,1)} %gather_rows.3), channel_id=1, source_target_pairs={{0,1},{1,0},{2,3},{3,2},{4,5},{5,4},{6,7},{7,6},{8,9},{9,8},{10,11... | collective-permute-start | bytes 9437192 | tf_op jit(solution)/shard_map/ppermute | solution.py:543
  18.5 12.2 %collective-permute-start.7 = (bf16[4,4,2,32,128]{4,3,2,1,0:T(8,128)(2,1)S(1)}, bf16[4,4,2,32,128]{4,3,2,1,0:T(8,128)(2,1)S(1)}, u32[]{:S(2)}, u32[]{:S(2)}) collective-permute-start(bf16[4,4,2,32,128]{4,3,2,1,0:T(8,128)(2,1)S(1)} %get-tuple-element.36), channel_id=1, source_target_pairs={{0,1},{1,0},{2,3},{3,2},{4,5},{5,4},{6,7},{7,6},{8,9},{9,8},{10,11... | collective-permute-start | bytes 786440 | tf_op jit(solution)/shard_map/ppermute | solution.py:543
  23.1 14.6 %collective-permute-start.4 = (bf16[24,4224]{1,0:T(8,128)(2,1)S(1)}, bf16[24,4224]{1,0:T(8,128)(2,1)S(1)}, u32[]{:S(2)}, u32[]{:S(2)}) collective-permute-start(bf16[24,4224]{1,0:T(8,128)(2,1)S(1)} %score_rows.3), channel_id=1, source_target_pairs={{0,64},{32,96},{1,65},{33,97},{2,66},{34,98},{3,67},{35,99},{4,68}... | collective-permute-start | bytes 608264 | tf_op jit(solution)/shard_map/ppermute | solution.py:576
  29.4 11.8 %collective-permute-start.3 = (bf16[24,6272]{1,0:T(8,128)(2,1)S(1)}, bf16[24,6272]{1,0:T(8,128)(2,1)S(1)}, u32[]{:S(2)}, u32[]{:S(2)}) collective-permute-start(bf16[24,6272]{1,0:T(8,128)(2,1)S(1)} %score_rows.4), channel_id=1, source_target_pairs={{0,64},{32,96},{1,65},{33,97},{2,66},{34,98},{3,67},{35,99},{4,68}... | collective-permute-start | bytes 903176 | tf_op jit(solution)/shard_map/ppermute | solution.py:576
  34.3 8.4 %collective-permute-start.2 = (bf16[24,6272]{1,0:T(8,128)(2,1)S(1)}, bf16[24,6272]{1,0:T(8,128)(2,1)S(1)}, u32[]{:S(2)}, u32[]{:S(2)}) collective-permute-start(bf16[24,6272]{1,0:T(8,128)(2,1)S(1)} %score_rows.5), channel_id=1, source_target_pairs={{0,64},{32,96},{1,65},{33,97},{2,66},{34,98},{3,67},{35,99},{4,68}... | collective-permute-start | bytes 903176 | tf_op jit(solution)/shard_map/ppermute | solution.py:576
  35.6 15.0 %collective-permute-start.10 = (bf16[2,4,2,32,128]{4,3,2,1,0:T(8,128)(2,1)S(1)}, bf16[2,4,2,32,128]{4,3,2,1,0:T(8,128)(2,1)S(1)}, u32[]{:S(2)}, u32[]{:S(2)}) collective-permute-start(bf16[2,4,2,32,128]{4,3,2,1,0:T(8,128)(2,1)S(1)} %get-tuple-element.54), channel_id=1, source_target_pairs={{0,6},{1,7},{2,4},{3,5},{4,2},{5,3},{6,0},{7,1},{8,14},{9,15},{10,... | collective-permute-start | bytes 393224 | tf_op jit(solution)/shard_map/ppermute | solution.py:543
  37.4 13.2 %collective-permute-start.8 = (bf16[2,4,2,32,128]{4,3,2,1,0:T(8,128)(2,1)S(1)}, bf16[2,4,2,32,128]{4,3,2,1,0:T(8,128)(2,1)S(1)}, u32[]{:S(2)}, u32[]{:S(2)}) collective-permute-start(bf16[2,4,2,32,128]{4,3,2,1,0:T(8,128)(2,1)S(1)} %get-tuple-element.52), channel_id=1, source_target_pairs={{0,2},{1,3},{2,0},{3,1},{4,6},{5,7},{6,4},{7,5},{8,10},{9,11},{10,... | collective-permute-start | bytes 393224 | tf_op jit(solution)/shard_map/ppermute | solution.py:543
  37.7 13.0 %collective-permute-start.9 = (bf16[2,4,2,32,128]{4,3,2,1,0:T(8,128)(2,1)S(1)}, bf16[2,4,2,32,128]{4,3,2,1,0:T(8,128)(2,1)S(1)}, u32[]{:S(2)}, u32[]{:S(2)}) collective-permute-start(bf16[2,4,2,32,128]{4,3,2,1,0:T(8,128)(2,1)S(1)} %get-tuple-element.53), channel_id=1, source_target_pairs={{0,4},{1,5},{2,6},{3,7},{4,0},{5,1},{6,2},{7,3},{8,12},{9,13},{10,... | collective-permute-start | bytes 393224 | tf_op jit(solution)/shard_map/ppermute | solution.py:543
  43.3 18.3 %all-to-all-start.1 = ((bf16[16,112,128]{2,1,0:T(8,128)(2,1)}), bf16[16,112,128]{2,1,0:T(8,128)(2,1)S(1)}, u32[]{:S(2)}, u32[]{:S(2)}) async-start(bf16[16,112,128]{2,1,0:T(8,128)(2,1)} %mix_rows.5), calls=%async_computation.1 | async-start | bytes 917504 | tf_op jit(solution)/shard_map/all_to_all | solution.py:551
  50.6 5.0 %copy-start.6 = (bf16[2,3,1024]{2,0,1:T(2,128)(2,1)S(1)}, bf16[2,3,1024]{2,0,1:T(2,128)(2,1)}, u32[]{:S(2)}) copy-start(bf16[2,3,1024]{2,0,1:T(2,128)(2,1)} %param.18) | copy-start | bytes 36868
  50.6 11.0 %copy-start.1 = (bf16[2,3,16,256]{3,2,1,0:T(8,128)(2,1)S(1)}, bf16[2,3,16,256]{3,2,1,0:T(8,128)(2,1)}, u32[]{:S(2)}) copy-start(bf16[2,3,16,256]{3,2,1,0:T(8,128)(2,1)} %query.2) | copy-start | bytes 147460
  50.6 13.0 %copy-start.8 = (f32[2,3,8]{2,0,1:T(2,128)S(1)}, f32[2,3,8]{2,0,1:T(2,128)}, u32[]{:S(2)}) copy-start(f32[2,3,8]{2,0,1:T(2,128)} %param.23) | copy-start | bytes 580
  50.6 13.0 %copy-start.9 = (f32[2,3,8]{2,0,1:T(2,128)S(1)}, f32[2,3,8]{2,0,1:T(2,128)}, u32[]{:S(2)}) copy-start(f32[2,3,8]{2,0,1:T(2,128)} %param.24) | copy-start | bytes 580
  50.7 14.2 %copy-start.2 = (bf16[2,3,8,128]{3,2,1,0:T(8,128)(2,1)S(1)}, bf16[2,3,8,128]{3,2,1,0:T(8,128)(2,1)}, u32[]{:S(2)}) copy-start(bf16[2,3,8,128]{3,2,1,0:T(8,128)(2,1)} %value.1) | copy-start | bytes 36868
  50.7 14.2 %copy-start.3 = (bf16[2,3,8,128]{3,2,1,0:T(8,128)(2,1)S(1)}, bf16[2,3,8,128]{3,2,1,0:T(8,128)(2,1)}, u32[]{:S(2)}) copy-start(bf16[2,3,8,128]{3,2,1,0:T(8,128)(2,1)} %gate.1) | copy-start | bytes 36868
  50.7 14.2 %copy-start.4 = (bf16[2,3,4,128]{3,2,1,0:T(4,128)(2,1)S(1)}, bf16[2,3,4,128]{3,2,1,0:T(4,128)(2,1)}, u32[]{:S(2)}) copy-start(bf16[2,3,4,128]{3,2,1,0:T(4,128)(2,1)} %query.3) | copy-start | bytes 18436
  50.7 14.2 %copy-start.5 = (bf16[2,3,4,128]{3,2,1,0:T(4,128)(2,1)S(1)}, bf16[2,3,4,128]{3,2,1,0:T(4,128)(2,1)}, u32[]{:S(2)}) copy-start(bf16[2,3,4,128]{3,2,1,0:T(4,128)(2,1)} %key.1) | copy-start | bytes 18436
  50.7 21.8 %copy-start.7 = (bf16[2,3,1024]{2,0,1:T(2,128)(2,1)S(1)}, bf16[2,3,1024]{2,0,1:T(2,128)(2,1)}, u32[]{:S(2)}) copy-start(bf16[2,3,1024]{2,0,1:T(2,128)(2,1)} %param.19) | copy-start | bytes 36868
  50.8 12.9 %collective-permute-start.11 = (bf16[4,2,2,32,128]{4,3,2,1,0:T(8,128)(2,1)S(1)}, bf16[4,2,2,32,128]{4,3,2,1,0:T(8,128)(2,1)S(1)}, u32[]{:S(2)}, u32[]{:S(2)}) collective-permute-start(bf16[4,2,2,32,128]{4,3,2,1,0:T(8,128)(2,1)S(1)} %get-tuple-element.60), channel_id=1, source_target_pairs={{0,8},{1,9},{2,10},{3,11},{4,12},{5,13},{6,14},{7,15},{8,0},{9,1},... | collective-permute-start | bytes 393224 | tf_op jit(solution)/shard_map/ppermute | solution.py:543
  52.8 11.8 %collective-permute-start.12 = (bf16[4,2,2,32,128]{4,3,2,1,0:T(8,128)(2,1)S(1)}, bf16[4,2,2,32,128]{4,3,2,1,0:T(8,128)(2,1)S(1)}, u32[]{:S(2)}, u32[]{:S(2)}) collective-permute-start(bf16[4,2,2,32,128]{4,3,2,1,0:T(8,128)(2,1)S(1)} %get-tuple-element.61), channel_id=1, source_target_pairs={{0,16},{1,17},{2,18},{3,19},{4,20},{5,21},{6,22},{7,23},{8,24},{9,... | collective-permute-start | bytes 393224 | tf_op jit(solution)/shard_map/ppermute | solution.py:543
  55.5 9.1 %collective-permute-start.13 = (bf16[4,2,2,32,128]{4,3,2,1,0:T(8,128)(2,1)S(1)}, bf16[4,2,2,32,128]{4,3,2,1,0:T(8,128)(2,1)S(1)}, u32[]{:S(2)}, u32[]{:S(2)}) collective-permute-start(bf16[4,2,2,32,128]{4,3,2,1,0:T(8,128)(2,1)S(1)} %get-tuple-element.62), channel_id=1, source_target_pairs={{0,24},{1,25},{2,26},{3,27},{4,28},{5,29},{6,30},{7,31},{8,16},{9,... | collective-permute-start | bytes 393224 | tf_op jit(solution)/shard_map/ppermute | solution.py:543
  61.6 6.4 %collective-permute-start.5 = (f32[3,2,1024]{2,1,0:T(2,128)S(1)}, f32[3,2,1024]{2,1,0:T(2,128)S(1)}, u32[]{:S(2)}, u32[]{:S(2)}) collective-permute-start(f32[3,2,1024]{2,1,0:T(2,128)S(1)} %get-tuple-element.46), channel_id=1, source_target_pairs={{64,32},{65,33},{66,34},{67,35},{68,36},{69,37},{70,38},{71,39},{7... | collective-permute-start | bytes 73736 | tf_op jit(solution)/shard_map/ppermute | solution.py:599
  62.3 10.3 %collective-permute-start.6 = (f32[3,2,1024]{2,1,0:T(2,128)S(1)}, f32[3,2,1024]{2,1,0:T(2,128)S(1)}, u32[]{:S(2)}, u32[]{:S(2)}) collective-permute-start(f32[3,2,1024]{2,1,0:T(2,128)S(1)} %get-tuple-element.47), channel_id=1, source_target_pairs={{64,0},{96,64},{65,1},{97,65},{66,2},{98,66},{67,3},{99,67},{68,4}... | collective-permute-start | bytes 73736 | tf_op jit(solution)/shard_map/ppermute | solution.py:598

commit v6 on v5

--- a/solution.py
+++ b/solution.py
@@ -17,10 +17,10 @@
 NEGATIVE = -1e30
 
 SLOTS = 32
-SIZES = (8, 12, 12)
-FIRSTS = (0, 8, 20)
+SIZES = (12, 12, 8)
+FIRSTS = (0, 12, 24)
 CHUNKS = 3
-GROUPS = ((8,), (4, 8), (4, 8))
+GROUPS = ((4, 8), (4, 8), (8,))
 NT = (((1,), (1,)), ((), ()))
 LIMIT = 16 * 2**20
 VMEM = pl.BlockSpec(memory_space=pltpu.VMEM)
@@ -194,40 +194,39 @@
 EXTRAS = 8
 
 
-def mix_kernel(order, weights, *refs, chunk):
-    last = chunk + 1 == CHUNKS
-    fetch_last = chunk + 2 == CHUNKS
-    made, left = refs[-2:]
-    if last:
-        own, other = refs[:2]
-        out = refs[-3]
-    elif fetch_last:
-        cache, swapped, swapped_last = refs[:3]
-        out, own_last, other_last, own, other, arrived, arrived_last = refs[-9:-2]
-    else:
-        cache, other = refs[:2]
-        swapped = None
-        out, own, _, arrived = refs[-6:-2]
+def mix_kernel(order, weights, cache, *refs, chunk):
+    given, more = chunk > 0, chunk + 1 < CHUNKS
+    refs = list(refs)
+    own = refs.pop(0) if given else None
+    other = refs.pop(0)
+    swapped = refs.pop(0) if more else None
+    if given:
+        refs.pop(0)
+    out = refs.pop(0)
+    following = [refs.pop(0) for _ in range(2)] if more else []
+    if not given:
+        own, arrived = refs.pop(0), refs.pop(0)
+    if more:
+        arrived_next = refs.pop(0)
+    made, left = refs
     size = SIZES[chunk]
     span = own.shape[1]
     width = 2 * span
 
     @pl.when(lax.axis_index("head") >= 2)
     def _():
-        if not last:
-            groups = fetches(order, cache, swapped, own, other, arrived, chunk)
+        if not given:
+            groups = fetches(order, cache, None, own, other, arrived, chunk)
             start(groups)
-        if fetch_last:
-            groups_last = fetches(
-                order, cache, swapped_last, own_last, other_last, arrived_last, chunk + 1
-            )
-            start(groups_last)
+        if more:
+            groups_next = fetches(order, cache, swapped, *following, arrived_next, chunk + 1)
+            start(groups_next)
         extra = weights[:, size * width :].astype(jnp.float32)
         extra = jnp.concatenate([extra, jnp.zeros((LANES - QROWS, LANES), jnp.float32)], axis=0)
         extra = jnp.transpose(extra)
         blank = jnp.zeros((16 - 6, LANES), jnp.float32)
         for pair in range(size // 2):
-            if not last:
+            if not given:
                 wait(groups, 2 * pair)
             rows, lines = [], []
             for n in (2 * pair, 2 * pair + 1):
@@ -250,42 +249,38 @@
         )
         copy.start()
         copy.wait()
-        if fetch_last:
-            for first in groups_last:
-                wait(groups_last, first)
+        if more:
+            for first in groups_next:
+                wait(groups_next, first)
 
 
 def mix_rows(order, weights, cache, swapped, chunk, before, rows, cost):
-    last = chunk + 1 == CHUNKS
-    fetch_last = chunk + 2 == CHUNKS
+    given, more = chunk > 0, chunk + 1 < CHUNKS
     size = SIZES[chunk]
-    held, held_last = held_rows(cache, size), held_rows(cache, SIZES[-1])
     payload = pltpu.HBM((SLOTS // 2, SLAB, LANES), jnp.bfloat16)
-    if last:
-        in_specs = [SMEM, VMEM, VMEM, VMEM]
-        operands = [far(order), near(weights), near(rows[0]), near(rows[1])]
-    else:
-        in_specs = [SMEM, VMEM, ANY, ANY if chunk else VMEM]
-        operands = [
-            far(order), near(weights), far(cache), (far if chunk else near)(swapped[chunk])
-        ]
-    if fetch_last:
+    in_specs = [SMEM, VMEM, ANY]
+    operands = [far(order), near(weights), far(cache)]
+    for array in rows if given else [swapped[chunk]]:
+        in_specs.append(VMEM)
+        operands.append(near(array))
+    if more:
         in_specs.append(ANY)
         operands.append(far(swapped[chunk + 1]))
     aliases = {}
-    if before is not None:
+    if given:
         in_specs.append(ANY)
         aliases = {len(operands): 0}
         operands.append(far(before))
+    following = [held_rows(cache, SIZES[chunk + 1])] * 2 if more else []
     made = pl.pallas_call(
         functools.partial(mix_kernel, chunk=chunk),
         name="mix_rows",
-        out_shape=[payload] + ([held_last, held_last] if fetch_last else []),
+        out_shape=[payload, *following],
         in_specs=in_specs,
-        out_specs=[ANY] + ([VMEM, VMEM] if fetch_last else []),
+        out_specs=[ANY] + [VMEM] * len(following),
         input_output_aliases=aliases,
-        scratch_shapes=([] if last else [held, held, arrivals(chunk)])
-        + ([arrivals(CHUNKS - 1)] if fetch_last else [])
+        scratch_shapes=([] if given else [held_rows(cache, size), arrivals(chunk)])
+        + ([arrivals(chunk + 1)] if more else [])
         + [pltpu.VMEM((size // 2, SLAB, LANES), jnp.bfloat16), pltpu.SemaphoreType.DMA((1,))],
         compiler_params=PARAMS,
         cost_estimate=pl.CostEstimate(flops=cost, bytes_accessed=0, transcendentals=0),

time: 73.9 us -> 73.1 us (0.989)
  no operation moved by 1% of the time
where the time goes in v6:
time: 73.1 us; the launch traced here: 72.4 us
  starting transfers between devices  32.6 us (45%)
  Pallas kernels  23.2 us (32%)
  waiting for transfers between devices  13.1 us (18%)
  other arithmetic  1.41 us (2%)
  local copies, waits for them, and re-layouts  1.08 us (1%)
  between operations  1.05 us (1%)
    all_to_all x2, starting transfers between devices, between_chips(): lax.all_to_all(array, 'wide', 0, 0, tiled=True, axis_index_groups=same_core)  15.4 us
    ppermute x9, starting transfers between devices, across(): return lax.ppermute(array, 'wide', pairs)  10.3 us
    pallas_call x3, Pallas kernels, score_rows(): pl.pallas_call(functools.partial(score_kernel, chunk=chunk), name='score_...  10.1 us
    all_to_all x2, waiting for transfers between devices, between_chips(): lax.all_to_all(array, 'wide', 0, 0, tiled=True, axis_index_groups=same_core)  7.62 us
    pallas_call x2, Pallas kernels, gather_rows(): pl.pallas_call(functools.partial(gather_kernel, first=first), name='gathe...  6.7 us
    ppermute x3, starting transfers between devices, on_device(): moved = [lax.ppermute(made, 'head', [(0, 2), (1, 3)]) for made in weights]  4.96 us
    ppermute x1, waiting for transfers between devices, on_device(): low_here = lax.ppermute(low, 'head', [(2, 0), (3, 2)])  4.29 us
    pallas_call x1, Pallas kernels, delta_rule(): pl.pallas_call(delta_kernel, name='delta_rule', out_shape=(jax.ShapeDtype...  3.15 us
  transfers between devices with their start and end apart: 16, of which 5 were waited for; matrix products, arithmetic and copies ran while one was open for 0% of the time, Pallas kernels for 32%

profile of v6, /device:TPU:0, one launch (start us, length us, event | category | flops | bytes accessed | tf_op | source)
XLA Modules:
  0.0 72.4 jit_solution(1695573575909315532)
XLA Ops:
  0.6 0.8 %select_bitcast_fusion = bf16[2,24,256]{2,1,0:T(8,128)(2,1)S(1)} fusion(bf16[2,3,16,256]{3,2,1,0:T(8,128)(2,1)} %query.2, pred[]{:T(512)S(6)} %eq.12), kind=kLoop, calls=%fused_computation.2 | loop fusion | flops 12288 | bytes 73729 | tf_op jit(solution)/shard_map/jit(_where)/select_n | solution.py:552
  1.4 0.8 %broadcast_in_dim.2 = bf16[16,2,24,256]{3,2,1,0:T(8,128)(2,1)} broadcast(bf16[2,24,256]{2,1,0:T(8,128)(2,1)S(1)} %select_bitcast_fusion), dimensions={1,2,3} | broadcast | bytes 417792 | tf_op jit(solution)/shard_map/broadcast_in_dim | solution.py:549
  2.2 8.1 %all-to-all-start = ((bf16[32,24,256]{2,1,0:T(8,128)(2,1)}), bf16[32,24,256]{2,1,0:T(8,128)(2,1)S(1)}, u32[]{:S(2)}, u32[]{:S(2)}) async-start(bf16[32,24,256]{2,1,0:T(8,128)(2,1)} %bitcast.2), calls=%async_computation | async-start | bytes 786432 | tf_op jit(solution)/shard_map/all_to_all | solution.py:546
  10.3 3.0 %gather_rows.2 = bf16[12,256,256]{2,1,0:T(8,128)(2,1)} custom-call(s32[64]{0:T(128)} %order.9, bf16[64,256,256]{2,1,0:T(8,128)(2,1)} %cache.15), custom_call_target="tpu_custom_call" | custom-call | tf_op jit(solution)/shard_map/gather_rows/pallas_call | solution.py:63
  13.4 0.0 copy-start
  13.4 0.1 collective-permute-start
  13.5 3.7 %gather_rows.3 = bf16[20,256,256]{2,1,0:T(8,128)(2,1)} custom-call(s32[64]{0:T(128)} %order.9, bf16[64,256,256]{2,1,0:T(8,128)(2,1)} %cache.15), custom_call_target="tpu_custom_call" | custom-call | tf_op jit(solution)/shard_map/gather_rows/pallas_call | solution.py:63
  17.1 0.4 collective-permute-start.1
  17.6 0.8 %split_states.1 = (bf16[4,4,2,32,128]{4,3,2,1,0:T(8,128)(2,1)S(1)}, bf16[4,4,2,32,128]{4,3,2,1,0:T(8,128)(2,1)S(1)}) custom-call(s32[64]{0:T(128)} %order.9, f32[64,32,128]{2,1,0:T(8,128)S(1)} %bitcast.18), custom_call_target="tpu_custom_call" | custom-call | tf_op jit(solution)/shard_map/split_states/pallas_call | solution.py:406
  18.3 0.2 collective-permute-start.7
  18.6 1.6 %all-to-all-done.refs_0_ = bf16[32,24,256]{2,1,0:T(8,128)(2,1)S(1)} async-done(((bf16[32,24,256]{2,1,0:T(8,128)(2,1)}), bf16[32,24,256]{2,1,0:T(8,128)(2,1)S(1)}, u32[]{:S(2)}, u32[]{:S(2)}) %all-to-all-start) | async-done | bytes 393248 | tf_op jit(solution)/shard_map/all_to_all | solution.py:546
  20.1 0.0 collective-permute-done.refs_1_
  20.1 3.4 %score_rows.3 = bf16[24,6272]{1,0:T(8,128)(2,1)S(1)} custom-call(s32[64]{0:T(128)} %order.9, s32[64]{0:T(128)} %lengths.5, bf16[32,24,256]{2,1,0:T(8,128)(2,1)S(1)} %get-tuple-element.41.query, bf16[64,256,256]{2,1,0:T(8,128)(2,1)} %cache.15, bf16[12,256,256]{2,1,0:T(8,128)(2,1)S(1)} %get-tuple-element.42.swapped.refs_0_), custom_call_target="tpu_custom_call" | custom-call | tf_op jit(solution)/shard_map/score_rows/pallas_call | solution.py:180
  23.6 2.3 %collective-permute-start.4 = (bf16[24,6272]{1,0:T(8,128)(2,1)S(1)}, bf16[24,6272]{1,0:T(8,128)(2,1)S(1)}, u32[]{:S(2)}, u32[]{:S(2)}) collective-permute-start(bf16[24,6272]{1,0:T(8,128)(2,1)S(1)} %score_rows.3), channel_id=1, source_target_pairs={{0,64},{32,96},{1,65},{33,97},{2,66},{34,98},{3,67},{35,99},{4,68}... | collective-permute-start | bytes 903176 | tf_op jit(solution)/shard_map/ppermute | solution.py:571
  25.9 0.0 collective-permute-done.1.swapped.refs_1_.refs_2_
  25.9 3.5 %score_rows.4 = bf16[24,6272]{1,0:T(8,128)(2,1)S(1)} custom-call(s32[64]{0:T(128)} %order.9, s32[64]{0:T(128)} %lengths.5, bf16[32,24,256]{2,1,0:T(8,128)(2,1)S(1)} %get-tuple-element.41.query, bf16[64,256,256]{2,1,0:T(8,128)(2,1)} %cache.15, bf16[20,256,256]{2,1,0:T(8,128)(2,1)} %collective-permute-done.1.swapped.refs_1_.refs_2_), custom_call_target="tpu_custom_call" | custom-call | tf_op jit(solution)/shard_map/score_rows/pallas_call | solution.py:180
  29.5 1.3 %collective-permute-start.3 = (bf16[24,6272]{1,0:T(8,128)(2,1)S(1)}, bf16[24,6272]{1,0:T(8,128)(2,1)S(1)}, u32[]{:S(2)}, u32[]{:S(2)}) collective-permute-start(bf16[24,6272]{1,0:T(8,128)(2,1)S(1)} %score_rows.4), channel_id=1, source_target_pairs={{0,64},{32,96},{1,65},{33,97},{2,66},{34,98},{3,67},{35,99},{4,68}... | collective-permute-start | bytes 903176 | tf_op jit(solution)/shard_map/ppermute | solution.py:571
  30.8 3.2 %score_rows.5 = bf16[24,4224]{1,0:T(8,128)(2,1)S(1)} custom-call(s32[64]{0:T(128)} %order.9, s32[64]{0:T(128)} %lengths.5, bf16[32,24,256]{2,1,0:T(8,128)(2,1)S(1)} %get-tuple-element.41.query, bf16[64,256,256]{2,1,0:T(8,128)(2,1)} %cache.15, bf16[20,256,256]{2,1,0:T(8,128)(2,1)} %collective-permute-done.1.swapped.refs_1_.refs_2_), custom_call_target="tpu_custom_call" | custom-call | tf_op jit(solution)/shard_map/score_rows/pallas_call | solution.py:180
  34.0 1.3 %collective-permute-start.2 = (bf16[24,4224]{1,0:T(8,128)(2,1)S(1)}, bf16[24,4224]{1,0:T(8,128)(2,1)S(1)}, u32[]{:S(2)}, u32[]{:S(2)}) collective-permute-start(bf16[24,4224]{1,0:T(8,128)(2,1)S(1)} %score_rows.5), channel_id=1, source_target_pairs={{0,64},{32,96},{1,65},{33,97},{2,66},{34,98},{3,67},{35,99},{4,68}... | collective-permute-start | bytes 608264 | tf_op jit(solution)/shard_map/ppermute | solution.py:571
  35.3 1.7 %collective-permute-start.10 = (bf16[2,4,2,32,128]{4,3,2,1,0:T(8,128)(2,1)S(1)}, bf16[2,4,2,32,128]{4,3,2,1,0:T(8,128)(2,1)S(1)}, u32[]{:S(2)}, u32[]{:S(2)}) collective-permute-start(bf16[2,4,2,32,128]{4,3,2,1,0:T(8,128)(2,1)S(1)} %get-tuple-element.60), channel_id=1, source_target_pairs={{0,6},{1,7},{2,4},{3,5},{4,2},{5,3},{6,0},{7,1},{8,14},{9,15},{10,... | collective-permute-start | bytes 393224 | tf_op jit(solution)/shard_map/ppermute | solution.py:538
  37.0 0.3 collective-permute-start.8
  37.2 2.9 %collective-permute-start.9 = (bf16[2,4,2,32,128]{4,3,2,1,0:T(8,128)(2,1)S(1)}, bf16[2,4,2,32,128]{4,3,2,1,0:T(8,128)(2,1)S(1)}, u32[]{:S(2)}, u32[]{:S(2)}) collective-permute-start(bf16[2,4,2,32,128]{4,3,2,1,0:T(8,128)(2,1)S(1)} %get-tuple-element.59), channel_id=1, source_target_pairs={{0,4},{1,5},{2,6},{3,7},{4,0},{5,1},{6,2},{7,3},{8,12},{9,13},{10,... | collective-permute-start | bytes 393224 | tf_op jit(solution)/shard_map/ppermute | solution.py:538
  40.1 0.9 %mix_rows.3 = (bf16[16,112,128]{2,1,0:T(8,128)(2,1)}, bf16[12,256,256]{2,1,0:T(8,128)(2,1)S(1)}, bf16[12,256,256]{2,1,0:T(8,128)(2,1)S(1)}) custom-call(s32[64]{0:T(128)} %order.9, bf16[24,6272]{1,0:T(8,128)(2,1)S(1)} %collective-permute-done.4.weights, bf16[64,256,256]{2,1,0:T(8,128)(2,1)} %cache.15, ...), custom_call_target="tpu_custom_call" | custom-call | flops 3000000000 | tf_op jit(solution)/shard_map/mix_rows/pallas_call | solution.py:275
  41.0 0.0 collective-permute-done.3.weights
  41.1 0.8 %mix_rows.4 = (bf16[16,112,128]{2,1,0:T(8,128)(2,1)}, bf16[8,256,256]{2,1,0:T(8,128)(2,1)S(1)}, bf16[8,256,256]{2,1,0:T(8,128)(2,1)S(1)}) custom-call(s32[64]{0:T(128)} %order.9, bf16[24,6272]{1,0:T(8,128)(2,1)S(1)} %collective-permute-done.3.weights, bf16[64,256,256]{2,1,0:T(8,128)(2,1)} %cache.15, ...), custom_call_target="tpu_custom_call", output_to_operand_aliasing={{0}: (6, {})} | custom-call | flops 3000000000 | tf_op jit(solution)/shard_map/mix_rows/pallas_call | solution.py:275
  41.8 0.2 collective-permute-done.2.weights
  42.0 0.7 mix_rows.5
  42.7 7.2 %all-to-all-start.1 = ((bf16[16,112,128]{2,1,0:T(8,128)(2,1)}), bf16[16,112,128]{2,1,0:T(8,128)(2,1)S(1)}, u32[]{:S(2)}, u32[]{:S(2)}) async-start(bf16[16,112,128]{2,1,0:T(8,128)(2,1)} %mix_rows.5), calls=%async_computation.1 | async-start | bytes 917504 | tf_op jit(solution)/shard_map/all_to_all | solution.py:546
  50.0 0.0 copy-start.6
  50.0 0.0 copy-start.1
  50.0 0.0 copy-start.8
  50.0 0.0 copy-start.9
  50.1 0.0 copy-start.2
  50.1 0.0 copy-start.3
  50.1 0.0 copy-start.4
  50.1 0.0 copy-start.5
  50.2 2.0 %collective-permute-start.11 = (bf16[4,2,2,32,128]{4,3,2,1,0:T(8,128)(2,1)S(1)}, bf16[4,2,2,32,128]{4,3,2,1,0:T(8,128)(2,1)S(1)}, u32[]{:S(2)}, u32[]{:S(2)}) collective-permute-start(bf16[4,2,2,32,128]{4,3,2,1,0:T(8,128)(2,1)S(1)} %get-tuple-element.66), channel_id=1, source_target_pairs={{0,8},{1,9},{2,10},{3,11},{4,12},{5,13},{6,14},{7,15},{8,0},{9,1},... | collective-permute-start | bytes 393224 | tf_op jit(solution)/shard_map/ppermute | solution.py:538
  52.2 2.7 %collective-permute-start.12 = (bf16[4,2,2,32,128]{4,3,2,1,0:T(8,128)(2,1)S(1)}, bf16[4,2,2,32,128]{4,3,2,1,0:T(8,128)(2,1)S(1)}, u32[]{:S(2)}, u32[]{:S(2)}) collective-permute-start(bf16[4,2,2,32,128]{4,3,2,1,0:T(8,128)(2,1)S(1)} %get-tuple-element.67), channel_id=1, source_target_pairs={{0,16},{1,17},{2,18},{3,19},{4,20},{5,21},{6,22},{7,23},{8,24},{9,... | collective-permute-start | bytes 393224 | tf_op jit(solution)/shard_map/ppermute | solution.py:538
  54.8 0.1 collective-permute-start.13
  55.0 0.0 copy-start.7
  55.0 6.0 %all-to-all-done.1.parts = bf16[16,112,128]{2,1,0:T(8,128)(2,1)S(1)} async-done(((bf16[16,112,128]{2,1,0:T(8,128)(2,1)}), bf16[16,112,128]{2,1,0:T(8,128)(2,1)S(1)}, u32[]{:S(2)}, u32[]{:S(2)}) %all-to-all-start.1) | async-done | bytes 458784 | tf_op jit(solution)/shard_map/all_to_all | solution.py:546
  61.0 0.7 collective-permute-start.5
  61.7 1.3 %collective-permute-start.6 = (f32[3,2,1024]{2,1,0:T(2,128)S(1)}, f32[3,2,1024]{2,1,0:T(2,128)S(1)}, u32[]{:S(2)}, u32[]{:S(2)}) collective-permute-start(f32[3,2,1024]{2,1,0:T(2,128)S(1)} %get-tuple-element.53), channel_id=1, source_target_pairs={{64,0},{96,64},{65,1},{97,65},{66,2},{98,66},{67,3},{99,67},{68,4}... | collective-permute-start | bytes 73736 | tf_op jit(solution)/shard_map/ppermute | solution.py:593
  63.0 0.9 %collective-permute-done.12.refs_2_ = bf16[4,2,2,32,128]{4,3,2,1,0:T(8,128)(2,1)S(1)} collective-permute-done((bf16[4,2,2,32,128]{4,3,2,1,0:T(8,128)(2,1)S(1)}, bf16[4,2,2,32,128]{4,3,2,1,0:T(8,128)(2,1)S(1)}, u32[]{:S(2)}, u32[]{:S(2)}) %collective-permute-start.12) | collective-permute-done | bytes 131104 | tf_op jit(solution)/shard_map/ppermute | solution.py:538
  64.0 0.2 copy.26
  64.3 3.1 %delta_rule.1 = (bf16[2,3,8,128]{3,2,1,0:T(8,128)(2,1)}, f32[2,8,128,128]{3,2,1,0:T(8,128)}) custom-call(f32[2,3,8]{2,1,0:T(4,128)S(1)} %copy.27.decay, f32[2,3,8]{2,1,0:T(4,128)S(1)} %copy.28.beta, bf16[2,8,128,128]{3,2,1,0:T(8,128)(2,1)S(1)} %bitcast.16, bf16[2,3,4,128]{3,2,1,0:T(4,128)(2,1)S(1)} %copy-done.4, bf16[2,3,4,128]{3,2,1,0:T(4,128)(2,1)S(1)} %copy-done.5, ...), custom_call_target="tpu_custom_call" | custom-call | tf_op jit(solution)/shard_map/delta_rule/pallas_call | solution.py:503
  67.5 4.3 %collective-permute-done.6 = f32[3,2,1024]{2,1,0:T(2,128)S(1)} collective-permute-done((f32[3,2,1024]{2,1,0:T(2,128)S(1)}, f32[3,2,1024]{2,1,0:T(2,128)S(1)}, u32[]{:S(2)}, u32[]{:S(2)}) %collective-permute-start.6) | collective-permute-done | bytes 24608 | tf_op jit(solution)/shard_map/ppermute | solution.py:593
  71.8 0.6 fusion.1
  (29 shorter events, 0.2 us)
Async XLA Ops:
  2.2 18.0 %all-to-all-start = ((bf16[32,24,256]{2,1,0:T(8,128)(2,1)}), bf16[32,24,256]{2,1,0:T(8,128)(2,1)S(1)}, u32[]{:S(2)}, u32[]{:S(2)}) async-start(bf16[32,24,256]{2,1,0:T(8,128)(2,1)} %bitcast.2), calls=%async_computation | async-start | bytes 786432 | tf_op jit(solution)/shard_map/all_to_all | solution.py:546
  13.4 4.2 %copy-start = (f32[64,8,4,128]{3,2,1,0:T(4,128)S(1)}, f32[64,8,4,128]{3,2,1,0:T(4,128)}, u32[]{:S(2)}) copy-start(f32[64,8,4,128]{3,2,1,0:T(4,128)} %param.14) | copy-start | bytes 3145732
  13.4 6.8 %collective-permute-start = (bf16[12,256,256]{2,1,0:T(8,128)(2,1)}, bf16[12,256,256]{2,1,0:T(8,128)(2,1)S(1)}, u32[]{:S(2)}, u32[]{:S(2)}) collective-permute-start(bf16[12,256,256]{2,1,0:T(8,128)(2,1)} %gather_rows.2), channel_id=1, source_target_pairs={{0,1},{1,0},{2,3},{3,2},{4,5},{5,4},{6,7},{7,6},{8,9},{9,8},{10,11... | collective-permute-start | bytes 4718600 | tf_op jit(solution)/shard_map/ppermute | solution.py:538
  17.1 8.8 %collective-permute-start.1 = (bf16[20,256,256]{2,1,0:T(8,128)(2,1)}, bf16[20,256,256]{2,1,0:T(8,128)(2,1)}, u32[]{:S(2)}, u32[]{:S(2)}) collective-permute-start(bf16[20,256,256]{2,1,0:T(8,128)(2,1)} %gather_rows.3), channel_id=1, source_target_pairs={{0,1},{1,0},{2,3},{3,2},{4,5},{5,4},{6,7},{7,6},{8,9},{9,8},{10,11... | collective-permute-start | bytes 7864328 | tf_op jit(solution)/shard_map/ppermute | solution.py:538
  18.3 12.4 %collective-permute-start.7 = (bf16[4,4,2,32,128]{4,3,2,1,0:T(8,128)(2,1)S(1)}, bf16[4,4,2,32,128]{4,3,2,1,0:T(8,128)(2,1)S(1)}, u32[]{:S(2)}, u32[]{:S(2)}) collective-permute-start(bf16[4,4,2,32,128]{4,3,2,1,0:T(8,128)(2,1)S(1)} %get-tuple-element.39), channel_id=1, source_target_pairs={{0,1},{1,0},{2,3},{3,2},{4,5},{5,4},{6,7},{7,6},{8,9},{9,8},{10,11... | collective-permute-start | bytes 786440 | tf_op jit(solution)/shard_map/ppermute | solution.py:538
  23.6 13.7 %collective-permute-start.4 = (bf16[24,6272]{1,0:T(8,128)(2,1)S(1)}, bf16[24,6272]{1,0:T(8,128)(2,1)S(1)}, u32[]{:S(2)}, u32[]{:S(2)}) collective-permute-start(bf16[24,6272]{1,0:T(8,128)(2,1)S(1)} %score_rows.3), channel_id=1, source_target_pairs={{0,64},{32,96},{1,65},{33,97},{2,66},{34,98},{3,67},{35,99},{4,68}... | collective-permute-start | bytes 903176 | tf_op jit(solution)/shard_map/ppermute | solution.py:571
  29.5 11.6 %collective-permute-start.3 = (bf16[24,6272]{1,0:T(8,128)(2,1)S(1)}, bf16[24,6272]{1,0:T(8,128)(2,1)S(1)}, u32[]{:S(2)}, u32[]{:S(2)}) collective-permute-start(bf16[24,6272]{1,0:T(8,128)(2,1)S(1)} %score_rows.4), channel_id=1, source_target_pairs={{0,64},{32,96},{1,65},{33,97},{2,66},{34,98},{3,67},{35,99},{4,68}... | collective-permute-start | bytes 903176 | tf_op jit(solution)/shard_map/ppermute | solution.py:571
  34.0 8.1 %collective-permute-start.2 = (bf16[24,4224]{1,0:T(8,128)(2,1)S(1)}, bf16[24,4224]{1,0:T(8,128)(2,1)S(1)}, u32[]{:S(2)}, u32[]{:S(2)}) collective-permute-start(bf16[24,4224]{1,0:T(8,128)(2,1)S(1)} %score_rows.5), channel_id=1, source_target_pairs={{0,64},{32,96},{1,65},{33,97},{2,66},{34,98},{3,67},{35,99},{4,68}... | collective-permute-start | bytes 608264 | tf_op jit(solution)/shard_map/ppermute | solution.py:571
  35.3 14.7 %collective-permute-start.10 = (bf16[2,4,2,32,128]{4,3,2,1,0:T(8,128)(2,1)S(1)}, bf16[2,4,2,32,128]{4,3,2,1,0:T(8,128)(2,1)S(1)}, u32[]{:S(2)}, u32[]{:S(2)}) collective-permute-start(bf16[2,4,2,32,128]{4,3,2,1,0:T(8,128)(2,1)S(1)} %get-tuple-element.60), channel_id=1, source_target_pairs={{0,6},{1,7},{2,4},{3,5},{4,2},{5,3},{6,0},{7,1},{8,14},{9,15},{10,... | collective-permute-start | bytes 393224 | tf_op jit(solution)/shard_map/ppermute | solution.py:538
  37.0 13.1 %collective-permute-start.8 = (bf16[2,4,2,32,128]{4,3,2,1,0:T(8,128)(2,1)S(1)}, bf16[2,4,2,32,128]{4,3,2,1,0:T(8,128)(2,1)S(1)}, u32[]{:S(2)}, u32[]{:S(2)}) collective-permute-start(bf16[2,4,2,32,128]{4,3,2,1,0:T(8,128)(2,1)S(1)} %get-tuple-element.58), channel_id=1, source_target_pairs={{0,2},{1,3},{2,0},{3,1},{4,6},{5,7},{6,4},{7,5},{8,10},{9,11},{10,... | collective-permute-start | bytes 393224 | tf_op jit(solution)/shard_map/ppermute | solution.py:538
  37.2 12.8 %collective-permute-start.9 = (bf16[2,4,2,32,128]{4,3,2,1,0:T(8,128)(2,1)S(1)}, bf16[2,4,2,32,128]{4,3,2,1,0:T(8,128)(2,1)S(1)}, u32[]{:S(2)}, u32[]{:S(2)}) collective-permute-start(bf16[2,4,2,32,128]{4,3,2,1,0:T(8,128)(2,1)S(1)} %get-tuple-element.59), channel_id=1, source_target_pairs={{0,4},{1,5},{2,6},{3,7},{4,0},{5,1},{6,2},{7,3},{8,12},{9,13},{10,... | collective-permute-start | bytes 393224 | tf_op jit(solution)/shard_map/ppermute | solution.py:538
  42.7 18.3 %all-to-all-start.1 = ((bf16[16,112,128]{2,1,0:T(8,128)(2,1)}), bf16[16,112,128]{2,1,0:T(8,128)(2,1)S(1)}, u32[]{:S(2)}, u32[]{:S(2)}) async-start(bf16[16,112,128]{2,1,0:T(8,128)(2,1)} %mix_rows.5), calls=%async_computation.1 | async-start | bytes 917504 | tf_op jit(solution)/shard_map/all_to_all | solution.py:546
  50.0 5.0 %copy-start.6 = (bf16[2,3,1024]{2,0,1:T(2,128)(2,1)S(1)}, bf16[2,3,1024]{2,0,1:T(2,128)(2,1)}, u32[]{:S(2)}) copy-start(bf16[2,3,1024]{2,0,1:T(2,128)(2,1)} %param.18) | copy-start | bytes 36868
  50.0 11.0 %copy-start.1 = (bf16[2,3,16,256]{3,2,1,0:T(8,128)(2,1)S(1)}, bf16[2,3,16,256]{3,2,1,0:T(8,128)(2,1)}, u32[]{:S(2)}) copy-start(bf16[2,3,16,256]{3,2,1,0:T(8,128)(2,1)} %query.2) | copy-start | bytes 147460
  50.0 13.0 %copy-start.8 = (f32[2,3,8]{2,0,1:T(2,128)S(1)}, f32[2,3,8]{2,0,1:T(2,128)}, u32[]{:S(2)}) copy-start(f32[2,3,8]{2,0,1:T(2,128)} %param.23) | copy-start | bytes 580
  50.0 13.0 %copy-start.9 = (f32[2,3,8]{2,0,1:T(2,128)S(1)}, f32[2,3,8]{2,0,1:T(2,128)}, u32[]{:S(2)}) copy-start(f32[2,3,8]{2,0,1:T(2,128)} %param.24) | copy-start | bytes 580
  50.1 14.2 %copy-start.2 = (bf16[2,3,8,128]{3,2,1,0:T(8,128)(2,1)S(1)}, bf16[2,3,8,128]{3,2,1,0:T(8,128)(2,1)}, u32[]{:S(2)}) copy-start(bf16[2,3,8,128]{3,2,1,0:T(8,128)(2,1)} %value.1) | copy-start | bytes 36868
  50.1 14.2 %copy-start.3 = (bf16[2,3,8,128]{3,2,1,0:T(8,128)(2,1)S(1)}, bf16[2,3,8,128]{3,2,1,0:T(8,128)(2,1)}, u32[]{:S(2)}) copy-start(bf16[2,3,8,128]{3,2,1,0:T(8,128)(2,1)} %gate.1) | copy-start | bytes 36868
  50.1 14.2 %copy-start.4 = (bf16[2,3,4,128]{3,2,1,0:T(4,128)(2,1)S(1)}, bf16[2,3,4,128]{3,2,1,0:T(4,128)(2,1)}, u32[]{:S(2)}) copy-start(bf16[2,3,4,128]{3,2,1,0:T(4,128)(2,1)} %query.3) | copy-start | bytes 18436
  50.1 14.2 %copy-start.5 = (bf16[2,3,4,128]{3,2,1,0:T(4,128)(2,1)S(1)}, bf16[2,3,4,128]{3,2,1,0:T(4,128)(2,1)}, u32[]{:S(2)}) copy-start(bf16[2,3,4,128]{3,2,1,0:T(4,128)(2,1)} %key.1) | copy-start | bytes 18436
  50.2 12.9 %collective-permute-start.11 = (bf16[4,2,2,32,128]{4,3,2,1,0:T(8,128)(2,1)S(1)}, bf16[4,2,2,32,128]{4,3,2,1,0:T(8,128)(2,1)S(1)}, u32[]{:S(2)}, u32[]{:S(2)}) collective-permute-start(bf16[4,2,2,32,128]{4,3,2,1,0:T(8,128)(2,1)S(1)} %get-tuple-element.66), channel_id=1, source_target_pairs={{0,8},{1,9},{2,10},{3,11},{4,12},{5,13},{6,14},{7,15},{8,0},{9,1},... | collective-permute-start | bytes 393224 | tf_op jit(solution)/shard_map/ppermute | solution.py:538
  52.2 11.8 %collective-permute-start.12 = (bf16[4,2,2,32,128]{4,3,2,1,0:T(8,128)(2,1)S(1)}, bf16[4,2,2,32,128]{4,3,2,1,0:T(8,128)(2,1)S(1)}, u32[]{:S(2)}, u32[]{:S(2)}) collective-permute-start(bf16[4,2,2,32,128]{4,3,2,1,0:T(8,128)(2,1)S(1)} %get-tuple-element.67), channel_id=1, source_target_pairs={{0,16},{1,17},{2,18},{3,19},{4,20},{5,21},{6,22},{7,23},{8,24},{9,... | collective-permute-start | bytes 393224 | tf_op jit(solution)/shard_map/ppermute | solution.py:538
  54.8 9.1 %collective-permute-start.13 = (bf16[4,2,2,32,128]{4,3,2,1,0:T(8,128)(2,1)S(1)}, bf16[4,2,2,32,128]{4,3,2,1,0:T(8,128)(2,1)S(1)}, u32[]{:S(2)}, u32[]{:S(2)}) collective-permute-start(bf16[4,2,2,32,128]{4,3,2,1,0:T(8,128)(2,1)S(1)} %get-tuple-element.68), channel_id=1, source_target_pairs={{0,24},{1,25},{2,26},{3,27},{4,28},{5,29},{6,30},{7,31},{8,16},{9,... | collective-permute-start | bytes 393224 | tf_op jit(solution)/shard_map/ppermute | solution.py:538
  55.0 16.8 %copy-start.7 = (bf16[2,3,1024]{2,0,1:T(2,128)(2,1)S(1)}, bf16[2,3,1024]{2,0,1:T(2,128)(2,1)}, u32[]{:S(2)}) copy-start(bf16[2,3,1024]{2,0,1:T(2,128)(2,1)} %param.19) | copy-start | bytes 36868
  61.0 6.4 %collective-permute-start.5 = (f32[3,2,1024]{2,1,0:T(2,128)S(1)}, f32[3,2,1024]{2,1,0:T(2,128)S(1)}, u32[]{:S(2)}, u32[]{:S(2)}) collective-permute-start(f32[3,2,1024]{2,1,0:T(2,128)S(1)} %get-tuple-element.52), channel_id=1, source_target_pairs={{64,32},{65,33},{66,34},{67,35},{68,36},{69,37},{70,38},{71,39},{7... | collective-permute-start | bytes 73736 | tf_op jit(solution)/shard_map/ppermute | solution.py:594
  61.7 10.1 %collective-permute-start.6 = (f32[3,2,1024]{2,1,0:T(2,128)S(1)}, f32[3,2,1024]{2,1,0:T(2,128)S(1)}, u32[]{:S(2)}, u32[]{:S(2)}) collective-permute-start(f32[3,2,1024]{2,1,0:T(2,128)S(1)} %get-tuple-element.53), channel_id=1, source_target_pairs={{64,0},{96,64},{65,1},{97,65},{66,2},{98,66},{67,3},{99,67},{68,4}... | collective-permute-start | bytes 73736 | tf_op jit(solution)/shard_map/ppermute | solution.py:593

commit v7 on v6

--- a/solution.py
+++ b/solution.py
@@ -590,8 +590,7 @@
     lin_out, final_states = delta_rule(
         states, lin_query, lin_key, lin_value, lin_decay, lin_beta, lin_gate
     )
-    low_here = lax.ppermute(low, "head", [(2, 0), (3, 2)])
-    high_here = lax.ppermute(high, "head", [(2, 1)])
+    low_here, high_here = hold([lax.ppermute(low, "head", [(2, 0), (3, 2)]), lax.ppermute(high, "head", [(2, 1)])], 10 * 10**9)
     result = jnp.where(
         head_index == 3, high, jnp.where(head_index == 1, high_here, low_here)
     )

time: 73.1 us -> 72.7 us (level)
  the two profiles are of different devices: /device:TPU:0 before, /device:TPU:6 now
where the time goes in v7:
time: 72.7 us; the launch traced here: 72 us
  starting transfers between devices  33.7 us (46%)
  Pallas kernels  22.5 us (31%)
  waiting for transfers between devices  11.5 us (16%)
  local copies, waits for them, and re-layouts  1.77 us (2%)
  other arithmetic  1.41 us (2%)
  between operations  1.07 us (1%)
    all_to_all x2, starting transfers between devices, between_chips(): lax.all_to_all(array, 'wide', 0, 0, tiled=True, axis_index_groups=same_core)  15.3 us
    ppermute x9, starting transfers between devices, across(): return lax.ppermute(array, 'wide', pairs)  11.3 us
    pallas_call x3, Pallas kernels, mix_rows(): pl.pallas_call(functools.partial(mix_kernel, chunk=chunk), name='mix_rows...  8.73 us
    all_to_all x2, waiting for transfers between devices, between_chips(): lax.all_to_all(array, 'wide', 0, 0, tiled=True, axis_index_groups=same_core)  7.62 us
    pallas_call x2, Pallas kernels, gather_rows(): pl.pallas_call(functools.partial(gather_kernel, first=first), name='gathe...  6.71 us
    ppermute x3, starting transfers between devices, on_device(): moved = [lax.ppermute(made, 'head', [(0, 2), (1, 3)]) for made in weights]  3.88 us
    ppermute x3, waiting for transfers between devices, on_device(): moved = [lax.ppermute(made, 'head', [(0, 2), (1, 3)]) for made in weights]  3.66 us
    pallas_call x1, Pallas kernels, delta_rule(): pl.pallas_call(delta_kernel, name='delta_rule', out_shape=(jax.ShapeDtype...  3.14 us
  transfers between devices with their start and end apart: 16, of which 4 were waited for; matrix products, arithmetic and copies ran while one was open for 0% of the time, Pallas kernels for 31%

profile of v7, /device:TPU:6, one launch (start us, length us, event | category | flops | bytes accessed | tf_op | source)
XLA Modules:
  0.0 72.0 jit_solution(16699141946934342394)
XLA Ops:
  0.6 0.8 %select_bitcast_fusion = bf16[2,24,256]{2,1,0:T(8,128)(2,1)S(1)} fusion(bf16[2,3,16,256]{3,2,1,0:T(8,128)(2,1)} %query.2, pred[]{:T(512)S(6)} %eq.12), kind=kLoop, calls=%fused_computation.2 | loop fusion | flops 12288 | bytes 73729 | tf_op jit(solution)/shard_map/jit(_where)/select_n | solution.py:552
  1.4 0.8 %broadcast_in_dim.2 = bf16[16,2,24,256]{3,2,1,0:T(8,128)(2,1)} broadcast(bf16[2,24,256]{2,1,0:T(8,128)(2,1)S(1)} %select_bitcast_fusion), dimensions={1,2,3} | broadcast | bytes 417792 | tf_op jit(solution)/shard_map/broadcast_in_dim | solution.py:549
  2.2 8.0 %all-to-all-start = ((bf16[32,24,256]{2,1,0:T(8,128)(2,1)}), bf16[32,24,256]{2,1,0:T(8,128)(2,1)S(1)}, u32[]{:S(2)}, u32[]{:S(2)}) async-start(bf16[32,24,256]{2,1,0:T(8,128)(2,1)} %bitcast.2), calls=%async_computation | async-start | bytes 786432 | tf_op jit(solution)/shard_map/all_to_all | solution.py:546
  10.2 3.0 %gather_rows.2 = bf16[12,256,256]{2,1,0:T(8,128)(2,1)} custom-call(s32[64]{0:T(128)} %order.9, bf16[64,256,256]{2,1,0:T(8,128)(2,1)} %cache.15), custom_call_target="tpu_custom_call" | custom-call | tf_op jit(solution)/shard_map/gather_rows/pallas_call | solution.py:63
  13.3 0.0 copy-start
  13.3 0.1 collective-permute-start
  13.4 3.7 %gather_rows.3 = bf16[20,256,256]{2,1,0:T(8,128)(2,1)} custom-call(s32[64]{0:T(128)} %order.9, bf16[64,256,256]{2,1,0:T(8,128)(2,1)} %cache.15), custom_call_target="tpu_custom_call" | custom-call | tf_op jit(solution)/shard_map/gather_rows/pallas_call | solution.py:63
  17.1 0.4 collective-permute-start.1
  17.5 0.8 %split_states.1 = (bf16[4,4,2,32,128]{4,3,2,1,0:T(8,128)(2,1)S(1)}, bf16[4,4,2,32,128]{4,3,2,1,0:T(8,128)(2,1)S(1)}) custom-call(s32[64]{0:T(128)} %order.9, f32[64,32,128]{2,1,0:T(8,128)S(1)} %bitcast.18), custom_call_target="tpu_custom_call" | custom-call | tf_op jit(solution)/shard_map/split_states/pallas_call | solution.py:406
  18.3 0.2 collective-permute-start.7
  18.5 1.6 %all-to-all-done.refs_0_ = bf16[32,24,256]{2,1,0:T(8,128)(2,1)S(1)} async-done(((bf16[32,24,256]{2,1,0:T(8,128)(2,1)}), bf16[32,24,256]{2,1,0:T(8,128)(2,1)S(1)}, u32[]{:S(2)}, u32[]{:S(2)}) %all-to-all-start) | async-done | bytes 393248 | tf_op jit(solution)/shard_map/all_to_all | solution.py:546
  20.1 0.0 collective-permute-done.refs_1_
  20.1 0.8 %score_rows.3 = bf16[24,6272]{1,0:T(8,128)(2,1)S(1)} custom-call(s32[64]{0:T(128)} %order.9, s32[64]{0:T(128)} %lengths.5, bf16[32,24,256]{2,1,0:T(8,128)(2,1)S(1)} %get-tuple-element.43.query, bf16[64,256,256]{2,1,0:T(8,128)(2,1)} %cache.15, bf16[12,256,256]{2,1,0:T(8,128)(2,1)S(1)} %get-tuple-element.44.swapped.refs_0_), custom_call_target="tpu_custom_call" | custom-call | tf_op jit(solution)/shard_map/score_rows/pallas_call | solution.py:180
  20.9 1.3 %collective-permute-start.4 = (bf16[24,6272]{1,0:T(8,128)(2,1)S(1)}, bf16[24,6272]{1,0:T(8,128)(2,1)S(1)}, u32[]{:S(2)}, u32[]{:S(2)}) collective-permute-start(bf16[24,6272]{1,0:T(8,128)(2,1)S(1)} %score_rows.3), channel_id=1, source_target_pairs={{0,64},{32,96},{1,65},{33,97},{2,66},{34,98},{3,67},{35,99},{4,68}... | collective-permute-start | bytes 903176 | tf_op jit(solution)/shard_map/ppermute | solution.py:571
  22.2 0.2 collective-permute-done.1.swapped.refs_1_.refs_2_
  22.4 0.8 %score_rows.4 = bf16[24,6272]{1,0:T(8,128)(2,1)S(1)} custom-call(s32[64]{0:T(128)} %order.9, s32[64]{0:T(128)} %lengths.5, bf16[32,24,256]{2,1,0:T(8,128)(2,1)S(1)} %get-tuple-element.43.query, bf16[64,256,256]{2,1,0:T(8,128)(2,1)} %cache.15, bf16[20,256,256]{2,1,0:T(8,128)(2,1)} %collective-permute-done.1.swapped.refs_1_.refs_2_), custom_call_target="tpu_custom_call" | custom-call | tf_op jit(solution)/shard_map/score_rows/pallas_call | solution.py:180
  23.2 1.3 %collective-permute-start.3 = (bf16[24,6272]{1,0:T(8,128)(2,1)S(1)}, bf16[24,6272]{1,0:T(8,128)(2,1)S(1)}, u32[]{:S(2)}, u32[]{:S(2)}) collective-permute-start(bf16[24,6272]{1,0:T(8,128)(2,1)S(1)} %score_rows.4), channel_id=1, source_target_pairs={{0,64},{32,96},{1,65},{33,97},{2,66},{34,98},{3,67},{35,99},{4,68}... | collective-permute-start | bytes 903176 | tf_op jit(solution)/shard_map/ppermute | solution.py:571
  24.5 0.0 collective-permute-done.7.refs_0_
  24.5 0.8 %score_rows.5 = bf16[24,4224]{1,0:T(8,128)(2,1)S(1)} custom-call(s32[64]{0:T(128)} %order.9, s32[64]{0:T(128)} %lengths.5, bf16[32,24,256]{2,1,0:T(8,128)(2,1)S(1)} %get-tuple-element.43.query, bf16[64,256,256]{2,1,0:T(8,128)(2,1)} %cache.15, bf16[20,256,256]{2,1,0:T(8,128)(2,1)} %collective-permute-done.1.swapped.refs_1_.refs_2_), custom_call_target="tpu_custom_call" | custom-call | tf_op jit(solution)/shard_map/score_rows/pallas_call | solution.py:180
  25.3 1.3 %collective-permute-start.2 = (bf16[24,4224]{1,0:T(8,128)(2,1)S(1)}, bf16[24,4224]{1,0:T(8,128)(2,1)S(1)}, u32[]{:S(2)}, u32[]{:S(2)}) collective-permute-start(bf16[24,4224]{1,0:T(8,128)(2,1)S(1)} %score_rows.5), channel_id=1, source_target_pairs={{0,64},{32,96},{1,65},{33,97},{2,66},{34,98},{3,67},{35,99},{4,68}... | collective-permute-start | bytes 608264 | tf_op jit(solution)/shard_map/ppermute | solution.py:571
  26.7 3.2 %collective-permute-start.10 = (bf16[2,4,2,32,128]{4,3,2,1,0:T(8,128)(2,1)S(1)}, bf16[2,4,2,32,128]{4,3,2,1,0:T(8,128)(2,1)S(1)}, u32[]{:S(2)}, u32[]{:S(2)}) collective-permute-start(bf16[2,4,2,32,128]{4,3,2,1,0:T(8,128)(2,1)S(1)} %get-tuple-element.64), channel_id=1, source_target_pairs={{0,6},{1,7},{2,4},{3,5},{4,2},{5,3},{6,0},{7,1},{8,14},{9,15},{10,... | collective-permute-start | bytes 393224 | tf_op jit(solution)/shard_map/ppermute | solution.py:538
  29.9 0.3 collective-permute-start.8
  30.1 3.7 %collective-permute-done.4.weights = bf16[24,6272]{1,0:T(8,128)(2,1)S(1)} collective-permute-done((bf16[24,6272]{1,0:T(8,128)(2,1)S(1)}, bf16[24,6272]{1,0:T(8,128)(2,1)S(1)}, u32[]{:S(2)}, u32[]{:S(2)}) %collective-permute-start.4) | collective-permute-done | bytes 301088 | tf_op jit(solution)/shard_map/ppermute | solution.py:571
  33.8 2.3 %collective-permute-start.9 = (bf16[2,4,2,32,128]{4,3,2,1,0:T(8,128)(2,1)S(1)}, bf16[2,4,2,32,128]{4,3,2,1,0:T(8,128)(2,1)S(1)}, u32[]{:S(2)}, u32[]{:S(2)}) collective-permute-start(bf16[2,4,2,32,128]{4,3,2,1,0:T(8,128)(2,1)S(1)} %get-tuple-element.63), channel_id=1, source_target_pairs={{0,4},{1,5},{2,6},{3,7},{4,0},{5,1},{6,2},{7,3},{8,12},{9,13},{10,... | collective-permute-start | bytes 393224 | tf_op jit(solution)/shard_map/ppermute | solution.py:538
  36.1 4.3 %mix_rows.3 = (bf16[16,112,128]{2,1,0:T(8,128)(2,1)}, bf16[12,256,256]{2,1,0:T(8,128)(2,1)S(1)}, bf16[12,256,256]{2,1,0:T(8,128)(2,1)S(1)}) custom-call(s32[64]{0:T(128)} %order.9, bf16[24,6272]{1,0:T(8,128)(2,1)S(1)} %collective-permute-done.4.weights, bf16[64,256,256]{2,1,0:T(8,128)(2,1)} %cache.15, ...), custom_call_target="tpu_custom_call" | custom-call | flops 3000000000 | tf_op jit(solution)/shard_map/mix_rows/pallas_call | solution.py:275
  40.4 0.0 collective-permute-done.3.weights
  40.5 2.6 %mix_rows.4 = (bf16[16,112,128]{2,1,0:T(8,128)(2,1)}, bf16[8,256,256]{2,1,0:T(8,128)(2,1)S(1)}, bf16[8,256,256]{2,1,0:T(8,128)(2,1)S(1)}) custom-call(s32[64]{0:T(128)} %order.9, bf16[24,6272]{1,0:T(8,128)(2,1)S(1)} %collective-permute-done.3.weights, bf16[64,256,256]{2,1,0:T(8,128)(2,1)} %cache.15, ...), custom_call_target="tpu_custom_call", output_to_operand_aliasing={{0}: (6, {})} | custom-call | flops 3000000000 | tf_op jit(solution)/shard_map/mix_rows/pallas_call | solution.py:275
  43.1 1.8 %mix_rows.5 = bf16[16,112,128]{2,1,0:T(8,128)(2,1)} custom-call(s32[64]{0:T(128)} %order.9, bf16[24,4224]{1,0:T(8,128)(2,1)S(1)} %collective-permute-done.2.weights, bf16[64,256,256]{2,1,0:T(8,128)(2,1)} %cache.15, bf16[8,256,256]{2,1,0:T(8,128)(2,1)S(1)} %get-tuple-element.51.refs_0_, ...), custom_call_target="tpu_custom_call", output_to_operand_aliasing={{}: (5, {})} | custom-call | flops 10000000000 | tf_op jit(solution)/shard_map/mix_rows/pallas_call | solution.py:275
  44.9 7.2 %all-to-all-start.1 = ((bf16[16,112,128]{2,1,0:T(8,128)(2,1)}), bf16[16,112,128]{2,1,0:T(8,128)(2,1)S(1)}, u32[]{:S(2)}, u32[]{:S(2)}) async-start(bf16[16,112,128]{2,1,0:T(8,128)(2,1)} %mix_rows.5), calls=%async_computation.1 | async-start | bytes 917504 | tf_op jit(solution)/shard_map/all_to_all | solution.py:546
  52.1 0.0 copy-start.6
  52.1 0.0 copy-start.1
  52.1 0.0 copy-start.8
  52.1 0.0 copy-start.9
  52.2 0.0 copy-start.2
  52.2 0.0 copy-start.3
  52.2 0.0 copy-start.4
  52.2 0.0 copy-start.5
  52.3 2.0 %collective-permute-start.11 = (bf16[4,2,2,32,128]{4,3,2,1,0:T(8,128)(2,1)S(1)}, bf16[4,2,2,32,128]{4,3,2,1,0:T(8,128)(2,1)S(1)}, u32[]{:S(2)}, u32[]{:S(2)}) collective-permute-start(bf16[4,2,2,32,128]{4,3,2,1,0:T(8,128)(2,1)S(1)} %get-tuple-element.70), channel_id=1, source_target_pairs={{0,8},{1,9},{2,10},{3,11},{4,12},{5,13},{6,14},{7,15},{8,0},{9,1},... | collective-permute-start | bytes 393224 | tf_op jit(solution)/shard_map/ppermute | solution.py:538
  54.3 2.7 %collective-permute-start.12 = (bf16[4,2,2,32,128]{4,3,2,1,0:T(8,128)(2,1)S(1)}, bf16[4,2,2,32,128]{4,3,2,1,0:T(8,128)(2,1)S(1)}, u32[]{:S(2)}, u32[]{:S(2)}) collective-permute-start(bf16[4,2,2,32,128]{4,3,2,1,0:T(8,128)(2,1)S(1)} %get-tuple-element.71), channel_id=1, source_target_pairs={{0,16},{1,17},{2,18},{3,19},{4,20},{5,21},{6,22},{7,23},{8,24},{9,... | collective-permute-start | bytes 393224 | tf_op jit(solution)/shard_map/ppermute | solution.py:538
  57.0 0.1 collective-permute-start.13
  57.1 6.1 %all-to-all-done.1.parts = bf16[16,112,128]{2,1,0:T(8,128)(2,1)S(1)} async-done(((bf16[16,112,128]{2,1,0:T(8,128)(2,1)}), bf16[16,112,128]{2,1,0:T(8,128)(2,1)S(1)}, u32[]{:S(2)}, u32[]{:S(2)}) %all-to-all-start.1) | async-done | bytes 458784 | tf_op jit(solution)/shard_map/all_to_all | solution.py:546
  63.2 0.6 combine_parts.1
  63.8 2.6 %collective-permute-start.5 = (f32[3,2,1024]{2,1,0:T(2,128)S(1)}, f32[3,2,1024]{2,1,0:T(2,128)S(1)}, u32[]{:S(2)}, u32[]{:S(2)}) collective-permute-start(f32[3,2,1024]{2,1,0:T(2,128)S(1)} %get-tuple-element.55), channel_id=1, source_target_pairs={{64,0},{96,64},{65,1},{97,65},{66,2},{98,66},{67,3},{99,67},{68,4}... | collective-permute-start | bytes 73736 | tf_op jit(solution)/shard_map/ppermute | solution.py:593
  66.4 0.7 collective-permute-start.6
  67.2 0.2 copy.28
  67.5 3.1 %delta_rule.1 = (bf16[2,3,8,128]{3,2,1,0:T(8,128)(2,1)}, f32[2,8,128,128]{3,2,1,0:T(8,128)}) custom-call(f32[2,3,8]{2,1,0:T(4,128)S(1)} %copy.29.decay, f32[2,3,8]{2,1,0:T(4,128)S(1)} %copy.30.beta, bf16[2,8,128,128]{3,2,1,0:T(8,128)(2,1)S(1)} %bitcast.16, bf16[2,3,4,128]{3,2,1,0:T(4,128)(2,1)S(1)} %copy-done.4, bf16[2,3,4,128]{3,2,1,0:T(4,128)(2,1)S(1)} %copy-done.5, ...), custom_call_target="tpu_custom_call" | custom-call | tf_op jit(solution)/shard_map/delta_rule/pallas_call | solution.py:503
  70.6 0.7 copy-done.7
  71.3 0.6 fusion.1
  (30 shorter events, 0.2 us)
Async XLA Ops:
  2.2 17.9 %all-to-all-start = ((bf16[32,24,256]{2,1,0:T(8,128)(2,1)}), bf16[32,24,256]{2,1,0:T(8,128)(2,1)S(1)}, u32[]{:S(2)}, u32[]{:S(2)}) async-start(bf16[32,24,256]{2,1,0:T(8,128)(2,1)} %bitcast.2), calls=%async_computation | async-start | bytes 786432 | tf_op jit(solution)/shard_map/all_to_all | solution.py:546
  13.3 4.2 %copy-start = (f32[64,8,4,128]{3,2,1,0:T(4,128)S(1)}, f32[64,8,4,128]{3,2,1,0:T(4,128)}, u32[]{:S(2)}) copy-start(f32[64,8,4,128]{3,2,1,0:T(4,128)} %param.14) | copy-start | bytes 3145732
  13.3 6.8 %collective-permute-start = (bf16[12,256,256]{2,1,0:T(8,128)(2,1)}, bf16[12,256,256]{2,1,0:T(8,128)(2,1)S(1)}, u32[]{:S(2)}, u32[]{:S(2)}) collective-permute-start(bf16[12,256,256]{2,1,0:T(8,128)(2,1)} %gather_rows.2), channel_id=1, source_target_pairs={{0,1},{1,0},{2,3},{3,2},{4,5},{5,4},{6,7},{7,6},{8,9},{9,8},{10,11... | collective-permute-start | bytes 4718600 | tf_op jit(solution)/shard_map/ppermute | solution.py:538
  17.1 5.3 %collective-permute-start.1 = (bf16[20,256,256]{2,1,0:T(8,128)(2,1)}, bf16[20,256,256]{2,1,0:T(8,128)(2,1)}, u32[]{:S(2)}, u32[]{:S(2)}) collective-permute-start(bf16[20,256,256]{2,1,0:T(8,128)(2,1)} %gather_rows.3), channel_id=1, source_target_pairs={{0,1},{1,0},{2,3},{3,2},{4,5},{5,4},{6,7},{7,6},{8,9},{9,8},{10,11... | collective-permute-start | bytes 7864328 | tf_op jit(solution)/shard_map/ppermute | solution.py:538
  18.3 6.3 %collective-permute-start.7 = (bf16[4,4,2,32,128]{4,3,2,1,0:T(8,128)(2,1)S(1)}, bf16[4,4,2,32,128]{4,3,2,1,0:T(8,128)(2,1)S(1)}, u32[]{:S(2)}, u32[]{:S(2)}) collective-permute-start(bf16[4,4,2,32,128]{4,3,2,1,0:T(8,128)(2,1)S(1)} %get-tuple-element.41), channel_id=1, source_target_pairs={{0,1},{1,0},{2,3},{3,2},{4,5},{5,4},{6,7},{7,6},{8,9},{9,8},{10,11... | collective-permute-start | bytes 786440 | tf_op jit(solution)/shard_map/ppermute | solution.py:538
  20.9 12.9 %collective-permute-start.4 = (bf16[24,6272]{1,0:T(8,128)(2,1)S(1)}, bf16[24,6272]{1,0:T(8,128)(2,1)S(1)}, u32[]{:S(2)}, u32[]{:S(2)}) collective-permute-start(bf16[24,6272]{1,0:T(8,128)(2,1)S(1)} %score_rows.3), channel_id=1, source_target_pairs={{0,64},{32,96},{1,65},{33,97},{2,66},{34,98},{3,67},{35,99},{4,68}... | collective-permute-start | bytes 903176 | tf_op jit(solution)/shard_map/ppermute | solution.py:571
  23.2 17.2 %collective-permute-start.3 = (bf16[24,6272]{1,0:T(8,128)(2,1)S(1)}, bf16[24,6272]{1,0:T(8,128)(2,1)S(1)}, u32[]{:S(2)}, u32[]{:S(2)}) collective-permute-start(bf16[24,6272]{1,0:T(8,128)(2,1)S(1)} %score_rows.4), channel_id=1, source_target_pairs={{0,64},{32,96},{1,65},{33,97},{2,66},{34,98},{3,67},{35,99},{4,68}... | collective-permute-start | bytes 903176 | tf_op jit(solution)/shard_map/ppermute | solution.py:571
  25.3 17.8 %collective-permute-start.2 = (bf16[24,4224]{1,0:T(8,128)(2,1)S(1)}, bf16[24,4224]{1,0:T(8,128)(2,1)S(1)}, u32[]{:S(2)}, u32[]{:S(2)}) collective-permute-start(bf16[24,4224]{1,0:T(8,128)(2,1)S(1)} %score_rows.5), channel_id=1, source_target_pairs={{0,64},{32,96},{1,65},{33,97},{2,66},{34,98},{3,67},{35,99},{4,68}... | collective-permute-start | bytes 608264 | tf_op jit(solution)/shard_map/ppermute | solution.py:571
  26.7 25.5 %collective-permute-start.10 = (bf16[2,4,2,32,128]{4,3,2,1,0:T(8,128)(2,1)S(1)}, bf16[2,4,2,32,128]{4,3,2,1,0:T(8,128)(2,1)S(1)}, u32[]{:S(2)}, u32[]{:S(2)}) collective-permute-start(bf16[2,4,2,32,128]{4,3,2,1,0:T(8,128)(2,1)S(1)} %get-tuple-element.64), channel_id=1, source_target_pairs={{0,6},{1,7},{2,4},{3,5},{4,2},{5,3},{6,0},{7,1},{8,14},{9,15},{10,... | collective-permute-start | bytes 393224 | tf_op jit(solution)/shard_map/ppermute | solution.py:538
  29.9 22.3 %collective-permute-start.8 = (bf16[2,4,2,32,128]{4,3,2,1,0:T(8,128)(2,1)S(1)}, bf16[2,4,2,32,128]{4,3,2,1,0:T(8,128)(2,1)S(1)}, u32[]{:S(2)}, u32[]{:S(2)}) collective-permute-start(bf16[2,4,2,32,128]{4,3,2,1,0:T(8,128)(2,1)S(1)} %get-tuple-element.62), channel_id=1, source_target_pairs={{0,2},{1,3},{2,0},{3,1},{4,6},{5,7},{6,4},{7,5},{8,10},{9,11},{10,... | collective-permute-start | bytes 393224 | tf_op jit(solution)/shard_map/ppermute | solution.py:538
  33.8 18.4 %collective-permute-start.9 = (bf16[2,4,2,32,128]{4,3,2,1,0:T(8,128)(2,1)S(1)}, bf16[2,4,2,32,128]{4,3,2,1,0:T(8,128)(2,1)S(1)}, u32[]{:S(2)}, u32[]{:S(2)}) collective-permute-start(bf16[2,4,2,32,128]{4,3,2,1,0:T(8,128)(2,1)S(1)} %get-tuple-element.63), channel_id=1, source_target_pairs={{0,4},{1,5},{2,6},{3,7},{4,0},{5,1},{6,2},{7,3},{8,12},{9,13},{10,... | collective-permute-start | bytes 393224 | tf_op jit(solution)/shard_map/ppermute | solution.py:538
  44.9 18.3 %all-to-all-start.1 = ((bf16[16,112,128]{2,1,0:T(8,128)(2,1)}), bf16[16,112,128]{2,1,0:T(8,128)(2,1)S(1)}, u32[]{:S(2)}, u32[]{:S(2)}) async-start(bf16[16,112,128]{2,1,0:T(8,128)(2,1)} %mix_rows.5), calls=%async_computation.1 | async-start | bytes 917504 | tf_op jit(solution)/shard_map/all_to_all | solution.py:546
  52.1 5.0 %copy-start.6 = (bf16[2,3,1024]{2,0,1:T(2,128)(2,1)S(1)}, bf16[2,3,1024]{2,0,1:T(2,128)(2,1)}, u32[]{:S(2)}) copy-start(bf16[2,3,1024]{2,0,1:T(2,128)(2,1)} %param.18) | copy-start | bytes 36868
  52.1 11.0 %copy-start.1 = (bf16[2,3,16,256]{3,2,1,0:T(8,128)(2,1)S(1)}, bf16[2,3,16,256]{3,2,1,0:T(8,128)(2,1)}, u32[]{:S(2)}) copy-start(bf16[2,3,16,256]{3,2,1,0:T(8,128)(2,1)} %query.2) | copy-start | bytes 147460
  52.1 14.9 %copy-start.8 = (f32[2,3,8]{2,0,1:T(2,128)S(1)}, f32[2,3,8]{2,0,1:T(2,128)}, u32[]{:S(2)}) copy-start(f32[2,3,8]{2,0,1:T(2,128)} %param.23) | copy-start | bytes 580
  52.1 14.9 %copy-start.9 = (f32[2,3,8]{2,0,1:T(2,128)S(1)}, f32[2,3,8]{2,0,1:T(2,128)}, u32[]{:S(2)}) copy-start(f32[2,3,8]{2,0,1:T(2,128)} %param.24) | copy-start | bytes 580
  52.2 15.2 %copy-start.2 = (bf16[2,3,8,128]{3,2,1,0:T(8,128)(2,1)S(1)}, bf16[2,3,8,128]{3,2,1,0:T(8,128)(2,1)}, u32[]{:S(2)}) copy-start(bf16[2,3,8,128]{3,2,1,0:T(8,128)(2,1)} %value.1) | copy-start | bytes 36868
  52.2 15.2 %copy-start.3 = (bf16[2,3,8,128]{3,2,1,0:T(8,128)(2,1)S(1)}, bf16[2,3,8,128]{3,2,1,0:T(8,128)(2,1)}, u32[]{:S(2)}) copy-start(bf16[2,3,8,128]{3,2,1,0:T(8,128)(2,1)} %gate.1) | copy-start | bytes 36868
  52.2 15.2 %copy-start.4 = (bf16[2,3,4,128]{3,2,1,0:T(4,128)(2,1)S(1)}, bf16[2,3,4,128]{3,2,1,0:T(4,128)(2,1)}, u32[]{:S(2)}) copy-start(bf16[2,3,4,128]{3,2,1,0:T(4,128)(2,1)} %query.3) | copy-start | bytes 18436
  52.2 15.2 %copy-start.5 = (bf16[2,3,4,128]{3,2,1,0:T(4,128)(2,1)S(1)}, bf16[2,3,4,128]{3,2,1,0:T(4,128)(2,1)}, u32[]{:S(2)}) copy-start(bf16[2,3,4,128]{3,2,1,0:T(4,128)(2,1)} %key.1) | copy-start | bytes 18436
  52.3 14.8 %collective-permute-start.11 = (bf16[4,2,2,32,128]{4,3,2,1,0:T(8,128)(2,1)S(1)}, bf16[4,2,2,32,128]{4,3,2,1,0:T(8,128)(2,1)S(1)}, u32[]{:S(2)}, u32[]{:S(2)}) collective-permute-start(bf16[4,2,2,32,128]{4,3,2,1,0:T(8,128)(2,1)S(1)} %get-tuple-element.70), channel_id=1, source_target_pairs={{0,8},{1,9},{2,10},{3,11},{4,12},{5,13},{6,14},{7,15},{8,0},{9,1},... | collective-permute-start | bytes 393224 | tf_op jit(solution)/shard_map/ppermute | solution.py:538
  54.3 12.8 %collective-permute-start.12 = (bf16[4,2,2,32,128]{4,3,2,1,0:T(8,128)(2,1)S(1)}, bf16[4,2,2,32,128]{4,3,2,1,0:T(8,128)(2,1)S(1)}, u32[]{:S(2)}, u32[]{:S(2)}) collective-permute-start(bf16[4,2,2,32,128]{4,3,2,1,0:T(8,128)(2,1)S(1)} %get-tuple-element.71), channel_id=1, source_target_pairs={{0,16},{1,17},{2,18},{3,19},{4,20},{5,21},{6,22},{7,23},{8,24},{9,... | collective-permute-start | bytes 393224 | tf_op jit(solution)/shard_map/ppermute | solution.py:538
  57.0 10.2 %collective-permute-start.13 = (bf16[4,2,2,32,128]{4,3,2,1,0:T(8,128)(2,1)S(1)}, bf16[4,2,2,32,128]{4,3,2,1,0:T(8,128)(2,1)S(1)}, u32[]{:S(2)}, u32[]{:S(2)}) collective-permute-start(bf16[4,2,2,32,128]{4,3,2,1,0:T(8,128)(2,1)S(1)} %get-tuple-element.72), channel_id=1, source_target_pairs={{0,24},{1,25},{2,26},{3,27},{4,28},{5,29},{6,30},{7,31},{8,16},{9,... | collective-permute-start | bytes 393224 | tf_op jit(solution)/shard_map/ppermute | solution.py:538
  63.8 6.8 %collective-permute-start.5 = (f32[3,2,1024]{2,1,0:T(2,128)S(1)}, f32[3,2,1024]{2,1,0:T(2,128)S(1)}, u32[]{:S(2)}, u32[]{:S(2)}) collective-permute-start(f32[3,2,1024]{2,1,0:T(2,128)S(1)} %get-tuple-element.55), channel_id=1, source_target_pairs={{64,0},{96,64},{65,1},{97,65},{66,2},{98,66},{67,3},{99,67},{68,4}... | collective-permute-start | bytes 73736 | tf_op jit(solution)/shard_map/ppermute | solution.py:593
  66.4 4.2 %collective-permute-start.6 = (f32[3,2,1024]{2,1,0:T(2,128)S(1)}, f32[3,2,1024]{2,1,0:T(2,128)S(1)}, u32[]{:S(2)}, u32[]{:S(2)}) collective-permute-start(f32[3,2,1024]{2,1,0:T(2,128)S(1)} %get-tuple-element.54), channel_id=1, source_target_pairs={{64,32},{65,33},{66,34},{67,35},{68,36},{69,37},{70,38},{71,39},{7... | collective-permute-start | bytes 73736 | tf_op jit(solution)/shard_map/ppermute | solution.py:593
  70.6 0.7 copy-start.7

commit v8 on v7

--- a/solution.py
+++ b/solution.py
@@ -17,10 +17,10 @@
 NEGATIVE = -1e30
 
 SLOTS = 32
-SIZES = (12, 12, 8)
-FIRSTS = (0, 12, 24)
+SIZES = (10, 14, 8)
+FIRSTS = (0, 10, 24)
 CHUNKS = 3
-GROUPS = ((4, 8), (4, 8), (8,))
+GROUPS = ((10,), (6, 8), (8,))
 NT = (((1,), (1,)), ((), ()))
 LIMIT = 16 * 2**20
 VMEM = pl.BlockSpec(memory_space=pltpu.VMEM)

time: 72.7 us -> 72.6 us (level)
  waiting for transfers between devices: 11.5 us -> 10.4 us
  starting transfers between devices: 33.7 us -> 34.6 us
    ppermute x3, waiting for transfers between devices: 3.66 us -> 2.12 us  [on_device(): moved = [lax.ppermute(made, 'head', [(0, 2), (1, 3)]) for made in weights]]
    ppermute x9, starting transfers between devices: 11.3 us -> 12.4 us  [across(): return lax.ppermute(array, 'wide', pairs)]
  transfers between devices with their start and end apart: 16 -> 16, of which waited for: 4 -> 5; matrix products, arithmetic and copies ran while one was open for 0% -> 0% of each run, Pallas kernels for 31% -> 32%
where the time goes in v8:
time: 72.6 us; the launch traced here: 71.9 us
  starting transfers between devices  34.6 us (48%)
  Pallas kernels  22.7 us (31%)
  waiting for transfers between devices  10.4 us (14%)
  local copies, waits for them, and re-layouts  1.77 us (2%)
  other arithmetic  1.41 us (2%)
  between operations  1.07 us (1%)
    all_to_all x2, starting transfers between devices, between_chips(): lax.all_to_all(array, 'wide', 0, 0, tiled=True, axis_index_groups=same_core)  14.9 us
    ppermute x9, starting transfers between devices, across(): return lax.ppermute(array, 'wide', pairs)  12.4 us
    pallas_call x3, Pallas kernels, mix_rows(): pl.pallas_call(functools.partial(mix_kernel, chunk=chunk), name='mix_rows...  8.97 us
    all_to_all x2, waiting for transfers between devices, between_chips(): lax.all_to_all(array, 'wide', 0, 0, tiled=True, axis_index_groups=same_core)  7.65 us
    pallas_call x2, Pallas kernels, gather_rows(): pl.pallas_call(functools.partial(gather_kernel, first=first), name='gathe...  6.68 us
    ppermute x3, starting transfers between devices, on_device(): moved = [lax.ppermute(made, 'head', [(0, 2), (1, 3)]) for made in weights]  3.88 us
    pallas_call x1, Pallas kernels, delta_rule(): pl.pallas_call(delta_kernel, name='delta_rule', out_shape=(jax.ShapeDtype...  3.14 us
    ppermute x1, starting transfers between devices, on_device(): lax.ppermute(low, 'head', [(2, 0), (3, 2)])  2.74 us
  transfers between devices with their start and end apart: 16, of which 5 were waited for; matrix products, arithmetic and copies ran while one was open for 0% of the time, Pallas kernels for 32%

profile of v8, /device:TPU:6, one launch (start us, length us, event | category | flops | bytes accessed | tf_op | source)
XLA Modules:
  0.0 71.9 jit_solution(18373121092881185215)
XLA Ops:
  0.6 0.8 %select_bitcast_fusion = bf16[2,24,256]{2,1,0:T(8,128)(2,1)S(1)} fusion(bf16[2,3,16,256]{3,2,1,0:T(8,128)(2,1)} %query.2, pred[]{:T(512)S(6)} %eq.12), kind=kLoop, calls=%fused_computation.2 | loop fusion | flops 12288 | bytes 73729 | tf_op jit(solution)/shard_map/jit(_where)/select_n | solution.py:552
  1.4 0.8 %broadcast_in_dim.2 = bf16[16,2,24,256]{3,2,1,0:T(8,128)(2,1)} broadcast(bf16[2,24,256]{2,1,0:T(8,128)(2,1)S(1)} %select_bitcast_fusion), dimensions={1,2,3} | broadcast | bytes 417792 | tf_op jit(solution)/shard_map/broadcast_in_dim | solution.py:549
  2.2 8.0 %all-to-all-start = ((bf16[32,24,256]{2,1,0:T(8,128)(2,1)}), bf16[32,24,256]{2,1,0:T(8,128)(2,1)S(1)}, u32[]{:S(2)}, u32[]{:S(2)}) async-start(bf16[32,24,256]{2,1,0:T(8,128)(2,1)} %bitcast.2), calls=%async_computation | async-start | bytes 786432 | tf_op jit(solution)/shard_map/all_to_all | solution.py:546
  10.2 2.9 %gather_rows.2 = bf16[10,256,256]{2,1,0:T(8,128)(2,1)} custom-call(s32[64]{0:T(128)} %order.9, bf16[64,256,256]{2,1,0:T(8,128)(2,1)} %cache.15), custom_call_target="tpu_custom_call" | custom-call | tf_op jit(solution)/shard_map/gather_rows/pallas_call | solution.py:63
  13.1 0.0 copy-start
  13.2 0.1 collective-permute-start
  13.2 3.8 %gather_rows.3 = bf16[22,256,256]{2,1,0:T(8,128)(2,1)} custom-call(s32[64]{0:T(128)} %order.9, bf16[64,256,256]{2,1,0:T(8,128)(2,1)} %cache.15), custom_call_target="tpu_custom_call" | custom-call | tf_op jit(solution)/shard_map/gather_rows/pallas_call | solution.py:63
  17.0 0.4 collective-permute-start.1
  17.5 0.8 %split_states.1 = (bf16[4,4,2,32,128]{4,3,2,1,0:T(8,128)(2,1)S(1)}, bf16[4,4,2,32,128]{4,3,2,1,0:T(8,128)(2,1)S(1)}) custom-call(s32[64]{0:T(128)} %order.9, f32[64,32,128]{2,1,0:T(8,128)S(1)} %bitcast.18), custom_call_target="tpu_custom_call" | custom-call | tf_op jit(solution)/shard_map/split_states/pallas_call | solution.py:406
  18.2 0.2 collective-permute-start.7
  18.5 1.6 %all-to-all-done.refs_0_ = bf16[32,24,256]{2,1,0:T(8,128)(2,1)S(1)} async-done(((bf16[32,24,256]{2,1,0:T(8,128)(2,1)}), bf16[32,24,256]{2,1,0:T(8,128)(2,1)S(1)}, u32[]{:S(2)}, u32[]{:S(2)}) %all-to-all-start) | async-done | bytes 393248 | tf_op jit(solution)/shard_map/all_to_all | solution.py:546
  20.1 0.0 collective-permute-done.refs_1_
  20.1 0.8 %score_rows.3 = bf16[24,5248]{1,0:T(8,128)(2,1)S(1)} custom-call(s32[64]{0:T(128)} %order.9, s32[64]{0:T(128)} %lengths.5, bf16[32,24,256]{2,1,0:T(8,128)(2,1)S(1)} %get-tuple-element.43.query, bf16[64,256,256]{2,1,0:T(8,128)(2,1)} %cache.15, bf16[10,256,256]{2,1,0:T(8,128)(2,1)S(1)} %get-tuple-element.44.swapped.refs_0_), custom_call_target="tpu_custom_call" | custom-call | tf_op jit(solution)/shard_map/score_rows/pallas_call | solution.py:180
  20.9 1.3 %collective-permute-start.4 = (bf16[24,5248]{1,0:T(8,128)(2,1)S(1)}, bf16[24,5248]{1,0:T(8,128)(2,1)S(1)}, u32[]{:S(2)}, u32[]{:S(2)}) collective-permute-start(bf16[24,5248]{1,0:T(8,128)(2,1)S(1)} %score_rows.3), channel_id=1, source_target_pairs={{0,64},{32,96},{1,65},{33,97},{2,66},{34,98},{3,67},{35,99},{4,68}... | collective-permute-start | bytes 755720 | tf_op jit(solution)/shard_map/ppermute | solution.py:571
  22.2 0.6 collective-permute-done.1.swapped.refs_1_.refs_2_
  22.7 0.8 %score_rows.4 = bf16[24,7296]{1,0:T(8,128)(2,1)S(1)} custom-call(s32[64]{0:T(128)} %order.9, s32[64]{0:T(128)} %lengths.5, bf16[32,24,256]{2,1,0:T(8,128)(2,1)S(1)} %get-tuple-element.43.query, bf16[64,256,256]{2,1,0:T(8,128)(2,1)} %cache.15, bf16[22,256,256]{2,1,0:T(8,128)(2,1)} %collective-permute-done.1.swapped.refs_1_.refs_2_), custom_call_target="tpu_custom_call" | custom-call | tf_op jit(solution)/shard_map/score_rows/pallas_call | solution.py:180
  23.6 1.3 %collective-permute-start.3 = (bf16[24,7296]{1,0:T(8,128)(2,1)S(1)}, bf16[24,7296]{1,0:T(8,128)(2,1)S(1)}, u32[]{:S(2)}, u32[]{:S(2)}) collective-permute-start(bf16[24,7296]{1,0:T(8,128)(2,1)S(1)} %score_rows.4), channel_id=1, source_target_pairs={{0,64},{32,96},{1,65},{33,97},{2,66},{34,98},{3,67},{35,99},{4,68}... | collective-permute-start | bytes 1050632 | tf_op jit(solution)/shard_map/ppermute | solution.py:571
  24.9 0.0 collective-permute-done.7.refs_0_
  24.9 0.8 %score_rows.5 = bf16[24,4224]{1,0:T(8,128)(2,1)S(1)} custom-call(s32[64]{0:T(128)} %order.9, s32[64]{0:T(128)} %lengths.5, bf16[32,24,256]{2,1,0:T(8,128)(2,1)S(1)} %get-tuple-element.43.query, bf16[64,256,256]{2,1,0:T(8,128)(2,1)} %cache.15, bf16[22,256,256]{2,1,0:T(8,128)(2,1)} %collective-permute-done.1.swapped.refs_1_.refs_2_), custom_call_target="tpu_custom_call" | custom-call | tf_op jit(solution)/shard_map/score_rows/pallas_call | solution.py:180
  25.7 1.3 %collective-permute-start.2 = (bf16[24,4224]{1,0:T(8,128)(2,1)S(1)}, bf16[24,4224]{1,0:T(8,128)(2,1)S(1)}, u32[]{:S(2)}, u32[]{:S(2)}) collective-permute-start(bf16[24,4224]{1,0:T(8,128)(2,1)S(1)} %score_rows.5), channel_id=1, source_target_pairs={{0,64},{32,96},{1,65},{33,97},{2,66},{34,98},{3,67},{35,99},{4,68}... | collective-permute-start | bytes 608264 | tf_op jit(solution)/shard_map/ppermute | solution.py:571
  27.0 3.2 %collective-permute-start.10 = (bf16[2,4,2,32,128]{4,3,2,1,0:T(8,128)(2,1)S(1)}, bf16[2,4,2,32,128]{4,3,2,1,0:T(8,128)(2,1)S(1)}, u32[]{:S(2)}, u32[]{:S(2)}) collective-permute-start(bf16[2,4,2,32,128]{4,3,2,1,0:T(8,128)(2,1)S(1)} %get-tuple-element.64), channel_id=1, source_target_pairs={{0,6},{1,7},{2,4},{3,5},{4,2},{5,3},{6,0},{7,1},{8,14},{9,15},{10,... | collective-permute-start | bytes 393224 | tf_op jit(solution)/shard_map/ppermute | solution.py:538
  30.2 0.3 collective-permute-start.8
  30.5 0.7 collective-permute-done.4.weights
  31.2 3.4 %collective-permute-start.9 = (bf16[2,4,2,32,128]{4,3,2,1,0:T(8,128)(2,1)S(1)}, bf16[2,4,2,32,128]{4,3,2,1,0:T(8,128)(2,1)S(1)}, u32[]{:S(2)}, u32[]{:S(2)}) collective-permute-start(bf16[2,4,2,32,128]{4,3,2,1,0:T(8,128)(2,1)S(1)} %get-tuple-element.63), channel_id=1, source_target_pairs={{0,4},{1,5},{2,6},{3,7},{4,0},{5,1},{6,2},{7,3},{8,12},{9,13},{10,... | collective-permute-start | bytes 393224 | tf_op jit(solution)/shard_map/ppermute | solution.py:538
  34.6 4.5 %mix_rows.3 = (bf16[16,112,128]{2,1,0:T(8,128)(2,1)}, bf16[14,256,256]{2,1,0:T(8,128)(2,1)S(1)}, bf16[14,256,256]{2,1,0:T(8,128)(2,1)S(1)}) custom-call(s32[64]{0:T(128)} %order.9, bf16[24,5248]{1,0:T(8,128)(2,1)S(1)} %collective-permute-done.4.weights, bf16[64,256,256]{2,1,0:T(8,128)(2,1)} %cache.15, ...), custom_call_target="tpu_custom_call" | custom-call | flops 3000000000 | tf_op jit(solution)/shard_map/mix_rows/pallas_call | solution.py:275
  39.1 1.4 %collective-permute-done.3.weights = bf16[24,7296]{1,0:T(8,128)(2,1)S(1)} collective-permute-done((bf16[24,7296]{1,0:T(8,128)(2,1)S(1)}, bf16[24,7296]{1,0:T(8,128)(2,1)S(1)}, u32[]{:S(2)}, u32[]{:S(2)}) %collective-permute-start.3) | collective-permute-done | bytes 350240 | tf_op jit(solution)/shard_map/ppermute | solution.py:571
  40.5 2.7 %mix_rows.4 = (bf16[16,112,128]{2,1,0:T(8,128)(2,1)}, bf16[8,256,256]{2,1,0:T(8,128)(2,1)S(1)}, bf16[8,256,256]{2,1,0:T(8,128)(2,1)S(1)}) custom-call(s32[64]{0:T(128)} %order.9, bf16[24,7296]{1,0:T(8,128)(2,1)S(1)} %collective-permute-done.3.weights, bf16[64,256,256]{2,1,0:T(8,128)(2,1)} %cache.15, ...), custom_call_target="tpu_custom_call", output_to_operand_aliasing={{0}: (6, {})} | custom-call | flops 3000000000 | tf_op jit(solution)/shard_map/mix_rows/pallas_call | solution.py:275
  43.3 1.8 %mix_rows.5 = bf16[16,112,128]{2,1,0:T(8,128)(2,1)} custom-call(s32[64]{0:T(128)} %order.9, bf16[24,4224]{1,0:T(8,128)(2,1)S(1)} %collective-permute-done.2.weights, bf16[64,256,256]{2,1,0:T(8,128)(2,1)} %cache.15, bf16[8,256,256]{2,1,0:T(8,128)(2,1)S(1)} %get-tuple-element.51.refs_0_, ...), custom_call_target="tpu_custom_call", output_to_operand_aliasing={{}: (5, {})} | custom-call | flops 10000000000 | tf_op jit(solution)/shard_map/mix_rows/pallas_call | solution.py:275
  45.1 6.8 %all-to-all-start.1 = ((bf16[16,112,128]{2,1,0:T(8,128)(2,1)}), bf16[16,112,128]{2,1,0:T(8,128)(2,1)S(1)}, u32[]{:S(2)}, u32[]{:S(2)}) async-start(bf16[16,112,128]{2,1,0:T(8,128)(2,1)} %mix_rows.5), calls=%async_computation.1 | async-start | bytes 917504 | tf_op jit(solution)/shard_map/all_to_all | solution.py:546
  51.9 0.0 copy-start.6
  51.9 0.0 copy-start.1
  51.9 0.0 copy-start.8
  51.9 0.0 copy-start.9
  52.0 0.0 copy-start.2
  52.0 0.0 copy-start.3
  52.0 0.0 copy-start.4
  52.0 0.0 copy-start.5
  52.1 2.0 %collective-permute-start.11 = (bf16[4,2,2,32,128]{4,3,2,1,0:T(8,128)(2,1)S(1)}, bf16[4,2,2,32,128]{4,3,2,1,0:T(8,128)(2,1)S(1)}, u32[]{:S(2)}, u32[]{:S(2)}) collective-permute-start(bf16[4,2,2,32,128]{4,3,2,1,0:T(8,128)(2,1)S(1)} %get-tuple-element.70), channel_id=1, source_target_pairs={{0,8},{1,9},{2,10},{3,11},{4,12},{5,13},{6,14},{7,15},{8,0},{9,1},... | collective-permute-start | bytes 393224 | tf_op jit(solution)/shard_map/ppermute | solution.py:538
  54.1 2.7 %collective-permute-start.12 = (bf16[4,2,2,32,128]{4,3,2,1,0:T(8,128)(2,1)S(1)}, bf16[4,2,2,32,128]{4,3,2,1,0:T(8,128)(2,1)S(1)}, u32[]{:S(2)}, u32[]{:S(2)}) collective-permute-start(bf16[4,2,2,32,128]{4,3,2,1,0:T(8,128)(2,1)S(1)} %get-tuple-element.71), channel_id=1, source_target_pairs={{0,16},{1,17},{2,18},{3,19},{4,20},{5,21},{6,22},{7,23},{8,24},{9,... | collective-permute-start | bytes 393224 | tf_op jit(solution)/shard_map/ppermute | solution.py:538
  56.8 0.1 collective-permute-start.13
  56.9 6.1 %all-to-all-done.1.parts = bf16[16,112,128]{2,1,0:T(8,128)(2,1)S(1)} async-done(((bf16[16,112,128]{2,1,0:T(8,128)(2,1)}), bf16[16,112,128]{2,1,0:T(8,128)(2,1)S(1)}, u32[]{:S(2)}, u32[]{:S(2)}) %all-to-all-start.1) | async-done | bytes 458784 | tf_op jit(solution)/shard_map/all_to_all | solution.py:546
  62.9 0.6 combine_parts.1
  63.6 2.7 %collective-permute-start.5 = (f32[3,2,1024]{2,1,0:T(2,128)S(1)}, f32[3,2,1024]{2,1,0:T(2,128)S(1)}, u32[]{:S(2)}, u32[]{:S(2)}) collective-permute-start(f32[3,2,1024]{2,1,0:T(2,128)S(1)} %get-tuple-element.55), channel_id=1, source_target_pairs={{64,0},{96,64},{65,1},{97,65},{66,2},{98,66},{67,3},{99,67},{68,4}... | collective-permute-start | bytes 73736 | tf_op jit(solution)/shard_map/ppermute | solution.py:593
  66.3 0.7 collective-permute-start.6
  67.1 0.2 copy.28
  67.4 3.1 %delta_rule.1 = (bf16[2,3,8,128]{3,2,1,0:T(8,128)(2,1)}, f32[2,8,128,128]{3,2,1,0:T(8,128)}) custom-call(f32[2,3,8]{2,1,0:T(4,128)S(1)} %copy.29.decay, f32[2,3,8]{2,1,0:T(4,128)S(1)} %copy.30.beta, bf16[2,8,128,128]{3,2,1,0:T(8,128)(2,1)S(1)} %bitcast.16, bf16[2,3,4,128]{3,2,1,0:T(4,128)(2,1)S(1)} %copy-done.4, bf16[2,3,4,128]{3,2,1,0:T(4,128)(2,1)S(1)} %copy-done.5, ...), custom_call_target="tpu_custom_call" | custom-call | tf_op jit(solution)/shard_map/delta_rule/pallas_call | solution.py:503
  70.6 0.7 copy-done.7
  71.3 0.6 fusion.1
  (30 shorter events, 0.2 us)
Async XLA Ops:
  2.2 17.9 %all-to-all-start = ((bf16[32,24,256]{2,1,0:T(8,128)(2,1)}), bf16[32,24,256]{2,1,0:T(8,128)(2,1)S(1)}, u32[]{:S(2)}, u32[]{:S(2)}) async-start(bf16[32,24,256]{2,1,0:T(8,128)(2,1)} %bitcast.2), calls=%async_computation | async-start | bytes 786432 | tf_op jit(solution)/shard_map/all_to_all | solution.py:546
  13.1 4.3 %copy-start = (f32[64,8,4,128]{3,2,1,0:T(4,128)S(1)}, f32[64,8,4,128]{3,2,1,0:T(4,128)}, u32[]{:S(2)}) copy-start(f32[64,8,4,128]{3,2,1,0:T(4,128)} %param.14) | copy-start | bytes 3145732
  13.2 6.9 %collective-permute-start = (bf16[10,256,256]{2,1,0:T(8,128)(2,1)}, bf16[10,256,256]{2,1,0:T(8,128)(2,1)S(1)}, u32[]{:S(2)}, u32[]{:S(2)}) collective-permute-start(bf16[10,256,256]{2,1,0:T(8,128)(2,1)} %gather_rows.2), channel_id=1, source_target_pairs={{0,1},{1,0},{2,3},{3,2},{4,5},{5,4},{6,7},{7,6},{8,9},{9,8},{10,11... | collective-permute-start | bytes 3932168 | tf_op jit(solution)/shard_map/ppermute | solution.py:538
  17.0 5.7 %collective-permute-start.1 = (bf16[22,256,256]{2,1,0:T(8,128)(2,1)}, bf16[22,256,256]{2,1,0:T(8,128)(2,1)}, u32[]{:S(2)}, u32[]{:S(2)}) collective-permute-start(bf16[22,256,256]{2,1,0:T(8,128)(2,1)} %gather_rows.3), channel_id=1, source_target_pairs={{0,1},{1,0},{2,3},{3,2},{4,5},{5,4},{6,7},{7,6},{8,9},{9,8},{10,11... | collective-permute-start | bytes 8650760 | tf_op jit(solution)/shard_map/ppermute | solution.py:538
  18.2 6.6 %collective-permute-start.7 = (bf16[4,4,2,32,128]{4,3,2,1,0:T(8,128)(2,1)S(1)}, bf16[4,4,2,32,128]{4,3,2,1,0:T(8,128)(2,1)S(1)}, u32[]{:S(2)}, u32[]{:S(2)}) collective-permute-start(bf16[4,4,2,32,128]{4,3,2,1,0:T(8,128)(2,1)S(1)} %get-tuple-element.41), channel_id=1, source_target_pairs={{0,1},{1,0},{2,3},{3,2},{4,5},{5,4},{6,7},{7,6},{8,9},{9,8},{10,11... | collective-permute-start | bytes 786440 | tf_op jit(solution)/shard_map/ppermute | solution.py:538
  20.9 10.3 %collective-permute-start.4 = (bf16[24,5248]{1,0:T(8,128)(2,1)S(1)}, bf16[24,5248]{1,0:T(8,128)(2,1)S(1)}, u32[]{:S(2)}, u32[]{:S(2)}) collective-permute-start(bf16[24,5248]{1,0:T(8,128)(2,1)S(1)} %score_rows.3), channel_id=1, source_target_pairs={{0,64},{32,96},{1,65},{33,97},{2,66},{34,98},{3,67},{35,99},{4,68}... | collective-permute-start | bytes 755720 | tf_op jit(solution)/shard_map/ppermute | solution.py:571
  23.6 17.0 %collective-permute-start.3 = (bf16[24,7296]{1,0:T(8,128)(2,1)S(1)}, bf16[24,7296]{1,0:T(8,128)(2,1)S(1)}, u32[]{:S(2)}, u32[]{:S(2)}) collective-permute-start(bf16[24,7296]{1,0:T(8,128)(2,1)S(1)} %score_rows.4), channel_id=1, source_target_pairs={{0,64},{32,96},{1,65},{33,97},{2,66},{34,98},{3,67},{35,99},{4,68}... | collective-permute-start | bytes 1050632 | tf_op jit(solution)/shard_map/ppermute | solution.py:571
  25.7 17.6 %collective-permute-start.2 = (bf16[24,4224]{1,0:T(8,128)(2,1)S(1)}, bf16[24,4224]{1,0:T(8,128)(2,1)S(1)}, u32[]{:S(2)}, u32[]{:S(2)}) collective-permute-start(bf16[24,4224]{1,0:T(8,128)(2,1)S(1)} %score_rows.5), channel_id=1, source_target_pairs={{0,64},{32,96},{1,65},{33,97},{2,66},{34,98},{3,67},{35,99},{4,68}... | collective-permute-start | bytes 608264 | tf_op jit(solution)/shard_map/ppermute | solution.py:571
  27.0 24.9 %collective-permute-start.10 = (bf16[2,4,2,32,128]{4,3,2,1,0:T(8,128)(2,1)S(1)}, bf16[2,4,2,32,128]{4,3,2,1,0:T(8,128)(2,1)S(1)}, u32[]{:S(2)}, u32[]{:S(2)}) collective-permute-start(bf16[2,4,2,32,128]{4,3,2,1,0:T(8,128)(2,1)S(1)} %get-tuple-element.64), channel_id=1, source_target_pairs={{0,6},{1,7},{2,4},{3,5},{4,2},{5,3},{6,0},{7,1},{8,14},{9,15},{10,... | collective-permute-start | bytes 393224 | tf_op jit(solution)/shard_map/ppermute | solution.py:538
  30.2 21.7 %collective-permute-start.8 = (bf16[2,4,2,32,128]{4,3,2,1,0:T(8,128)(2,1)S(1)}, bf16[2,4,2,32,128]{4,3,2,1,0:T(8,128)(2,1)S(1)}, u32[]{:S(2)}, u32[]{:S(2)}) collective-permute-start(bf16[2,4,2,32,128]{4,3,2,1,0:T(8,128)(2,1)S(1)} %get-tuple-element.62), channel_id=1, source_target_pairs={{0,2},{1,3},{2,0},{3,1},{4,6},{5,7},{6,4},{7,5},{8,10},{9,11},{10,... | collective-permute-start | bytes 393224 | tf_op jit(solution)/shard_map/ppermute | solution.py:538
  31.2 20.8 %collective-permute-start.9 = (bf16[2,4,2,32,128]{4,3,2,1,0:T(8,128)(2,1)S(1)}, bf16[2,4,2,32,128]{4,3,2,1,0:T(8,128)(2,1)S(1)}, u32[]{:S(2)}, u32[]{:S(2)}) collective-permute-start(bf16[2,4,2,32,128]{4,3,2,1,0:T(8,128)(2,1)S(1)} %get-tuple-element.63), channel_id=1, source_target_pairs={{0,4},{1,5},{2,6},{3,7},{4,0},{5,1},{6,2},{7,3},{8,12},{9,13},{10,... | collective-permute-start | bytes 393224 | tf_op jit(solution)/shard_map/ppermute | solution.py:538
  45.1 17.9 %all-to-all-start.1 = ((bf16[16,112,128]{2,1,0:T(8,128)(2,1)}), bf16[16,112,128]{2,1,0:T(8,128)(2,1)S(1)}, u32[]{:S(2)}, u32[]{:S(2)}) async-start(bf16[16,112,128]{2,1,0:T(8,128)(2,1)} %mix_rows.5), calls=%async_computation.1 | async-start | bytes 917504 | tf_op jit(solution)/shard_map/all_to_all | solution.py:546
  51.9 5.0 %copy-start.6 = (bf16[2,3,1024]{2,0,1:T(2,128)(2,1)S(1)}, bf16[2,3,1024]{2,0,1:T(2,128)(2,1)}, u32[]{:S(2)}) copy-start(bf16[2,3,1024]{2,0,1:T(2,128)(2,1)} %param.18) | copy-start | bytes 36868
  51.9 11.0 %copy-start.1 = (bf16[2,3,16,256]{3,2,1,0:T(8,128)(2,1)S(1)}, bf16[2,3,16,256]{3,2,1,0:T(8,128)(2,1)}, u32[]{:S(2)}) copy-start(bf16[2,3,16,256]{3,2,1,0:T(8,128)(2,1)} %query.2) | copy-start | bytes 147460
  51.9 15.1 %copy-start.8 = (f32[2,3,8]{2,0,1:T(2,128)S(1)}, f32[2,3,8]{2,0,1:T(2,128)}, u32[]{:S(2)}) copy-start(f32[2,3,8]{2,0,1:T(2,128)} %param.23) | copy-start | bytes 580
  51.9 15.1 %copy-start.9 = (f32[2,3,8]{2,0,1:T(2,128)S(1)}, f32[2,3,8]{2,0,1:T(2,128)}, u32[]{:S(2)}) copy-start(f32[2,3,8]{2,0,1:T(2,128)} %param.24) | copy-start | bytes 580
  52.0 15.4 %copy-start.2 = (bf16[2,3,8,128]{3,2,1,0:T(8,128)(2,1)S(1)}, bf16[2,3,8,128]{3,2,1,0:T(8,128)(2,1)}, u32[]{:S(2)}) copy-start(bf16[2,3,8,128]{3,2,1,0:T(8,128)(2,1)} %value.1) | copy-start | bytes 36868
  52.0 15.4 %copy-start.3 = (bf16[2,3,8,128]{3,2,1,0:T(8,128)(2,1)S(1)}, bf16[2,3,8,128]{3,2,1,0:T(8,128)(2,1)}, u32[]{:S(2)}) copy-start(bf16[2,3,8,128]{3,2,1,0:T(8,128)(2,1)} %gate.1) | copy-start | bytes 36868
  52.0 15.4 %copy-start.4 = (bf16[2,3,4,128]{3,2,1,0:T(4,128)(2,1)S(1)}, bf16[2,3,4,128]{3,2,1,0:T(4,128)(2,1)}, u32[]{:S(2)}) copy-start(bf16[2,3,4,128]{3,2,1,0:T(4,128)(2,1)} %query.3) | copy-start | bytes 18436
  52.0 15.4 %copy-start.5 = (bf16[2,3,4,128]{3,2,1,0:T(4,128)(2,1)S(1)}, bf16[2,3,4,128]{3,2,1,0:T(4,128)(2,1)}, u32[]{:S(2)}) copy-start(bf16[2,3,4,128]{3,2,1,0:T(4,128)(2,1)} %key.1) | copy-start | bytes 18436
  52.1 15.0 %collective-permute-start.11 = (bf16[4,2,2,32,128]{4,3,2,1,0:T(8,128)(2,1)S(1)}, bf16[4,2,2,32,128]{4,3,2,1,0:T(8,128)(2,1)S(1)}, u32[]{:S(2)}, u32[]{:S(2)}) collective-permute-start(bf16[4,2,2,32,128]{4,3,2,1,0:T(8,128)(2,1)S(1)} %get-tuple-element.70), channel_id=1, source_target_pairs={{0,8},{1,9},{2,10},{3,11},{4,12},{5,13},{6,14},{7,15},{8,0},{9,1},... | collective-permute-start | bytes 393224 | tf_op jit(solution)/shard_map/ppermute | solution.py:538
  54.1 13.0 %collective-permute-start.12 = (bf16[4,2,2,32,128]{4,3,2,1,0:T(8,128)(2,1)S(1)}, bf16[4,2,2,32,128]{4,3,2,1,0:T(8,128)(2,1)S(1)}, u32[]{:S(2)}, u32[]{:S(2)}) collective-permute-start(bf16[4,2,2,32,128]{4,3,2,1,0:T(8,128)(2,1)S(1)} %get-tuple-element.71), channel_id=1, source_target_pairs={{0,16},{1,17},{2,18},{3,19},{4,20},{5,21},{6,22},{7,23},{8,24},{9,... | collective-permute-start | bytes 393224 | tf_op jit(solution)/shard_map/ppermute | solution.py:538
  56.8 10.3 %collective-permute-start.13 = (bf16[4,2,2,32,128]{4,3,2,1,0:T(8,128)(2,1)S(1)}, bf16[4,2,2,32,128]{4,3,2,1,0:T(8,128)(2,1)S(1)}, u32[]{:S(2)}, u32[]{:S(2)}) collective-permute-start(bf16[4,2,2,32,128]{4,3,2,1,0:T(8,128)(2,1)S(1)} %get-tuple-element.72), channel_id=1, source_target_pairs={{0,24},{1,25},{2,26},{3,27},{4,28},{5,29},{6,30},{7,31},{8,16},{9,... | collective-permute-start | bytes 393224 | tf_op jit(solution)/shard_map/ppermute | solution.py:538
  63.6 7.0 %collective-permute-start.5 = (f32[3,2,1024]{2,1,0:T(2,128)S(1)}, f32[3,2,1024]{2,1,0:T(2,128)S(1)}, u32[]{:S(2)}, u32[]{:S(2)}) collective-permute-start(f32[3,2,1024]{2,1,0:T(2,128)S(1)} %get-tuple-element.55), channel_id=1, source_target_pairs={{64,0},{96,64},{65,1},{97,65},{66,2},{98,66},{67,3},{99,67},{68,4}... | collective-permute-start | bytes 73736 | tf_op jit(solution)/shard_map/ppermute | solution.py:593
  66.3 4.2 %collective-permute-start.6 = (f32[3,2,1024]{2,1,0:T(2,128)S(1)}, f32[3,2,1024]{2,1,0:T(2,128)S(1)}, u32[]{:S(2)}, u32[]{:S(2)}) collective-permute-start(f32[3,2,1024]{2,1,0:T(2,128)S(1)} %get-tuple-element.54), channel_id=1, source_target_pairs={{64,32},{65,33},{66,34},{67,35},{68,36},{69,37},{70,38},{71,39},{7... | collective-permute-start | bytes 73736 | tf_op jit(solution)/shard_map/ppermute | solution.py:593
  70.6 0.7 copy-start.7
